TPU v7x, 32 devices: a whole 2x2x4 slice. The times are simulated.
32 devices in a mesh: dp: 16 (over z, x, core), tensor: 2 (over y).
Axes of the slice: x: 2, y: 2, z: 4, core: 2. Of those that a mesh axis runs over, the one named last changes fastest.
Arguments:
- tokens: bfloat16 [6144, 768], P('dp'), may hold values from -6 to 6
- project_weight: bfloat16 [768, 3, 768], P('dp', None, 'tensor'), may hold values from -0.21875 to 0.21875
- project_bias: float32 [2, 768], P(None, 'tensor'), may hold values from -2 to 2
- output_weight: bfloat16 [768, 768], P('tensor', 'dp'), may hold values from -0.875 to 0.875
- output_bias: float32 [2, 768], replicated, may hold values from -2 to 2
- expand_weight: bfloat16 [768, 3072], P('dp', 'tensor'), may hold values from -0.21875 to 0.21875
- expand_bias: float32 [3072], P('tensor'), may hold values from -2 to 2
- shrink_weight: bfloat16 [3072, 768], P('tensor', 'dp'), may hold values from -0.109375 to 0.109375
- norm_gain: float32 [2, 768], replicated, may hold values from 0.5 to 1.5
- norm_shift: float32 [2, 768], replicated, may hold values from -2 to 2
- doc_lengths: int32 [16, 4], P('dp'), may hold values from 1 to 256, 384 in all within a row
- cluster_perm: int32 [16, 12, 384], P('dp', 'tensor'), may hold values from 0 to 383, each once within a row
- masked: int32 [6144], P('dp'), may hold values from 0 to 1, as said below
- out_grad: bfloat16 [6144, 768], P('dp'), may hold values from -6 to 6
Outputs:
- layer_out: bfloat16 [6144, 768], P('dp')
- tokens_grad: float32 [6144, 768], P('dp')
- project_weight_grad: float32 [768, 3, 768], P('dp', None, 'tensor')
- project_bias_grad: float32 [2, 768], P(None, 'tensor')
- output_weight_grad: float32 [768, 768], P('tensor', 'dp')
- output_bias_grad: float32 [2, 768], replicated
- expand_weight_grad: float32 [768, 3072], P('dp', 'tensor')
- expand_bias_grad: float32 [3072], P('tensor')
- shrink_weight_grad: float32 [3072, 768], P('tensor', 'dp')
- norm_gain_grad: float32 [2, 768], replicated
- norm_shift_grad: float32 [2, 768], replicated
Inputs may be any that keep to these rules, and one draw needn't show every extreme that they name: `doc_lengths`: row g holds, in order, the lengths of the documents packed into the 384 positions of group g; they sum to 384 and the longest is 256. `cluster_perm`: for each group and head, a permutation of the group's positions. `masked`: 1 marks a position whose output gradient counts, 0 one whose gradient is zero.
All inputs are finite; a program needn't handle non-finite values.
Results may differ from a plain program's by a relative error of at most 0.014.
Values may be sent and summed in bfloat16 or wider, within the bound.
No kernel may reach another device: no remote copies, remote signals or barrier semaphores. Data moves between devices by JAX's collectives and lax.ppermute only.
A program may use at most 128 MiB of HBM per device.

v0:
```python
import jax
import jax.numpy as jnp
from jax import lax
from jax.sharding import PartitionSpec as P

HEAD = 64
CLUSTER = 128


norm_eps = 1e-05


def layer_norm(rows_in, gain_row, shift_row):
    center = jnp.mean(rows_in, axis=-1, keepdims=True)
    offset = rows_in - center
    spread = jnp.mean(offset * offset, axis=-1, keepdims=True)
    return offset * lax.rsqrt(spread + norm_eps) * gain_row + shift_row


def exact_gelu(values_in):
    return jax.nn.gelu(values_in, approximate=False)


def doc_index(lengths, row_count):
    bounds = jnp.cumsum(lengths)
    places = jnp.arange(row_count, dtype=jnp.int32)
    return jnp.sum((places[:, None] >= bounds[None, :]).astype(jnp.int32), axis=1)


def shards(
    tokens,
    project_weight,
    project_bias,
    output_weight,
    output_bias,
    expand_weight,
    expand_bias,
    shrink_weight,
    norm_gain,
    norm_shift,
    doc_lengths,
    cluster_perm,
    masked,
    out_grad,
):
    full_project, full_output, full_expand, full_shrink = (
        lax.all_gather(project_weight, "dp", axis=0, tiled=True),
        lax.all_gather(output_weight, "dp", axis=1, tiled=True),
        lax.all_gather(expand_weight, "dp", axis=0, tiled=True),
        lax.all_gather(shrink_weight, "dp", axis=1, tiled=True),
    )
    row_count = tokens.shape[0]
    columns = project_weight.shape[2]
    heads_here = columns // HEAD
    blocks = row_count // CLUSTER
    score_scale = HEAD ** (-0.5)
    perm_rows = cluster_perm[0]
    doc_ids = doc_index(doc_lengths[0], row_count)
    head_rows = jnp.arange(heads_here, dtype=jnp.int32)[:, None]

    def to_clusters(matrix):
        by_head = matrix.reshape(row_count, heads_here, HEAD)
        picked = by_head[perm_rows, head_rows]
        return picked.reshape(heads_here, blocks, CLUSTER, HEAD)

    def from_clusters(matrix):
        flat_rows = matrix.reshape(heads_here, row_count, HEAD)
        placed = jnp.zeros_like(flat_rows).at[head_rows, perm_rows].set(flat_rows)
        return placed.transpose(1, 0, 2).reshape(row_count, columns)

    doc_perm = doc_ids[perm_rows].reshape(heads_here, blocks, CLUSTER)
    same_doc = doc_perm[..., :, None] == doc_perm[..., None, :]

    def scored(q_view, k_view):
        raw_scores = (
            jnp.einsum("hcqe,hcke->hcqk", q_view, k_view, preferred_element_type=jnp.float32)
            * score_scale
        )
        return jnp.where(same_doc, raw_scores, -1e30)

    projected = jnp.einsum("td,dcf->tcf", tokens, full_project, preferred_element_type=jnp.float32)
    queries = (projected[:, 0] + project_bias[0]).astype(jnp.bfloat16)
    keys_rows = projected[:, 1].astype(jnp.bfloat16)
    values = (projected[:, 2] + project_bias[1]).astype(jnp.bfloat16)
    q_parts = to_clusters(queries)
    k_parts = to_clusters(keys_rows)
    v_parts = to_clusters(values)
    scores = scored(q_parts, k_parts)
    row_top = jnp.max(scores, axis=-1, keepdims=True)
    exp_terms = jnp.exp(scores - row_top)
    totals = jnp.sum(exp_terms, axis=-1, keepdims=True)
    prob_low = (exp_terms / totals).astype(jnp.bfloat16)
    log_total = row_top + jnp.log(totals)
    mixed_rows = jnp.einsum(
        "hcqk,hcke->hcqe", prob_low, v_parts, preferred_element_type=jnp.float32
    )
    attended = from_clusters(mixed_rows).astype(jnp.bfloat16)
    attention = (
        lax.psum(jnp.dot(attended, full_output, preferred_element_type=jnp.float32), "tensor")
        + output_bias[0]
    )
    residual_one = tokens.astype(jnp.float32) + attention
    first_norm, norm_one_back = jax.vjp(layer_norm, residual_one, norm_gain[0], norm_shift[0])
    first_low = first_norm.astype(jnp.bfloat16)
    inner_pre = jnp.dot(first_low, full_expand, preferred_element_type=jnp.float32) + expand_bias
    active, gelu_back = jax.vjp(exact_gelu, inner_pre)
    active_low = active.astype(jnp.bfloat16)
    feed_out = (
        lax.psum(jnp.dot(active_low, full_shrink, preferred_element_type=jnp.float32), "tensor")
        + output_bias[1]
    )
    layer_out, norm_two_back = jax.vjp(
        layer_norm, first_norm + feed_out, norm_gain[1], norm_shift[1]
    )
    seed_grad = out_grad.astype(jnp.float32) * masked.astype(jnp.float32)[:, None]
    residual_two_grad, gain_two_grad, shift_two_grad = norm_two_back(seed_grad)
    feed_low = residual_two_grad.astype(jnp.bfloat16)
    shrink_grad = jnp.einsum("tf,td->fd", active_low, feed_low, preferred_element_type=jnp.float32)
    active_grad = jnp.einsum("td,fd->tf", feed_low, full_shrink, preferred_element_type=jnp.float32)
    (inner_grad,) = gelu_back(active_grad)
    inner_low = inner_grad.astype(jnp.bfloat16)
    expand_grad = jnp.einsum("td,tf->df", first_low, inner_low, preferred_element_type=jnp.float32)
    expand_bias_grad = jnp.sum(inner_low, axis=0, dtype=jnp.float32)
    first_grad = (
        lax.psum(
            jnp.einsum("tf,df->td", inner_low, full_expand, preferred_element_type=jnp.float32),
            "tensor",
        )
        + residual_two_grad
    )
    residual_one_grad, gain_one_grad, shift_one_grad = norm_one_back(first_grad)
    attention_low = residual_one_grad.astype(jnp.bfloat16)
    output_grad = jnp.einsum(
        "tc,td->cd", attended, attention_low, preferred_element_type=jnp.float32
    )
    attended_grad = jnp.einsum(
        "td,cd->tc", attention_low, full_output, preferred_element_type=jnp.float32
    ).astype(jnp.bfloat16)
    grad_parts = to_clusters(attended_grad)
    probs_full = jnp.exp(scored(q_parts, k_parts) - log_total)
    probs_low = probs_full.astype(jnp.bfloat16)
    value_grad = jnp.einsum(
        "hcqk,hcqe->hcke", probs_low, grad_parts, preferred_element_type=jnp.float32
    )
    probs_grad = jnp.einsum(
        "hcqe,hcke->hcqk", grad_parts, v_parts, preferred_element_type=jnp.float32
    )
    center_term = jnp.sum(probs_grad * probs_full, axis=-1, keepdims=True)
    score_low = (probs_full * (probs_grad - center_term)).astype(jnp.bfloat16)
    query_grad = (
        jnp.einsum("hcqk,hcke->hcqe", score_low, k_parts, preferred_element_type=jnp.float32)
        * score_scale
    )
    keys_grad = (
        jnp.einsum("hcqk,hcqe->hcke", score_low, q_parts, preferred_element_type=jnp.float32)
        * score_scale
    )
    project_low = jnp.stack(
        [from_clusters(query_grad), from_clusters(keys_grad), from_clusters(value_grad)], axis=1
    ).astype(jnp.bfloat16)
    project_grad = jnp.einsum(
        "td,tcf->dcf", tokens, project_low, preferred_element_type=jnp.float32
    )
    project_bias_grad = jnp.sum(project_low[:, 0::2], axis=0, dtype=jnp.float32)
    tokens_grad = (
        lax.psum(
            jnp.einsum(
                "tcf,dcf->td", project_low, full_project, preferred_element_type=jnp.float32
            ).astype(jnp.bfloat16),
            "tensor",
        ).astype(jnp.float32)
        + residual_one_grad
    )
    output_bias_grad = jnp.stack(
        [jnp.sum(residual_one_grad, axis=0), jnp.sum(residual_two_grad, axis=0)]
    )
    gain_stack = jnp.stack([gain_one_grad, gain_two_grad])
    shift_stack = jnp.stack([shift_one_grad, shift_two_grad])
    vector_sums = lax.psum(
        (project_bias_grad, output_bias_grad, expand_bias_grad, gain_stack, shift_stack), "dp"
    )
    project_part, output_part, expand_part, shrink_part = (
        lax.psum_scatter(project_grad, "dp", scatter_dimension=0, tiled=True),
        lax.psum_scatter(output_grad, "dp", scatter_dimension=1, tiled=True),
        lax.psum_scatter(expand_grad, "dp", scatter_dimension=0, tiled=True),
        lax.psum_scatter(shrink_grad, "dp", scatter_dimension=1, tiled=True),
    )
    return (
        layer_out.astype(jnp.bfloat16),
        tokens_grad,
        project_part,
        vector_sums[0],
        output_part,
        vector_sums[1],
        expand_part,
        vector_sums[2],
        shrink_part,
        vector_sums[3],
        vector_sums[4],
    )


def solution(mesh):
    in_specs = (
        P("dp", None),
        P("dp", None, "tensor"),
        P(None, "tensor"),
        P("tensor", "dp"),
        P(),
        P("dp", "tensor"),
        P("tensor"),
        P("tensor", "dp"),
        P(),
        P(),
        P("dp", None),
        P("dp", "tensor", None),
        P("dp"),
        P("dp", None),
    )
    out_specs = (
        P("dp", None),
        P("dp", None),
        P("dp", None, "tensor"),
        P(None, "tensor"),
        P("tensor", "dp"),
        P(),
        P("dp", "tensor"),
        P("tensor"),
        P("tensor", "dp"),
        P(),
        P(),
    )
    return jax.shard_map(shards, mesh=mesh, in_specs=in_specs, out_specs=out_specs, check_vma=False)
```

profile of v0, /device:TPU:0, one launch (start us, length us, event | category | flops | bytes accessed | tf_op | source)
XLA Modules:
  0.0 792.1 jit_solution(7437251646926809812)
XLA Ops:
  11.2 13.9 %gather_fusion = s32[2304]{0:T(1024)S(1)} fusion(s32[384]{0:T(512)S(1)} %convert_reduce_fusion.2, s32[3072]{0:T(1024)S(1)} %pad_clamp_fusion), kind=kCustom, calls=%fused_computation | custom fusion | bytes 27648 | tf_op jit(solution)/shard_map/gather | solution.py:71
  26.6 25.1 %all_gather.13 = bf16[384,768]{0,1:T(8,128)(2,1)S(1)} all-gather(bf16[384,48]{0,1:T(8,128)(2,1)S(1)} %copy-done.33), channel_id=1, replica_groups=mesh['dp'=16,'tensor'=2] {'dp'}, dimensions={1}, use_global_device_ids=true | all-gather | bytes 626688 | tf_op jit(solution)/shard_map/all_gather | solution.py:48
  59.9 11.6 %gather_fusion.2 = bf16[2304,64]{1,0:T(8,128)(2,1)S(1)} fusion(bf16[384,6,64]{2,0,1:T(8,128)(2,1)S(1)} %copy.185, s32[2304]{0:T(1024)S(1)} %reshape.248), kind=kCustom, calls=%fused_computation.2 | custom fusion | bytes 608256 | tf_op jit(solution)/shard_map/gather | solution.py:63
  72.4 16.9 %gather_fusion.3 = bf16[2304,64]{1,0:T(8,128)(2,1)} fusion(bf16[384,6,64]{2,0,1:T(8,128)(2,1)S(1)} %add_convert_fusion.2, s32[2304]{0:T(1024)S(1)} %reshape.248), kind=kCustom, calls=%fused_computation.3 | custom fusion | bytes 608256 | tf_op jit(solution)/shard_map/gather | solution.py:63
  89.7 11.6 %gather_fusion.1 = bf16[2304,64]{1,0:T(8,128)(2,1)S(1)} fusion(bf16[384,6,64]{2,0,1:T(8,128)(2,1)S(1)} %add_convert_fusion.3, s32[2304]{0:T(1024)S(1)} %reshape.248), kind=kCustom, calls=%fused_computation.1 | custom fusion | bytes 608256 | tf_op jit(solution)/shard_map/gather | solution.py:63
  106.0 10.2 %scatter_custom_fusion = f32[2304,64]{1,0:T(8,128)S(1)} fusion(s32[2304]{0:T(1024)} %reshape.272, f32[2304,64]{1,0:T(8,128)} %bitcast.98, f32[]{:T(128)} %constant.39.clone.1), kind=kCustom, calls=%fused_computation.80 | custom fusion | bytes 590336
  122.5 39.2 %all-reduce.8.cloned.1.call-done = f32[384,768]{1,0:T(8,128)} async-done(((f32[384,768]{1,0:T(8,128)}), f32[384,768]{1,0:T(8,128)}) %all-reduce.8.cloned.1.call-update) | async-done | bytes 1179664 | tf_op jit(solution)/shard_map/psum | solution.py:99
  164.1 42.5 %all-gather.6.cloned.1.call-done = bf16[768,1536]{1,0:T(8,128)(2,1)} async-done(((bf16[48,1536]{1,0:T(8,128)(2,1)}), bf16[768,1536]{1,0:T(8,128)(2,1)}) %all-gather.6.cloned.1.call-update) | async-done | bytes 2359312 | tf_op jit(solution)/shard_map/all_gather | solution.py:49
  206.6 9.1 %multiply_convert_fusion = (bf16[384,1536]{1,0:T(8,128)(2,1)S(1)}, f32[384,1536]{1,0:T(8,128)}, f32[384,1536]{1,0:T(8,128)}) fusion(f32[1536]{0:T(1024)} %param.20, bf16[768,1536]{1,0:T(8,128)(2,1)} %all-gather.6.cloned.1.call-done, f32[384,768]{1,0:T(8,128)S(1)} %get-tuple-element.108, f32[768]{0:T(1024)} %get-tuple-element.88, ...), kind=kOutput, calls=%fused_computation.14 | convolution fusion | flops 946372608 | bytes 9452544 | tf_op jit(solution)/shard_map/dot_general | solution.py:105
  215.7 34.4 %all-gather.8.cloned.1.call-done = bf16[1536,768]{0,1:T(8,128)(2,1)} async-done(((bf16[1536,48]{0,1:T(8,128)(2,1)}), bf16[1536,768]{0,1:T(8,128)(2,1)}) %all-gather.8.cloned.1.call-update) | async-done | bytes 2359312 | tf_op jit(solution)/shard_map/all_gather | solution.py:50
  254.6 41.2 %all-reduce.10.cloned.1.call-done = f32[384,768]{1,0:T(8,128)} async-done(((f32[384,768]{1,0:T(8,128)}), f32[384,768]{1,0:T(8,128)}) %all-reduce.10.cloned.1.call-update) | async-done | bytes 1179664 | tf_op jit(solution)/shard_map/psum | solution.py:109
  309.4 41.5 %all-reduce.12.cloned.1.call-done = f32[384,768]{1,0:T(8,128)} async-done(((f32[384,768]{1,0:T(8,128)}), f32[384,768]{1,0:T(8,128)}) %all-reduce.12.cloned.1.call-update) | async-done | bytes 1179664 | tf_op jit(solution)/shard_map/psum | solution.py:125
  355.5 11.6 %gather_fusion.4 = bf16[2304,64]{1,0:T(8,128)(2,1)S(1)} fusion(bf16[384,6,64]{2,0,1:T(8,128)(2,1)S(1)} %copy.195, s32[2304]{0:T(1024)S(1)} %reshape.248), kind=kCustom, calls=%fused_computation.4 | custom fusion | bytes 608256 | tf_op jit(solution)/shard_map/gather | solution.py:63
  373.4 10.2 %scatter_custom_fusion.3 = f32[2304,64]{1,0:T(8,128)S(1)} fusion(s32[2304]{0:T(1024)} %reshape.272, f32[2304,64]{1,0:T(8,128)} %bitcast.91, f32[]{:T(128)} %constant.39.clone.1), kind=kCustom, calls=%fused_computation.74 | custom fusion | bytes 590336
  386.4 10.5 %scatter_custom_fusion.1 = f32[2304,64]{1,0:T(8,128)S(1)} fusion(s32[2304]{0:T(1024)} %reshape.272, f32[2304,64]{1,0:T(8,128)} %bitcast.93, f32[]{:T(128)} %constant.39.clone.1), kind=kCustom, calls=%fused_computation.78 | custom fusion | bytes 590336
  399.1 10.2 %scatter_custom_fusion.2 = f32[2304,64]{1,0:T(8,128)S(1)} fusion(s32[2304]{0:T(1024)} %reshape.272, f32[2304,64]{1,0:T(8,128)} %bitcast.92, f32[]{:T(128)} %constant.39.clone.1), kind=kCustom, calls=%fused_computation.76 | custom fusion | bytes 590336
  416.4 6.3 copy.220
  426.4 5.1 fusion.33
  432.8 4.9 fusion.30
  446.0 63.4 %all-reduce.1 = (f32[2,384]{1,0:T(2,128)}, f32[2,768]{1,0:T(2,128)}, f32[1536]{0:T(1024)}, f32[2,768]{1,0:T(2,128)}, f32[2,768]{1,0:T(2,128)}) all-reduce(f32[2,384]{1,0:T(2,128)S(1)} %convert_reduce_fusion.1, f32[2,768]{1,0:T(2,128)S(1)} %get-tuple-element.123, ...), channel_id=1, replica_groups=mesh['dp'=16,'tensor'=2] {'dp'}, use_global_device_ids=true, to_apply=%region_23.24 | all-reduce | flops 6912 | bytes 55296 | tf_op jit(solution)/shard_map/psum | solution.py:179
  509.3 55.4 %all-reduce.16.cloned.1.call-done = f32[768,3,384]{2,1,0:T(4,128)} async-done(((f32[768,3,384]{2,1,0:T(4,128)}), f32[768,3,384]{2,1,0:T(4,128)}) %all-reduce.16.cloned.1.call-update) | async-done | bytes 3538960
  566.4 60.3 %reduce-scatter.4.cloned.1.call-done = f32[384,48]{0,1:T(8,128)} async-done(((f32[384,768]{0,1:T(8,128)}), f32[384,48]{0,1:T(8,128)}) %reduce-scatter.4.cloned.1.call-update) | async-done | bytes 73744 | tf_op jit(solution)/shard_map/reduce_scatter | solution.py:184
  626.7 78.9 %reduce-scatter.6.cloned.1.call-done = f32[48,1536]{1,0:T(8,128)} async-done(((f32[768,1536]{1,0:T(8,128)}), f32[48,1536]{1,0:T(8,128)}) %reduce-scatter.6.cloned.1.call-update) | async-done | bytes 294928 | tf_op jit(solution)/shard_map/reduce_scatter | solution.py:185
  705.6 79.6 %reduce-scatter.8.cloned.1.call-done = f32[1536,48]{0,1:T(8,128)} async-done(((f32[1536,768]{0,1:T(8,128)}), f32[1536,48]{0,1:T(8,128)}) %reduce-scatter.8.cloned.1.call-update) | async-done | bytes 294928 | tf_op jit(solution)/shard_map/reduce_scatter | solution.py:186
  (236 shorter events, 83.0 us)
Async XLA Ops:
  7.2 47.7 %all-gather.4.cloned.1.call-start = ((), (), s32[]{:S(2)}) async-start(), calls=%async_computation.3 | async-start | bytes 1880064 | tf_op jit(solution)/shard_map/all_gather | solution.py:47
  7.9 153.8 %all-reduce.8.cloned.1.call-start = ((), (), s32[]{:S(2)}) async-start(), calls=%async_computation.4 | async-start | bytes 2359296 | tf_op jit(solution)/shard_map/psum | solution.py:99
  11.2 43.6 %copy-start.9 = (bf16[384,768]{1,0:T(8,128)(2,1)S(1)}, bf16[384,768]{1,0:T(8,128)(2,1)}, u32[]{:S(2)}) copy-start(bf16[384,768]{1,0:T(8,128)(2,1)} %param.14) | copy-start | bytes 1769476
  51.7 65.1 %copy-start.4 = (bf16[384,768]{0,1:T(8,128)(2,1)}, bf16[384,768]{0,1:T(8,128)(2,1)S(1)}, u32[]{:S(2)}) copy-start(bf16[384,768]{0,1:T(8,128)(2,1)S(1)} %all_gather.13) | copy-start | bytes 1769476
  71.5 29.8 %copy-start.12 = (bf16[2304,64]{1,0:T(8,128)(2,1)}, bf16[2304,64]{1,0:T(8,128)(2,1)S(1)}, u32[]{:S(2)}) copy-start(bf16[2304,64]{1,0:T(8,128)(2,1)S(1)} %gather_fusion.2) | copy-start | bytes 884740
  119.1 42.6 %copy-start.10 = (bf16[384,768]{1,0:T(8,128)(2,1)S(1)}, bf16[384,768]{1,0:T(8,128)(2,1)}, u32[]{:S(2)}) copy-start(bf16[384,768]{1,0:T(8,128)(2,1)} %param.14) | copy-start | bytes 1769476
  119.1 87.5 %all-gather.6.cloned.1.call-start = ((), (), s32[]{:S(2)}) async-start(), calls=%async_computation.5 | async-start | bytes 2506752 | tf_op jit(solution)/shard_map/all_gather | solution.py:49
  119.8 130.3 %all-gather.8.cloned.1.call-start = ((), (), s32[]{:S(2)}) async-start(), calls=%async_computation.6 | async-start | bytes 2506752 | tf_op jit(solution)/shard_map/all_gather | solution.py:50
  120.4 175.4 %all-reduce.10.cloned.1.call-start = ((), (), s32[]{:S(2)}) async-start(), calls=%async_computation.7 | async-start | bytes 2359296 | tf_op jit(solution)/shard_map/psum | solution.py:109
  163.2 43.4 %copy-start.23 = (f32[384]{0:T(512)}, f32[384]{0:T(512)S(1)}, u32[]{:S(2)}) copy-start(f32[384]{0:T(512)S(1)} %broadcast_multiply_fusion.1) | copy-start | bytes 4612
  163.5 43.1 %copy-start.37 = (f32[384]{0:T(512)}, f32[384]{0:T(512)S(1)}, u32[]{:S(2)}) copy-start(f32[384]{0:T(512)S(1)} %multiply_reduce_fusion.6) | copy-start | bytes 4612
  215.7 38.2 %copy-start.8 = (bf16[384,1536]{1,0:T(8,128)(2,1)}, bf16[384,1536]{1,0:T(8,128)(2,1)S(1)}, u32[]{:S(2)}) copy-start(bf16[384,1536]{1,0:T(8,128)(2,1)S(1)} %get-tuple-element.105) | copy-start | bytes 3538948
  253.9 41.9 %copy-start.21 = (f32[768]{0:T(1024)S(1)}, f32[768]{0:T(1024)}, u32[]{:S(2)}) copy-start(f32[768]{0:T(1024)} %get-tuple-element.88) | copy-start | bytes 9220
  253.9 41.9 %copy-start.24 = (f32[384]{0:T(512)S(1)}, f32[384]{0:T(512)}, u32[]{:S(2)}) copy-start(f32[384]{0:T(512)} %copy-done.23) | copy-start | bytes 4612
  253.9 41.9 %copy-start.27 = (f32[384]{0:T(512)S(1)}, f32[384]{0:T(512)}, u32[]{:S(2)}) copy-start(f32[384]{0:T(512)} %fusion.28) | copy-start | bytes 4612
  253.9 41.9 %copy-start.42 = (f32[768]{0:T(1024)S(1)}, f32[768]{0:T(1024)}, u32[]{:S(2)}) copy-start(f32[768]{0:T(1024)} %get-tuple-element.89) | copy-start | bytes 9220
  254.0 96.9 %all-reduce.12.cloned.1.call-start = ((), (), s32[]{:S(2)}) async-start(), calls=%async_computation.8 | async-start | bytes 2359296 | tf_op jit(solution)/shard_map/psum | solution.py:125
  254.6 43.4 %copy-start.36 = (f32[384]{0:T(512)}, f32[384]{0:T(512)S(1)}, u32[]{:S(2)}) copy-start(f32[384]{0:T(512)S(1)} %convert_element_type.90) | copy-start | bytes 4612
  302.2 48.6 %copy-start.2 = (f32[384,768]{1,0:T(8,128)}, f32[384,768]{1,0:T(8,128)S(1)}, u32[]{:S(2)}) copy-start(f32[384,768]{1,0:T(8,128)S(1)} %get-tuple-element.102) | copy-start | bytes 3538948
  307.8 135.8 %all-reduce.14.cloned.1.call-start = ((), (), s32[]{:S(2)}) async-start(), calls=%async_computation.9 | async-start | bytes 1179648 | tf_op jit(solution)/shard_map/psum | solution.py:166
  413.5 151.3 %all-reduce.16.cloned.1.call-start = ((), (), s32[]{:S(2)}) async-start(), calls=%async_computation.13 | async-start | bytes 9437184
  422.7 204.0 %reduce-scatter.4.cloned.1.call-start = ((), (), s32[]{:S(2)}) async-start(), calls=%async_computation.10 | async-start | bytes 1253376 | tf_op jit(solution)/shard_map/reduce_scatter | solution.py:184
  425.8 279.8 %reduce-scatter.6.cloned.1.call-start = ((), (), s32[]{:S(2)}) async-start(), calls=%async_computation.11 | async-start | bytes 5013504 | tf_op jit(solution)/shard_map/reduce_scatter | solution.py:185
  431.5 353.6 %reduce-scatter.8.cloned.1.call-start = ((), (), s32[]{:S(2)}) async-start(), calls=%async_computation.12 | async-start | bytes 5013504 | tf_op jit(solution)/shard_map/reduce_scatter | solution.py:186
  (47 other events, 128.2 us)
Sparse Core Ops, SparseCore 0:
  10.3 44.4 all-gather.3
  119.2 42.4 all-reduce.7
  164.2 42.3 all-gather.5
  209.0 41.0 all-gather.7
  254.1 41.6 all-reduce.9
  307.9 42.8 all-reduce.11
  413.6 29.9 all-reduce.13
  447.2 117.4 all-reduce.15
  568.9 57.7 reduce-scatter.3
  631.0 74.5 reduce-scatter.5
  710.5 74.5 reduce-scatter.7
where the time goes:
time: 801 us; the launch traced here: 792 us
  waiting for transfers between devices  482 us (60%)
  local copies, waits for them, and re-layouts  139 us (17%)
  blocking collectives  88.5 us (11%)
  matrix products  48.3 us (6%)
  other arithmetic  18.2 us (2%)
  between operations  15.8 us (2%)
    reduce_scatter x1, waiting for transfers between devices, shards(): lax.psum_scatter(shrink_grad, 'dp', scatter_dimension=1, tiled=True)  79.6 us
    reduce_scatter x1, waiting for transfers between devices, shards(): lax.psum_scatter(expand_grad, 'dp', scatter_dimension=0, tiled=True)  78.9 us
    psum x1, blocking collectives, shards(): lax.psum((project_bias_grad, output_bias_grad, expand_bias_grad, gain_sta...  63.4 us
    reduce_scatter x1, waiting for transfers between devices, shards(): lax.psum_scatter(output_grad, 'dp', scatter_dimension=1, tiled=True)  60.3 us
    unnamed x12, waiting for transfers between devices  57.4 us
    unnamed x132, local copies, waits for them, and re-layouts  54.9 us
    gather x4, local copies, waits for them, and re-layouts, to_clusters(): picked = by_head[perm_rows, head_rows]  51.6 us
    all_gather x1, waiting for transfers between devices, shards(): lax.all_gather(expand_weight, 'dp', axis=0, tiled=True)  42.5 us
  transfers between devices with their start and end apart: 11, of which 11 were waited for; matrix products, arithmetic and copies ran while one was open for 7% of the time, Pallas kernels for 0%

commit v1 on v0

v1 whole, which is shorter than its diff:
```python
import functools

import jax
import jax.numpy as jnp
from jax import lax
from jax.experimental import pallas as pl
from jax.experimental.pallas import tpu as pltpu
from jax.sharding import PartitionSpec as P

HEAD = 64
CLUSTER = 128
PAIR = 128
NORM_EPS = 1e-05
EXCLUDED = -1e30
VMEM_BYTES = 50 * 1024 * 1024

F32 = jnp.float32
BF16 = jnp.bfloat16

NN = (((1,), (0,)), ((), ()))
NT = (((1,), (1,)), ((), ()))
TN = (((0,), (0,)), ((), ()))


def dot(a, b, dims=NN):
    return lax.dot_general(a, b, dims, preferred_element_type=F32)


def swap(array, axis, offset, size):
    return lax.ppermute(array, axis, [(i, i ^ offset) for i in range(size)])


def gather_pieces(shard, dp):
    pieces = {0: shard}
    for base in range(4, dp, 4):
        pieces[base] = swap(shard, "dp", base, dp)
    for offset in sorted(pieces):
        pieces[offset ^ 2] = swap(pieces[offset], "dp", 2, dp)
    for offset in sorted(pieces):
        pieces[offset ^ 1] = swap(pieces[offset], "dp", 1, dp)
    return [pieces[o] for o in range(dp)]


def scatter_sum(keep, send, dp):
    quarter = dp // 4
    got = swap(send, "dp", 1, dp)
    total = keep.astype(F32) + got.astype(F32)
    got = swap(total[quarter:].astype(BF16), "dp", 2, dp)
    total = total[:quarter] + got.astype(F32)
    out = total[0]
    for k in range(1, quarter):
        out = out + swap(total[k].astype(BF16), "dp", 4 * k, dp).astype(F32)
    return out


def sum_all(vector, dp):
    offset = 1
    while offset < dp:
        vector = vector + swap(vector, "dp", offset, dp)
        offset *= 2
    return vector


def other_half(array):
    return lax.ppermute(array, "tensor", [(0, 1), (1, 0)])


def any_spec():
    return pl.BlockSpec(memory_space=pl.ANY)


def vmem_spec():
    return pl.BlockSpec(memory_space=pltpu.VMEM)


def smem_spec():
    return pl.BlockSpec(memory_space=pltpu.SMEM)


def call(body, outs, ins, name, scratch=(), flops=0, nbytes=0, in_specs=None):
    if in_specs is None:
        in_specs = [vmem_spec()] * len(ins)
    return pl.pallas_call(
        body,
        out_shape=tuple(jax.ShapeDtypeStruct(s, d) for s, d in outs),
        in_specs=in_specs,
        out_specs=tuple(vmem_spec() for _ in outs),
        scratch_shapes=list(scratch),
        compiler_params=pltpu.CompilerParams(vmem_limit_bytes=VMEM_BYTES),
        cost_estimate=pl.CostEstimate(flops=flops, bytes_accessed=nbytes, transcendentals=0),
        name=name,
    )(*ins)


def fetch(pieces, whole, sems):
    count = len(pieces)
    copies = []
    me = lax.axis_index("dp") if count > 1 else 0
    for o, piece in enumerate(pieces):
        rows = piece.shape[-2]
        start = pl.multiple_of((me ^ o) * rows, 16) if count > 1 else 0
        if len(piece.shape) == 3:
            target = whole.at[:, pl.ds(start, rows), :]
        else:
            target = whole.at[pl.ds(start, rows), :]
        copy = pltpu.make_async_copy(piece, target, sems.at[o])
        copy.start()
        copies.append(copy)
    return copies


def arrive(copies):
    for copy in copies:
        copy.wait()


def norm_rows(v):
    center = jnp.mean(v, axis=-1, keepdims=True)
    offset = v - center
    spread = jnp.mean(offset * offset, axis=-1, keepdims=True)
    scale = lax.rsqrt(spread + NORM_EPS)
    return offset * scale, scale


def norm_back(e, n, scale, gain):
    ea = e * gain
    return scale * (
        ea
        - jnp.mean(ea, axis=-1, keepdims=True)
        - n * jnp.mean(ea * n, axis=-1, keepdims=True)
    )


def admitted_kernel(heads, docs, lengths_ref, perm_ref, bias_ref):
    rows = bias_ref.shape[1]
    spot = lax.broadcasted_iota(jnp.int32, (rows, PAIR), 0)
    lane = lax.broadcasted_iota(jnp.int32, (rows, PAIR), 1)
    doc = jnp.zeros((rows, PAIR), jnp.int32)
    bound = jnp.int32(0)
    for k in range(docs):
        bound = bound + lengths_ref[0, k]
        doc = doc + (spot >= bound).astype(jnp.int32)
    doc_hot = (lane == doc + PAIR // 2).astype(F32)
    cluster_hot = (lane == spot // CLUSTER).astype(BF16)
    place = lax.broadcasted_iota(jnp.int32, (rows, rows), 0)
    for h in range(heads):
        here = (place == perm_ref[h : h + 1, :]).astype(BF16)
        key = (dot(here, cluster_hot) + doc_hot).astype(BF16)
        same = dot(key, key, NT)
        bias_ref[h] = jnp.where(same > 1.5, 0.0, EXCLUDED).astype(BF16)


def attention_kernel(count, heads, scale, *refs):
    pieces, refs = refs[:count], refs[count:]
    tokens_ref, bias_ref, admit_ref, qkv_ref, prob_ref, out_ref, whole, sems = refs
    arrive(fetch(pieces, whole, sems))
    tokens = tokens_ref[...]
    for s in range(3):
        part = dot(tokens, whole[s])
        if s == 0:
            part = part + bias_ref[0:1, :]
        if s == 2:
            part = part + bias_ref[1:2, :]
        qkv_ref[s] = part.astype(BF16)
    lane = lax.broadcasted_iota(jnp.int32, (tokens.shape[0], PAIR), 1)
    for pair in range(heads // 2):
        columns = slice(pair * PAIR, (pair + 1) * PAIR)
        q = qkv_ref[0, :, columns]
        k = qkv_ref[1, :, columns]
        v = qkv_ref[2, :, columns]
        mixed = []
        for side in range(2):
            mine = (lane < HEAD) if side == 0 else (lane >= HEAD)
            scores = dot(jnp.where(mine, q, jnp.zeros_like(q)), k, NT) * scale
            scores = scores + admit_ref[2 * pair + side].astype(F32)
            top = jnp.max(scores, axis=-1, keepdims=True)
            terms = jnp.exp(scores - top)
            total = jnp.sum(terms, axis=-1, keepdims=True)
            prob = (terms * (1.0 / total)).astype(BF16)
            prob_ref[2 * pair + side] = prob
            mixed.append(dot(prob, v))
        out_ref[:, columns] = jnp.where(lane < HEAD, mixed[0], mixed[1]).astype(BF16)


def output_kernel(count, *refs):
    pieces, refs = refs[:count], refs[count:]
    attended_ref, out_ref, whole, sems = refs
    arrive(fetch(pieces, whole, sems))
    out_ref[...] = dot(attended_ref[...], whole[...], NT).astype(BF16)


def feed_kernel(count, *refs):
    expand, shrink, refs = refs[:count], refs[count : 2 * count], refs[2 * count :]
    (tokens_ref, own_ref, got_ref, out_bias_ref, gain_ref, shift_ref, bias_ref,
     n_ref, scale_ref, low_ref, active_ref, slope_ref, out_ref,
     expand_all, shrink_all, sems) = refs
    one = fetch(expand, expand_all, sems.at[0])
    two = fetch(shrink, shrink_all, sems.at[1])
    attention = own_ref[...].astype(F32) + got_ref[...].astype(F32) + out_bias_ref[0:1, :]
    n, scale = norm_rows(tokens_ref[...].astype(F32) + attention)
    n_ref[...] = n
    scale_ref[...] = jnp.broadcast_to(scale, scale_ref.shape)
    low_ref[...] = (n * gain_ref[0:1, :] + shift_ref[0:1, :]).astype(BF16)
    arrive(one)
    units = expand_all.shape[1]
    step = 256
    for start in range(0, units, step):
        part = slice(start, start + step)
        pre = dot(low_ref[...], expand_all[:, part]) + bias_ref[:, part]
        half = 0.5 * (1.0 + lax.erf(pre * (2.0**-0.5)))
        active_ref[:, part] = (pre * half).astype(BF16)
        bell = jnp.exp(-0.5 * pre * pre) * 0.3989422804014327
        slope_ref[:, part] = (half + pre * bell).astype(BF16)
    arrive(two)
    out_ref[...] = dot(active_ref[...], shrink_all[...], NT).astype(BF16)


def feed_back_kernel(count, *refs):
    expand, shrink, refs = refs[:count], refs[count : 2 * count], refs[2 * count :]
    (n_ref, own_ref, got_ref, out_bias_ref, gain_ref, shift_ref, seed_ref, masked_ref, slope_ref,
     layer_ref, two_ref, low_ref, inner_ref, first_ref, sums_ref, inner_sum_ref,
     expand_all, shrink_all, sems) = refs
    two = fetch(shrink, shrink_all, sems.at[1])
    one = fetch(expand, expand_all, sems.at[0])
    first = n_ref[...] * gain_ref[0:1, :] + shift_ref[0:1, :]
    feed = own_ref[...].astype(F32) + got_ref[...].astype(F32) + out_bias_ref[1:2, :]
    n, scale = norm_rows(first + feed)
    gain = gain_ref[1:2, :]
    layer_ref[...] = (n * gain + shift_ref[1:2, :]).astype(BF16)
    e = seed_ref[...].astype(F32) * masked_ref[...]
    grad = norm_back(e, n, scale, gain)
    two_ref[...] = grad
    low_ref[...] = grad.astype(BF16)
    sums_ref[0:1, :] = jnp.sum(e * n, axis=0, keepdims=True)
    sums_ref[1:2, :] = jnp.sum(e, axis=0, keepdims=True)
    sums_ref[2:3, :] = jnp.sum(grad, axis=0, keepdims=True)
    arrive(two)
    units = shrink_all.shape[1]
    step = 256
    for start in range(0, units, step):
        part = slice(start, start + step)
        inner = (dot(low_ref[...], shrink_all[:, part]) * slope_ref[:, part].astype(F32)).astype(BF16)
        inner_ref[:, part] = inner
        inner_sum_ref[:, part] = jnp.sum(inner.astype(F32), axis=0, keepdims=True)
    arrive(one)
    first_ref[...] = dot(inner_ref[...], expand_all[...], NT).astype(BF16)


def weight_grad_kernel(dp, left_ref, right_ref, keep_ref, send_ref, whole):
    whole[...] = dot(left_ref[...], right_ref[...], TN)
    me = lax.axis_index("dp")
    rows = keep_ref.shape[1]
    for o in range(dp):
        z, x, c = o // 4, (o // 2) % 2, o % 2
        start = pl.multiple_of((me ^ o) * rows, 16)
        block = whole[pl.ds(start, rows), :].astype(BF16)
        target = send_ref if c else keep_ref
        target[x * (dp // 4) + z] = block


def norm_one_back_kernel(own_ref, got_ref, two_ref, n_ref, scale_ref, gain_ref, one_ref, low_ref, sums_ref):
    e = own_ref[...].astype(F32) + got_ref[...].astype(F32) + two_ref[...]
    n = n_ref[...]
    grad = norm_back(e, n, scale_ref[:, 0:1], gain_ref[0:1, :])
    one_ref[...] = grad
    low_ref[...] = grad.astype(BF16)
    sums_ref[0:1, :] = jnp.sum(e * n, axis=0, keepdims=True)
    sums_ref[1:2, :] = jnp.sum(e, axis=0, keepdims=True)
    sums_ref[2:3, :] = jnp.sum(grad, axis=0, keepdims=True)


def attention_back_kernel(count, heads, scale, *refs):
    pieces, refs = refs[:count], refs[count:]
    low_ref, qkv_ref, prob_ref, grads_ref, sums_ref, whole, given, sems = refs
    arrive(fetch(pieces, whole, sems))
    given[...] = dot(low_ref[...], whole[...]).astype(BF16)
    lane = lax.broadcasted_iota(jnp.int32, (given.shape[0], PAIR), 1)
    for pair in range(heads // 2):
        columns = slice(pair * PAIR, (pair + 1) * PAIR)
        q = qkv_ref[0, :, columns]
        k = qkv_ref[1, :, columns]
        v = qkv_ref[2, :, columns]
        d = given[:, columns]
        parts = []
        for side in range(2):
            mine = (lane < HEAD) if side == 0 else (lane >= HEAD)
            prob = prob_ref[2 * pair + side]
            d_prob = dot(jnp.where(mine, d, jnp.zeros_like(d)), v, NT)
            wide = prob.astype(F32)
            center = jnp.sum(d_prob * wide, axis=-1, keepdims=True)
            score = (wide * (d_prob - center)).astype(BF16)
            parts.append((dot(score, k), dot(score, q, TN), dot(prob, d, TN)))
        for s in range(3):
            both = jnp.where(lane < HEAD, parts[0][s], parts[1][s])
            if s < 2:
                both = both * scale
            both = both.astype(BF16)
            grads_ref[s, :, columns] = both
            if s != 1:
                sums_ref[s // 2 : s // 2 + 1, columns] = jnp.sum(both.astype(F32), axis=0, keepdims=True)


def input_grad_kernel(count, *refs):
    pieces, refs = refs[:count], refs[count:]
    grads_ref, out_ref, whole, sems = refs
    arrive(fetch(pieces, whole, sems))
    total = dot(grads_ref[0], whole[0], NT)
    total = total + dot(grads_ref[1], whole[1], NT)
    total = total + dot(grads_ref[2], whole[2], NT)
    out_ref[...] = total.astype(BF16)


def project_grad_kernel(dp, tokens_ref, grads_ref, keep_ref, send_ref, whole):
    me = lax.axis_index("dp")
    rows = keep_ref.shape[2]
    for s in range(3):
        whole[...] = dot(tokens_ref[...], grads_ref[s], TN)
        for o in range(dp):
            z, x, c = o // 4, (o // 2) % 2, o % 2
            start = pl.multiple_of((me ^ o) * rows, 16)
            block = whole[pl.ds(start, rows), :].astype(BF16)
            target = send_ref if c else keep_ref
            target[x * (dp // 4) + z, s] = block


def plain_grad_kernel(left_ref, right_ref, out_ref):
    out_ref[...] = dot(left_ref[...], right_ref[...], TN)


def shards(
    dp,
    tokens,
    project_weight,
    project_bias,
    output_weight,
    output_bias,
    expand_weight,
    expand_bias,
    shrink_weight,
    norm_gain,
    norm_shift,
    doc_lengths,
    cluster_perm,
    masked,
    out_grad,
):
    rows, width = tokens.shape
    piece_rows, _, columns = project_weight.shape
    units = expand_weight.shape[1]
    heads = columns // HEAD
    scale = HEAD ** (-0.5)
    in_pieces = dp >= 4 and dp & (dp - 1) == 0 and piece_rows % 16 == 0

    project_shard = project_weight.transpose(1, 0, 2)
    output_shard = output_weight.T
    shrink_shard = shrink_weight.T
    if in_pieces:
        project_all = gather_pieces(project_shard, dp)
        output_all = gather_pieces(output_shard, dp)
        expand_all = gather_pieces(expand_weight, dp)
        shrink_all = gather_pieces(shrink_shard, dp)
    else:
        project_all = [lax.all_gather(project_shard, "dp", axis=1, tiled=True)]
        output_all = [lax.all_gather(output_shard, "dp", axis=0, tiled=True)]
        expand_all = [lax.all_gather(expand_weight, "dp", axis=0, tiled=True)]
        shrink_all = [lax.all_gather(shrink_shard, "dp", axis=0, tiled=True)]
    count = len(project_all)

    def whole(*shape):
        return pltpu.VMEM(shape, BF16)

    def sems(*shape):
        return pltpu.SemaphoreType.DMA(shape)

    (admit,) = call(
        functools.partial(admitted_kernel, heads, doc_lengths.shape[1]),
        [((heads, rows, rows), BF16)],
        [doc_lengths, cluster_perm[0]],
        "admitted",
        in_specs=[smem_spec(), vmem_spec()],
        flops=2 * heads * rows * rows * 2 * PAIR,
        nbytes=2 * heads * rows * rows,
    )
    qkv, prob, attended = call(
        functools.partial(attention_kernel, count, heads, scale),
        [((3, rows, columns), BF16), ((heads, rows, rows), BF16), ((rows, columns), BF16)],
        [*project_all, tokens, project_bias, admit],
        "attention",
        scratch=[whole(3, width, columns), sems(count)],
        in_specs=[any_spec()] * count + [vmem_spec()] * 3,
        flops=2 * rows * width * 3 * columns + 4 * heads * rows * rows * PAIR,
        nbytes=6 * width * columns,
    )
    (attention_own,) = call(
        functools.partial(output_kernel, count),
        [((rows, width), BF16)],
        [*output_all, attended],
        "attention_output",
        scratch=[whole(width, columns), sems(count)],
        in_specs=[any_spec()] * count + [vmem_spec()],
        flops=2 * rows * width * columns,
        nbytes=2 * width * columns,
    )
    attention_got = other_half(attention_own)
    n_one, scale_one, first_low, active_low, slope, feed_own = call(
        functools.partial(feed_kernel, count),
        [
            ((rows, width), F32),
            ((rows, PAIR), F32),
            ((rows, width), BF16),
            ((rows, units), BF16),
            ((rows, units), BF16),
            ((rows, width), BF16),
        ],
        [
            *expand_all, *shrink_all, tokens, attention_own, attention_got, output_bias,
            norm_gain, norm_shift, expand_bias[None, :],
        ],
        "feed_forward",
        scratch=[whole(width, units), whole(width, units), sems(2, count)],
        in_specs=[any_spec()] * (2 * count) + [vmem_spec()] * 7,
        flops=4 * rows * width * units,
        nbytes=4 * width * units,
    )
    feed_got = other_half(feed_own)
    layer_out, residual_two, feed_low, inner_low, first_own, sums_two, inner_sum = call(
        functools.partial(feed_back_kernel, count),
        [
            ((rows, width), BF16),
            ((rows, width), F32),
            ((rows, width), BF16),
            ((rows, units), BF16),
            ((rows, width), BF16),
            ((3, width), F32),
            ((1, units), F32),
        ],
        [
            *expand_all, *shrink_all, n_one, feed_own, feed_got, output_bias,
            norm_gain, norm_shift, out_grad, masked.astype(F32)[:, None], slope,
        ],
        "feed_backward",
        scratch=[whole(width, units), whole(width, units), sems(2, count)],
        in_specs=[any_spec()] * (2 * count) + [vmem_spec()] * 9,
        flops=4 * rows * width * units,
        nbytes=4 * width * units,
    )
    first_got = other_half(first_own)

    def weight_grad(left, right, name):
        wide = right.shape[1]
        if in_pieces:
            keep, send = call(
                functools.partial(weight_grad_kernel, dp),
                [((dp // 2, piece_rows, wide), BF16)] * 2,
                [left, right],
                name,
                scratch=[pltpu.VMEM((width, wide), F32)],
                flops=2 * rows * width * wide,
                nbytes=2 * width * wide,
            )
            return scatter_sum(keep, send, dp)
        (grad,) = call(plain_grad_kernel, [((width, wide), F32)], [left, right], name)
        return lax.psum_scatter(grad, "dp", scatter_dimension=0, tiled=True)

    shrink_part = weight_grad(feed_low, active_low, "shrink_grad")
    expand_part = weight_grad(first_low, inner_low, "expand_grad")
    residual_one, attention_low, sums_one = call(
        norm_one_back_kernel,
        [((rows, width), F32), ((rows, width), BF16), ((3, width), F32)],
        [first_own, first_got, residual_two, n_one, scale_one, norm_gain],
        "norm_one_backward",
    )
    project_low, project_sums = call(
        functools.partial(attention_back_kernel, count, heads, scale),
        [((3, rows, columns), BF16), ((2, columns), F32)],
        [*output_all, attention_low, qkv, prob],
        "attention_backward",
        scratch=[whole(width, columns), whole(rows, columns), sems(count)],
        in_specs=[any_spec()] * count + [vmem_spec()] * 3,
        flops=2 * rows * width * columns + 8 * heads * rows * rows * PAIR,
        nbytes=2 * width * columns,
    )
    output_part = weight_grad(attention_low, attended, "output_grad")
    (tokens_own,) = call(
        functools.partial(input_grad_kernel, count),
        [((rows, width), BF16)],
        [*project_all, project_low],
        "input_grad",
        scratch=[whole(3, width, columns), sems(count)],
        in_specs=[any_spec()] * count + [vmem_spec()],
        flops=6 * rows * width * columns,
        nbytes=6 * width * columns,
    )
    tokens_got = other_half(tokens_own)
    if in_pieces:
        keep, send = call(
            functools.partial(project_grad_kernel, dp),
            [((dp // 2, 3, piece_rows, columns), BF16)] * 2,
            [tokens, project_low],
            "project_grad",
            scratch=[pltpu.VMEM((width, columns), F32)],
            flops=6 * rows * width * columns,
            nbytes=6 * width * columns,
        )
        project_part = scatter_sum(keep, send, dp)
    else:
        project_part = jnp.stack(
            [weight_grad(tokens, project_low[s], "project_grad") for s in range(3)]
        )
    tokens_grad = tokens_own.astype(F32) + tokens_got.astype(F32) + residual_one

    pieces = [sums_one, sums_two, inner_sum, project_sums]
    vector = jnp.concatenate([p.reshape(-1, PAIR) for p in pieces])
    vector = sum_all(vector, dp) if in_pieces else lax.psum(vector, "dp")
    ends, parts = 0, []
    for p in pieces:
        step = p.size // PAIR
        parts.append(vector[ends : ends + step].reshape(p.shape))
        ends += step
    one, two, inner_total, project_total = parts
    return (
        layer_out,
        tokens_grad,
        project_part.transpose(1, 0, 2),
        project_total,
        output_part.T,
        jnp.stack([one[2], two[2]]),
        expand_part,
        inner_total[0],
        shrink_part.T,
        jnp.stack([one[0], two[0]]),
        jnp.stack([one[1], two[1]]),
    )


def solution(mesh):
    in_specs = (
        P("dp", None),
        P("dp", None, "tensor"),
        P(None, "tensor"),
        P("tensor", "dp"),
        P(),
        P("dp", "tensor"),
        P("tensor"),
        P("tensor", "dp"),
        P(),
        P(),
        P("dp", None),
        P("dp", "tensor", None),
        P("dp"),
        P("dp", None),
    )
    out_specs = (
        P("dp", None),
        P("dp", None),
        P("dp", None, "tensor"),
        P(None, "tensor"),
        P("tensor", "dp"),
        P(),
        P("dp", "tensor"),
        P("tensor"),
        P("tensor", "dp"),
        P(),
        P(),
    )
    body = functools.partial(shards, mesh.shape["dp"])
    return jax.shard_map(body, mesh=mesh, in_specs=in_specs, out_specs=out_specs, check_vma=False)
```

time: 801 us -> 257 us (0.32)
  waiting for transfers between devices: 482 us -> 103 us
  local copies, waits for them, and re-layouts: 139 us -> 13.3 us
  blocking collectives: 88.5 us -> 0 us
  starting transfers between devices: 0.83 us -> 72.8 us
  Pallas kernels: 0 us -> 55.3 us
  matrix products: 48.3 us -> 0 us
  between operations: 15.8 us -> 1.65 us
  other arithmetic: 18.2 us -> 9.9 us
    reduce_scatter x3 -> x0, waiting for transfers between devices: 219 us -> none  [the longest x1 79.6 us: shards(): lax.psum_scatter(shrink_grad, 'dp', scatter_dimension=1, tiled=True)]
    psum x4 -> x0, waiting for transfers between devices: 126 us -> none  [the longest x1 41.5 us: shards(): lax.psum(jnp.einsum('tf,df->td', inner_low, full_expand, preferred_elemen...]
    ppermute x0 -> x88, waiting for transfers between devices: none -> 103 us  [the longest x84 75.6 us: swap(): return lax.ppermute(array, axis, [(i, i ^ offset) for i in range(size)])]
    all_gather x3 -> x0, waiting for transfers between devices: 80 us -> none  [the longest x1 42.5 us: shards(): lax.all_gather(expand_weight, 'dp', axis=0, tiled=True)]
    ppermute x0 -> x88, starting transfers between devices: none -> 72.8 us  [the longest x84 66.4 us: swap(): return lax.ppermute(array, axis, [(i, i ^ offset) for i in range(size)])]
    gather x5 -> x0, local copies, waits for them, and re-layouts: 65.6 us -> none  [the longest x4 51.6 us: to_clusters(): picked = by_head[perm_rows, head_rows]]
    psum x1 -> x0, blocking collectives: 63.4 us -> none  [shards(): lax.psum((project_bias_grad, output_bias_grad, expand_bias_grad, gain_sta...]
    unnamed x12 -> x0, waiting for transfers between devices: 57.4 us -> none
  transfers between devices with their start and end apart: 11 -> 88, of which waited for: 11 -> 32; matrix products, arithmetic and copies ran while one was open for 7% -> 5% of each run, Pallas kernels for 0% -> 8%
where the time goes in v1:
time: 257 us; the launch traced here: 256 us
  waiting for transfers between devices  103 us (40%)
  starting transfers between devices  72.8 us (28%)
  Pallas kernels  55.3 us (22%)
  local copies, waits for them, and re-layouts  13.3 us (5%)
  other arithmetic  9.9 us (4%)
    ppermute x84, waiting for transfers between devices, swap(): return lax.ppermute(array, axis, [(i, i ^ offset) for i in range(size)])  75.6 us
    ppermute x84, starting transfers between devices, swap(): return lax.ppermute(array, axis, [(i, i ^ offset) for i in range(size)])  66.4 us
    pallas_call x12, Pallas kernels, call(): pl.pallas_call(body, out_shape=tuple((jax.ShapeDtypeStruct(s, d) for s, d...  55.3 us
    ppermute x4, waiting for transfers between devices, other_half(): return lax.ppermute(array, 'tensor', [(0, 1), (1, 0)])  27.6 us
    unnamed x142, local copies, waits for them, and re-layouts  10.9 us
    ppermute x4, starting transfers between devices, other_half(): return lax.ppermute(array, 'tensor', [(0, 1), (1, 0)])  6.3 us
  transfers between devices with their start and end apart: 88, of which 32 were waited for; matrix products, arithmetic and copies ran while one was open for 5% of the time, Pallas kernels for 8%

profile of v1, /device:TPU:0, one launch (start us, length us, event | category | flops | bytes accessed | tf_op | source)
XLA Modules:
  0.0 256.1 jit_solution(9386668349692337503)
XLA Ops:
  0.7 5.1 %collective-permute-start.41 = (bf16[48,384]{1,0:T(8,128)(2,1)}, bf16[48,384]{1,0:T(8,128)(2,1)S(1)}, u32[]{:S(2)}, u32[]{:S(2)}) collective-permute-start(bf16[48,384]{1,0:T(8,128)(2,1)} %bitcast.122), channel_id=1, source_target_pairs={{0,24},{2,26},{4,28},{6,30},{8,16},{10,18},{12,20},{14,22},{16,8},... | collective-permute-start | bytes 110600 | tf_op jit(solution)/shard_map/ppermute | solution.py:30
  14.8 2.5 collective-permute-start.56
  24.2 3.5 %collective-permute-start.22 = (bf16[48,1536]{1,0:T(8,128)(2,1)}, bf16[48,1536]{1,0:T(8,128)(2,1)S(1)}, u32[]{:S(2)}, u32[]{:S(2)}) collective-permute-start(bf16[48,1536]{1,0:T(8,128)(2,1)} %bitcast.108), channel_id=1, source_target_pairs={{0,16},{2,18},{4,20},{6,22},{8,24},{10,26},{12,28},{14,30},{16,0},... | collective-permute-start | bytes 442376 | tf_op jit(solution)/shard_map/ppermute | solution.py:30
  27.6 6.7 %collective-permute-done.52.refs_8_ = bf16[3,48,384]{2,1,0:T(8,128)(2,1)S(1)} collective-permute-done((bf16[3,48,384]{2,1,0:T(8,128)(2,1)}, bf16[3,48,384]{2,1,0:T(8,128)(2,1)S(1)}, u32[]{:S(2)}, u32[]{:S(2)}) %collective-permute-start.52) | collective-permute-done | bytes 110624 | tf_op jit(solution)/shard_map/ppermute | solution.py:30
  38.0 2.8 %collective-permute-start.11 = (bf16[48,1536]{1,0:T(8,128)(2,1)}, bf16[48,1536]{1,0:T(8,128)(2,1)S(1)}, u32[]{:S(2)}, u32[]{:S(2)}) collective-permute-start(bf16[48,1536]{1,0:T(8,128)(2,1)} %refs_0_.3), channel_id=1, source_target_pairs={{0,24},{2,26},{4,28},{6,30},{8,16},{10,18},{12,20},{14,22},{16,8},... | collective-permute-start | bytes 442376 | tf_op jit(solution)/shard_map/ppermute | solution.py:30
  41.4 4.9 %collective-permute-done.18.refs_20_ = bf16[48,1536]{1,0:T(8,128)(2,1)S(1)} collective-permute-done((bf16[48,1536]{1,0:T(8,128)(2,1)}, bf16[48,1536]{1,0:T(8,128)(2,1)S(1)}, u32[]{:S(2)}, u32[]{:S(2)}) %collective-permute-start.18) | collective-permute-done | bytes 147488 | tf_op jit(solution)/shard_map/ppermute | solution.py:30
  48.3 7.0 %collective-permute-done.7.refs_8_ = bf16[48,1536]{1,0:T(8,128)(2,1)S(1)} collective-permute-done((bf16[48,1536]{1,0:T(8,128)(2,1)}, bf16[48,1536]{1,0:T(8,128)(2,1)S(1)}, u32[]{:S(2)}, u32[]{:S(2)}) %collective-permute-start.7) | collective-permute-done | bytes 147488 | tf_op jit(solution)/shard_map/ppermute | solution.py:30
  57.9 3.3 %collective-permute-done.54.refs_10_ = bf16[3,48,384]{2,1,0:T(8,128)(2,1)S(1)} collective-permute-done((bf16[3,48,384]{2,1,0:T(8,128)(2,1)S(1)}, bf16[3,48,384]{2,1,0:T(8,128)(2,1)S(1)}, u32[]{:S(2)}, u32[]{:S(2)}) %collective-permute-start.54) | collective-permute-done | bytes 110624 | tf_op jit(solution)/shard_map/ppermute | solution.py:30
  66.6 2.4 admitted.1.refs_18_
  70.3 7.5 %attention.1 = (bf16[3,384,384]{2,1,0:T(8,128)(2,1)S(1)}, bf16[6,384,384]{2,1,0:T(8,128)(2,1)}, bf16[384,384]{1,0:T(8,128)(2,1)S(1)}) custom-call(bf16[3,48,384]{2,1,0:T(8,128)(2,1)S(1)} %bitcast.119, bf16[3,48,384]{2,1,0:T(8,128)(2,1)S(1)} %collective-permute-done.45.refs_1_, bf16[3,48,384]{2,1,0:T(8,128)(2,1)S(1)} %collective-permute-done.46.refs_2_, ...), custom_call_target="tpu_custom_call" | custom-call | flops 1132462080 | bytes 1769472 | tf_op jit(solution)/shard_map/attention/pallas_call | solution.py:83
  87.7 3.7 %collective-permute-done.9.refs_10_ = bf16[48,1536]{1,0:T(8,128)(2,1)S(1)} collective-permute-done((bf16[48,1536]{1,0:T(8,128)(2,1)S(1)}, bf16[48,1536]{1,0:T(8,128)(2,1)S(1)}, u32[]{:S(2)}, u32[]{:S(2)}) %collective-permute-start.9) | collective-permute-done | bytes 147488 | tf_op jit(solution)/shard_map/ppermute | solution.py:30
  98.1 12.1 %feed_forward.1 = (f32[384,768]{1,0:T(8,128)}, f32[384,128]{1,0:T(8,128)}, bf16[384,768]{1,0:T(8,128)(2,1)}, bf16[384,1536]{1,0:T(8,128)(2,1)}, bf16[384,1536]{1,0:T(8,128)(2,1)}, /*index=5*/bf16[384,768]{1,0:T(8,128)(2,1)}) custom-call(bf16[48,1536]{1,0:T(8,128)(2,1)S(1)} %copy-done.10, bf16[48,1536]{1,0:T(8,128)(2,1)S(1)} %collective-permute-done.refs_1_, ...), custom_call_target="tpu_custom_call" | custom-call | flops 1811939328 | bytes 4718592 | tf_op jit(solution)/shard_map/feed_forward/pallas_call | solution.py:83
  112.6 13.0 %collective-permute-done.61.refs_34_ = bf16[384,768]{1,0:T(8,128)(2,1)S(1)} collective-permute-done((bf16[384,768]{1,0:T(8,128)(2,1)}, bf16[384,768]{1,0:T(8,128)(2,1)S(1)}, u32[]{:S(2)}, u32[]{:S(2)}) %collective-permute-start.61) | collective-permute-done | bytes 589856 | tf_op jit(solution)/shard_map/ppermute | solution.py:65
  126.4 13.6 %feed_backward.1 = (bf16[384,768]{1,0:T(8,128)(2,1)}, f32[384,768]{1,0:T(8,128)}, bf16[384,768]{1,0:T(8,128)(2,1)}, bf16[384,1536]{1,0:T(8,128)(2,1)}, bf16[384,...) custom-call(bf16[48,1536]{1,0:T(8,128)(2,1)S(1)} %copy-done.10, ...), custom_call_target="tpu_custom_call" | custom-call | flops 1811939328 | bytes 4718592 | tf_op jit(solution)/shard_map/feed_backward/pallas_call | solution.py:83
  141.7 12.8 %collective-permute-done.62.got_ref = bf16[384,768]{1,0:T(8,128)(2,1)S(1)} collective-permute-done((bf16[384,768]{1,0:T(8,128)(2,1)}, bf16[384,768]{1,0:T(8,128)(2,1)S(1)}, u32[]{:S(2)}, u32[]{:S(2)}) %collective-permute-start.62) | collective-permute-done | bytes 589856 | tf_op jit(solution)/shard_map/ppermute | solution.py:65
  155.6 2.5 norm_one_backward.1
  158.1 6.0 %attention_backward.1 = (bf16[3,384,384]{2,1,0:T(8,128)(2,1)S(1)}, f32[2,384]{1,0:T(2,128)S(1)}) custom-call(bf16[48,384]{1,0:T(8,128)(2,1)S(1)} %bitcast.128, bf16[48,384]{1,0:T(8,128)(2,1)S(1)} %collective-permute-done.30.refs_1_, bf16[48,384]{1,0:T(8,128)(2,1)S(1)} %collective-permute-done.31.refs_2_, ...), custom_call_target="tpu_custom_call" | custom-call | flops 1132462080 | bytes 589824 | tf_op jit(solution)/shard_map/attention_backward/pallas_call | solution.py:83
  167.6 2.7 %shrink_grad.1 = (bf16[8,48,1536]{2,1,0:T(8,128)(2,1)S(1)}, bf16[8,48,1536]{2,1,0:T(8,128)(2,1)}) custom-call(bf16[384,768]{1,0:T(8,128)(2,1)S(1)} %copy-done.53, bf16[384,1536]{1,0:T(8,128)(2,1)S(1)} %copy-done.57), custom_call_target="tpu_custom_call" | custom-call | flops 905969664 | bytes 2359296 | tf_op jit(solution)/shard_map/shrink_grad/pallas_call | solution.py:83
  171.2 2.7 %expand_grad.1 = (bf16[8,48,1536]{2,1,0:T(8,128)(2,1)S(1)}, bf16[8,48,1536]{2,1,0:T(8,128)(2,1)}) custom-call(bf16[384,768]{1,0:T(8,128)(2,1)S(1)} %copy-done.58, bf16[384,1536]{1,0:T(8,128)(2,1)S(1)} %copy-done.49), custom_call_target="tpu_custom_call" | custom-call | flops 905969664 | bytes 2359296 | tf_op jit(solution)/shard_map/expand_grad/pallas_call | solution.py:83
  191.9 2.5 collective-permute-start.77
  211.2 7.1 %collective-permute-done.84 = bf16[4,48,1536]{2,1,0:T(8,128)(2,1)S(1)} collective-permute-done((bf16[4,48,1536]{2,1,0:T(8,128)(2,1)S(1)}, bf16[4,48,1536]{2,1,0:T(8,128)(2,1)S(1)}, u32[]{:S(2)}, u32[]{:S(2)}) %collective-permute-start.84) | collective-permute-done | bytes 589856 | tf_op jit(solution)/shard_map/ppermute | solution.py:30
  222.1 8.9 %collective-permute-done.79 = bf16[4,48,1536]{2,1,0:T(8,128)(2,1)S(1)} collective-permute-done((bf16[4,48,1536]{2,1,0:T(8,128)(2,1)S(1)}, bf16[4,48,1536]{2,1,0:T(8,128)(2,1)S(1)}, u32[]{:S(2)}, u32[]{:S(2)}) %collective-permute-start.79) | collective-permute-done | bytes 589856 | tf_op jit(solution)/shard_map/ppermute | solution.py:30
  239.5 2.5 collective-permute-start.68
  242.0 10.8 %collective-permute-done.81 = bf16[48,1536]{1,0:T(8,128)(2,1)S(1)} collective-permute-done((bf16[48,1536]{1,0:T(8,128)(2,1)S(1)}, bf16[48,1536]{1,0:T(8,128)(2,1)S(1)}, u32[]{:S(2)}, u32[]{:S(2)}) %collective-permute-start.81) | collective-permute-done | bytes 147488 | tf_op jit(solution)/shard_map/ppermute | solution.py:30
  (347 shorter events, 107.9 us)
Async XLA Ops:
  17.3 17.1 %collective-permute-start.52 = (bf16[3,48,384]{2,1,0:T(8,128)(2,1)}, bf16[3,48,384]{2,1,0:T(8,128)(2,1)S(1)}, u32[]{:S(2)}, u32[]{:S(2)}) collective-permute-start(bf16[3,48,384]{2,1,0:T(8,128)(2,1)} %bitcast.115), channel_id=1, source_target_pairs={{0,16},{2,18},{4,20},{6,22},{8,24},{10,26},{12,28},{14,30},{16,0},... | collective-permute-start | bytes 331784 | tf_op jit(solution)/shard_map/ppermute | solution.py:30
  18.4 16.1 %collective-permute-start.48 = (bf16[3,48,384]{2,1,0:T(8,128)(2,1)}, bf16[3,48,384]{2,1,0:T(8,128)(2,1)S(1)}, u32[]{:S(2)}, u32[]{:S(2)}) collective-permute-start(bf16[3,48,384]{2,1,0:T(8,128)(2,1)} %bitcast.116), channel_id=1, source_target_pairs={{0,8},{2,10},{4,12},{6,14},{8,0},{10,2},{12,4},{14,6},{16,24},{18,... | collective-permute-start | bytes 331784 | tf_op jit(solution)/shard_map/ppermute | solution.py:30
  19.2 17.0 %collective-permute-start.46 = (bf16[3,48,384]{2,1,0:T(8,128)(2,1)}, bf16[3,48,384]{2,1,0:T(8,128)(2,1)S(1)}, u32[]{:S(2)}, u32[]{:S(2)}) collective-permute-start(bf16[3,48,384]{2,1,0:T(8,128)(2,1)} %bitcast.117), channel_id=1, source_target_pairs={{0,4},{2,6},{4,0},{6,2},{8,12},{10,14},{12,8},{14,10},{16,20},{18,... | collective-permute-start | bytes 331784 | tf_op jit(solution)/shard_map/ppermute | solution.py:30
  22.3 15.7 %collective-permute-start.26 = (bf16[48,1536]{1,0:T(8,128)(2,1)}, bf16[48,1536]{1,0:T(8,128)(2,1)S(1)}, u32[]{:S(2)}, u32[]{:S(2)}) collective-permute-start(bf16[48,1536]{1,0:T(8,128)(2,1)} %bitcast.107), channel_id=1, source_target_pairs={{0,24},{2,26},{4,28},{6,30},{8,16},{10,18},{12,20},{14,22},{16,8},... | collective-permute-start | bytes 442376 | tf_op jit(solution)/shard_map/ppermute | solution.py:30
  24.2 16.6 %collective-permute-start.22 = (bf16[48,1536]{1,0:T(8,128)(2,1)}, bf16[48,1536]{1,0:T(8,128)(2,1)S(1)}, u32[]{:S(2)}, u32[]{:S(2)}) collective-permute-start(bf16[48,1536]{1,0:T(8,128)(2,1)} %bitcast.108), channel_id=1, source_target_pairs={{0,16},{2,18},{4,20},{6,22},{8,24},{10,26},{12,28},{14,30},{16,0},... | collective-permute-start | bytes 442376 | tf_op jit(solution)/shard_map/ppermute | solution.py:30
  40.8 14.5 %collective-permute-start.7 = (bf16[48,1536]{1,0:T(8,128)(2,1)}, bf16[48,1536]{1,0:T(8,128)(2,1)S(1)}, u32[]{:S(2)}, u32[]{:S(2)}) collective-permute-start(bf16[48,1536]{1,0:T(8,128)(2,1)} %refs_0_.3), channel_id=1, source_target_pairs={{0,16},{2,18},{4,20},{6,22},{8,24},{10,26},{12,28},{14,30},{16,0},... | collective-permute-start | bytes 442376 | tf_op jit(solution)/shard_map/ppermute | solution.py:30
  63.2 14.8 %collective-permute-start = (bf16[48,1536]{1,0:T(8,128)(2,1)}, bf16[48,1536]{1,0:T(8,128)(2,1)S(1)}, u32[]{:S(2)}, u32[]{:S(2)}) collective-permute-start(bf16[48,1536]{1,0:T(8,128)(2,1)} %refs_0_.3), channel_id=1, source_target_pairs={{0,2},{2,0},{4,6},{6,4},{8,10},{10,8},{12,14},{14,12},{16,18},{18,... | collective-permute-start | bytes 442376 | tf_op jit(solution)/shard_map/ppermute | solution.py:30
  63.7 14.7 %collective-permute-start.28 = (bf16[48,1536]{1,0:T(8,128)(2,1)S(1)}, bf16[48,1536]{1,0:T(8,128)(2,1)S(1)}, u32[]{:S(2)}, u32[]{:S(2)}) collective-permute-start(bf16[48,1536]{1,0:T(8,128)(2,1)S(1)} %collective-permute-done.26.refs_28_), channel_id=1, source_target_pairs={{0,4},{2,6},{4,0},{6,2},{8,12},{10,14},{12,8},{14,10},{16,20},{18,... | collective-permute-start | bytes 442376 | tf_op jit(solution)/shard_map/ppermute | solution.py:30
  64.0 14.5 %collective-permute-start.27 = (bf16[48,1536]{1,0:T(8,128)(2,1)S(1)}, bf16[48,1536]{1,0:T(8,128)(2,1)S(1)}, u32[]{:S(2)}, u32[]{:S(2)}) collective-permute-start(bf16[48,1536]{1,0:T(8,128)(2,1)S(1)} %collective-permute-done.26.refs_28_), channel_id=1, source_target_pairs={{0,2},{2,0},{4,6},{6,4},{8,10},{10,8},{12,14},{14,12},{16,18},{18,... | collective-permute-start | bytes 442376 | tf_op jit(solution)/shard_map/ppermute | solution.py:30
  64.1 14.9 %collective-permute-start.24 = (bf16[48,1536]{1,0:T(8,128)(2,1)S(1)}, bf16[48,1536]{1,0:T(8,128)(2,1)S(1)}, u32[]{:S(2)}, u32[]{:S(2)}) collective-permute-start(bf16[48,1536]{1,0:T(8,128)(2,1)S(1)} %collective-permute-done.22.refs_24_), channel_id=1, source_target_pairs={{0,4},{2,6},{4,0},{6,2},{8,12},{10,14},{12,8},{14,10},{16,20},{18,... | collective-permute-start | bytes 442376 | tf_op jit(solution)/shard_map/ppermute | solution.py:30
  65.8 16.3 %collective-permute-start.23 = (bf16[48,1536]{1,0:T(8,128)(2,1)S(1)}, bf16[48,1536]{1,0:T(8,128)(2,1)S(1)}, u32[]{:S(2)}, u32[]{:S(2)}) collective-permute-start(bf16[48,1536]{1,0:T(8,128)(2,1)S(1)} %collective-permute-done.22.refs_24_), channel_id=1, source_target_pairs={{0,2},{2,0},{4,6},{6,4},{8,10},{10,8},{12,14},{14,12},{16,18},{18,... | collective-permute-start | bytes 442376 | tf_op jit(solution)/shard_map/ppermute | solution.py:30
  82.1 15.1 %collective-permute-start.60 = (bf16[384,768]{1,0:T(8,128)(2,1)S(1)}, bf16[384,768]{1,0:T(8,128)(2,1)S(1)}, u32[]{:S(2)}, u32[]{:S(2)}) collective-permute-start(bf16[384,768]{1,0:T(8,128)(2,1)S(1)} %attention_output.1.refs_33_), channel_id=1, source_target_pairs={{0,1},{1,0},{2,3},{3,2},{4,5},{5,4},{6,7},{7,6},{8,9},{9,8},{10,11... | collective-permute-start | bytes 1769480 | tf_op jit(solution)/shard_map/ppermute | solution.py:65
  110.3 15.3 %collective-permute-start.61 = (bf16[384,768]{1,0:T(8,128)(2,1)}, bf16[384,768]{1,0:T(8,128)(2,1)S(1)}, u32[]{:S(2)}, u32[]{:S(2)}) collective-permute-start(bf16[384,768]{1,0:T(8,128)(2,1)} %get-tuple-element.42.refs_33_), channel_id=1, source_target_pairs={{0,1},{1,0},{2,3},{3,2},{4,5},{5,4},{6,7},{7,6},{8,9},{9,8},{10,11... | collective-permute-start | bytes 1769480 | tf_op jit(solution)/shard_map/ppermute | solution.py:65
  140.1 14.5 %collective-permute-start.62 = (bf16[384,768]{1,0:T(8,128)(2,1)}, bf16[384,768]{1,0:T(8,128)(2,1)S(1)}, u32[]{:S(2)}, u32[]{:S(2)}) collective-permute-start(bf16[384,768]{1,0:T(8,128)(2,1)} %get-tuple-element.45.own_ref), channel_id=1, source_target_pairs={{0,1},{1,0},{2,3},{3,2},{4,5},{5,4},{6,7},{7,6},{8,9},{9,8},{10,11... | collective-permute-start | bytes 1769480 | tf_op jit(solution)/shard_map/ppermute | solution.py:65
  170.2 30.1 %collective-permute-start.83 = (bf16[8,48,1536]{2,1,0:T(8,128)(2,1)}, bf16[8,48,1536]{2,1,0:T(8,128)(2,1)}, u32[]{:S(2)}, u32[]{:S(2)}) collective-permute-start(bf16[8,48,1536]{2,1,0:T(8,128)(2,1)} %get-tuple-element.68), channel_id=1, source_target_pairs={{0,2},{2,0},{4,6},{6,4},{8,10},{10,8},{12,14},{14,12},{16,18},{18,... | collective-permute-start | bytes 3538952 | tf_op jit(solution)/shard_map/ppermute | solution.py:30
  174.9 28.7 %collective-permute-start.78 = (bf16[8,48,1536]{2,1,0:T(8,128)(2,1)}, bf16[8,48,1536]{2,1,0:T(8,128)(2,1)}, u32[]{:S(2)}, u32[]{:S(2)}) collective-permute-start(bf16[8,48,1536]{2,1,0:T(8,128)(2,1)} %get-tuple-element.64), channel_id=1, source_target_pairs={{0,2},{2,0},{4,6},{6,4},{8,10},{10,8},{12,14},{14,12},{16,18},{18,... | collective-permute-start | bytes 3538952 | tf_op jit(solution)/shard_map/ppermute | solution.py:30
  202.0 16.3 %collective-permute-start.84 = (bf16[4,48,1536]{2,1,0:T(8,128)(2,1)S(1)}, bf16[4,48,1536]{2,1,0:T(8,128)(2,1)S(1)}, u32[]{:S(2)}, u32[]{:S(2)}) collective-permute-start(bf16[4,48,1536]{2,1,0:T(8,128)(2,1)S(1)} %slice.269), channel_id=1, source_target_pairs={{0,4},{2,6},{4,0},{6,2},{8,12},{10,14},{12,8},{14,10},{16,20},{18,... | collective-permute-start | bytes 1769480 | tf_op jit(solution)/shard_map/ppermute | solution.py:30
  205.3 25.7 %collective-permute-start.79 = (bf16[4,48,1536]{2,1,0:T(8,128)(2,1)S(1)}, bf16[4,48,1536]{2,1,0:T(8,128)(2,1)S(1)}, u32[]{:S(2)}, u32[]{:S(2)}) collective-permute-start(bf16[4,48,1536]{2,1,0:T(8,128)(2,1)S(1)} %slice.270), channel_id=1, source_target_pairs={{0,4},{2,6},{4,0},{6,2},{8,12},{10,14},{12,8},{14,10},{16,20},{18,... | collective-permute-start | bytes 1769480 | tf_op jit(solution)/shard_map/ppermute | solution.py:30
  209.5 28.4 %collective-permute-start.65 = (bf16[4,3,48,384]{3,2,1,0:T(8,128)(2,1)S(1)}, bf16[4,3,48,384]{3,2,1,0:T(8,128)(2,1)S(1)}, u32[]{:S(2)}, u32[]{:S(2)}) collective-permute-start(bf16[4,3,48,384]{3,2,1,0:T(8,128)(2,1)S(1)} %slice.271), channel_id=1, source_target_pairs={{0,4},{2,6},{4,0},{6,2},{8,12},{10,14},{12,8},{14,10},{16,20},{18,... | collective-permute-start | bytes 1327112 | tf_op jit(solution)/shard_map/ppermute | solution.py:30
  218.9 14.0 %collective-permute-start.87 = (bf16[48,1536]{1,0:T(8,128)(2,1)S(1)}, bf16[48,1536]{1,0:T(8,128)(2,1)S(1)}, u32[]{:S(2)}, u32[]{:S(2)}) collective-permute-start(bf16[48,1536]{1,0:T(8,128)(2,1)S(1)} %get-tuple-element.78), channel_id=1, source_target_pairs={{0,24},{2,26},{4,28},{6,30},{8,16},{10,18},{12,20},{14,22},{16,8},... | collective-permute-start | bytes 442376 | tf_op jit(solution)/shard_map/ppermute | solution.py:30
  220.3 14.6 %collective-permute-start.86 = (bf16[48,1536]{1,0:T(8,128)(2,1)S(1)}, bf16[48,1536]{1,0:T(8,128)(2,1)S(1)}, u32[]{:S(2)}, u32[]{:S(2)}) collective-permute-start(bf16[48,1536]{1,0:T(8,128)(2,1)S(1)} %get-tuple-element.79), channel_id=1, source_target_pairs={{0,16},{2,18},{4,20},{6,22},{8,24},{10,26},{12,28},{14,30},{16,0},... | collective-permute-start | bytes 442376 | tf_op jit(solution)/shard_map/ppermute | solution.py:30
  232.9 19.8 %collective-permute-start.81 = (bf16[48,1536]{1,0:T(8,128)(2,1)S(1)}, bf16[48,1536]{1,0:T(8,128)(2,1)S(1)}, u32[]{:S(2)}, u32[]{:S(2)}) collective-permute-start(bf16[48,1536]{1,0:T(8,128)(2,1)S(1)} %get-tuple-element.82), channel_id=1, source_target_pairs={{0,16},{2,18},{4,20},{6,22},{8,24},{10,26},{12,28},{14,30},{16,0},... | collective-permute-start | bytes 442376 | tf_op jit(solution)/shard_map/ppermute | solution.py:30
  238.1 15.4 %collective-permute-start.66 = (bf16[3,48,384]{2,1,0:T(8,128)(2,1)S(1)}, bf16[3,48,384]{2,1,0:T(8,128)(2,1)S(1)}, u32[]{:S(2)}, u32[]{:S(2)}) collective-permute-start(bf16[3,48,384]{2,1,0:T(8,128)(2,1)S(1)} %get-tuple-element.83), channel_id=1, source_target_pairs={{0,8},{2,10},{4,12},{6,14},{8,0},{10,2},{12,4},{14,6},{16,24},{18,... | collective-permute-start | bytes 331784 | tf_op jit(solution)/shard_map/ppermute | solution.py:30
  239.5 14.0 %collective-permute-start.68 = (bf16[3,48,384]{2,1,0:T(8,128)(2,1)S(1)}, bf16[3,48,384]{2,1,0:T(8,128)(2,1)S(1)}, u32[]{:S(2)}, u32[]{:S(2)}) collective-permute-start(bf16[3,48,384]{2,1,0:T(8,128)(2,1)S(1)} %get-tuple-element.84), channel_id=1, source_target_pairs={{0,24},{2,26},{4,28},{6,30},{8,16},{10,18},{12,20},{14,22},{16,8},... | collective-permute-start | bytes 331784 | tf_op jit(solution)/shard_map/ppermute | solution.py:30
  (134 other events, 1303.1 us)

commit v2 on v1

v2 whole, which is shorter than its diff:
```python
import functools

import jax
import jax.numpy as jnp
from jax import lax
from jax.experimental import pallas as pl
from jax.experimental.pallas import tpu as pltpu
from jax.sharding import PartitionSpec as P

HEAD = 64
CLUSTER = 128
PAIR = 128
NORM_EPS = 1e-05
EXCLUDED = -1e30
VMEM_BYTES = 24 * 1024 * 1024

F32 = jnp.float32
BF16 = jnp.bfloat16

NN = (((1,), (0,)), ((), ()))
NT = (((1,), (1,)), ((), ()))
TN = (((0,), (0,)), ((), ()))


def dot(a, b, dims=NN):
    return lax.dot_general(a, b, dims, preferred_element_type=F32)


def swap(array, axis, offset, size):
    return lax.ppermute(array, axis, [(i, i ^ offset) for i in range(size)])


def after(array, *earlier):
    return lax.optimization_barrier((array, *earlier))[0]


def far_steps(dp):
    steps, step = [], dp // 2
    while step >= 4:
        steps.append(step)
        step //= 2
    return steps


def gather_far(shard, dp, early, late):
    pieces = {0: after(shard, *early) if early else shard}
    for step in far_steps(dp):
        for offset in list(pieces):
            held = after(pieces[offset], *late) if offset and late else pieces[offset]
            pieces[offset ^ step] = swap(held, "dp", step, dp)
    return pieces


def gather_near(pieces, dp, gate):
    pieces = dict(pieces)
    for offset in list(pieces):
        if offset ^ 2 not in pieces:
            held = after(pieces[offset], *gate) if gate else pieces[offset]
            pieces[offset ^ 2] = swap(held, "dp", 2, dp)
    for offset in list(pieces):
        pieces[offset ^ 1] = swap(pieces[offset], "dp", 1, dp)
    return [pieces[o] for o in range(dp)]


def block_orders(dp, steps):
    offsets = [0]
    for step in reversed(steps[1:]):
        offsets = offsets + [o ^ step for o in offsets]
    return offsets, [o ^ steps[0] for o in offsets]


def halve_kernel(*refs):
    (keep_ref, got_ref), outs = refs[:2], refs[2:]
    total = keep_ref[...].astype(F32) + got_ref[...].astype(F32)
    if len(outs) == 1:
        outs[0][...] = total[0]
    else:
        half = total.shape[0] // 2
        outs[0][...] = total[:half]
        outs[1][...] = total[half:].astype(BF16)


def scatter_sum(keep, send, dp, steps, name):
    sends = [send]
    for i, step in enumerate(steps):
        got = swap(send, "dp", step, dp)
        shape = keep.shape[1:]
        half = keep.shape[0] // 2
        last = half == 0
        outs = [(shape, F32)] if last else [((half, *shape), F32), ((half, *shape), BF16)]
        result = call(halve_kernel, outs, [keep, got], f"{name}_sum_{step}")
        if last:
            return result[0], sends
        keep, send = result
        sends.append(send)


def sum_all(vector, dp):
    offset = 1
    while offset < dp:
        vector = vector + swap(vector, "dp", offset, dp)
        offset *= 2
    return vector


def other_half(array):
    return lax.ppermute(array, "tensor", [(0, 1), (1, 0)])


def any_spec():
    return pl.BlockSpec(memory_space=pl.ANY)


def vmem_spec():
    return pl.BlockSpec(memory_space=pltpu.VMEM)


def smem_spec():
    return pl.BlockSpec(memory_space=pltpu.SMEM)


def call(body, outs, ins, name, scratch=(), in_specs=None, us=2):
    if in_specs is None:
        in_specs = [vmem_spec()] * len(ins)
    return pl.pallas_call(
        body,
        out_shape=tuple(jax.ShapeDtypeStruct(s, d) for s, d in outs),
        in_specs=in_specs,
        out_specs=tuple(vmem_spec() for _ in outs),
        scratch_shapes=list(scratch),
        compiler_params=pltpu.CompilerParams(vmem_limit_bytes=VMEM_BYTES),
        cost_estimate=pl.CostEstimate(flops=1000, bytes_accessed=us * 3_000_000, transcendentals=0),
        name=name,
    )(*ins)


def fetch(pieces, whole, sems):
    count = len(pieces)
    copies = []
    me = lax.axis_index("dp") if count > 1 else 0
    for o, piece in enumerate(pieces):
        rows = piece.shape[-2]
        start = pl.multiple_of((me ^ o) * rows, 16) if count > 1 else 0
        if len(piece.shape) == 3:
            target = whole.at[:, pl.ds(start, rows), :]
        else:
            target = whole.at[pl.ds(start, rows), :]
        copy = pltpu.make_async_copy(piece, target, sems.at[o])
        copy.start()
        copies.append(copy)
    return copies


def arrive(copies):
    for copy in copies:
        copy.wait()


def norm_rows(v):
    center = jnp.mean(v, axis=-1, keepdims=True)
    offset = v - center
    spread = jnp.mean(offset * offset, axis=-1, keepdims=True)
    scale = lax.rsqrt(spread + NORM_EPS)
    return offset * scale, scale


def norm_back(e, n, scale, gain):
    ea = e * gain
    return scale * (
        ea
        - jnp.mean(ea, axis=-1, keepdims=True)
        - n * jnp.mean(ea * n, axis=-1, keepdims=True)
    )


def admitted_kernel(heads, docs, lengths_ref, perm_ref, bias_ref):
    rows = bias_ref.shape[1]
    spot = lax.broadcasted_iota(jnp.int32, (rows, PAIR), 0)
    lane = lax.broadcasted_iota(jnp.int32, (rows, PAIR), 1)
    doc = jnp.zeros((rows, PAIR), jnp.int32)
    bound = jnp.int32(0)
    for k in range(docs):
        bound = bound + lengths_ref[0, k]
        doc = doc + (spot >= bound).astype(jnp.int32)
    doc_hot = (lane == doc + PAIR // 2).astype(F32)
    cluster_hot = (lane == spot // CLUSTER).astype(BF16)
    place = lax.broadcasted_iota(jnp.int32, (rows, rows), 0)
    for h in range(heads):
        here = (place == perm_ref[h : h + 1, :]).astype(BF16)
        key = (dot(here, cluster_hot) + doc_hot).astype(BF16)
        same = dot(key, key, NT)
        bias_ref[h] = jnp.where(same > 1.5, 0.0, EXCLUDED).astype(BF16)


def attention_kernel(count, heads, scale, *refs):
    pieces, refs = refs[:count], refs[count:]
    tokens_ref, bias_ref, admit_ref, qkv_ref, prob_ref, attended_ref, out_ref, whole, sems = refs
    arrive(fetch(pieces, whole, sems))
    tokens = tokens_ref[...]
    for s in range(3):
        part = dot(tokens, whole[s])
        if s == 0:
            part = part + bias_ref[0:1, :]
        if s == 2:
            part = part + bias_ref[1:2, :]
        qkv_ref[s] = part.astype(BF16)
    lane = lax.broadcasted_iota(jnp.int32, (tokens.shape[0], PAIR), 1)
    for pair in range(heads // 2):
        columns = slice(pair * PAIR, (pair + 1) * PAIR)
        q = qkv_ref[0, :, columns]
        k = qkv_ref[1, :, columns]
        v = qkv_ref[2, :, columns]
        mixed = []
        for side in range(2):
            mine = (lane < HEAD) if side == 0 else (lane >= HEAD)
            scores = dot(jnp.where(mine, q, jnp.zeros_like(q)), k, NT) * scale
            scores = scores + admit_ref[2 * pair + side].astype(F32)
            top = jnp.max(scores, axis=-1, keepdims=True)
            terms = jnp.exp(scores - top)
            total = jnp.sum(terms, axis=-1, keepdims=True)
            prob = (terms * (1.0 / total)).astype(BF16)
            prob_ref[2 * pair + side] = prob
            mixed.append(dot(prob, v))
        attended_ref[:, columns] = jnp.where(lane < HEAD, mixed[0], mixed[1]).astype(BF16)
    out_ref[...] = dot(attended_ref[...], whole[3], NT).astype(BF16)


def expand_kernel(count, *refs):
    pieces, refs = refs[:count], refs[count:]
    (tokens_ref, own_ref, got_ref, out_bias_ref, gain_ref, shift_ref, bias_ref,
     n_ref, scale_ref, low_ref, active_ref, slope_ref, whole, sems) = refs
    copies = fetch(pieces, whole, sems)
    attention = own_ref[...].astype(F32) + got_ref[...].astype(F32) + out_bias_ref[0:1, :]
    n, scale = norm_rows(tokens_ref[...].astype(F32) + attention)
    n_ref[...] = n
    scale_ref[...] = jnp.broadcast_to(scale, scale_ref.shape)
    low_ref[...] = (n * gain_ref[0:1, :] + shift_ref[0:1, :]).astype(BF16)
    arrive(copies)
    units = whole.shape[1]
    step = 256
    for start in range(0, units, step):
        part = slice(start, start + step)
        pre = dot(low_ref[...], whole[:, part]) + bias_ref[:, part]
        half = 0.5 * (1.0 + lax.erf(pre * (2.0**-0.5)))
        active_ref[:, part] = (pre * half).astype(BF16)
        bell = jnp.exp(-0.5 * pre * pre) * 0.3989422804014327
        slope_ref[:, part] = (half + pre * bell).astype(BF16)


def shrink_kernel(count, *refs):
    pieces, refs = refs[:count], refs[count:]
    active_ref, out_ref, whole, sems = refs
    arrive(fetch(pieces, whole, sems))
    out_ref[...] = dot(active_ref[...], whole[...], NT).astype(BF16)


def feed_back_kernel(
    expand_all, shrink_all, n_ref, own_ref, got_ref, out_bias_ref, gain_ref, shift_ref, seed_ref,
    masked_ref, slope_ref, layer_ref, two_ref, low_ref, inner_ref, first_ref, sums_ref, inner_sum_ref,
):
    first = n_ref[...] * gain_ref[0:1, :] + shift_ref[0:1, :]
    feed = own_ref[...].astype(F32) + got_ref[...].astype(F32) + out_bias_ref[1:2, :]
    n, scale = norm_rows(first + feed)
    gain = gain_ref[1:2, :]
    layer_ref[...] = (n * gain + shift_ref[1:2, :]).astype(BF16)
    e = seed_ref[...].astype(F32) * masked_ref[...]
    grad = norm_back(e, n, scale, gain)
    two_ref[...] = grad
    low_ref[...] = grad.astype(BF16)
    sums_ref[0:1, :] = jnp.sum(e * n, axis=0, keepdims=True)
    sums_ref[1:2, :] = jnp.sum(e, axis=0, keepdims=True)
    sums_ref[2:3, :] = jnp.sum(grad, axis=0, keepdims=True)
    units = shrink_all.shape[1]
    step = 256
    for start in range(0, units, step):
        part = slice(start, start + step)
        inner = (dot(low_ref[...], shrink_all[:, part]) * slope_ref[:, part].astype(F32)).astype(BF16)
        inner_ref[:, part] = inner
        inner_sum_ref[:, part] = jnp.sum(inner.astype(F32), axis=0, keepdims=True)
    first_ref[...] = dot(inner_ref[...], expand_all[...], NT).astype(BF16)


def weight_grad_kernel(orders, left_ref, right_ref, keep_ref, send_ref, whole):
    whole[...] = dot(left_ref[...], right_ref[...], TN)
    me = lax.axis_index("dp")
    rows = keep_ref.shape[1]
    for order, target in zip(orders, (keep_ref, send_ref)):
        for k, o in enumerate(order):
            start = pl.multiple_of((me ^ o) * rows, 16)
            target[k] = whole[pl.ds(start, rows), :].astype(BF16)


def norm_one_back_kernel(own_ref, got_ref, two_ref, n_ref, scale_ref, gain_ref, one_ref, low_ref, sums_ref):
    e = own_ref[...].astype(F32) + got_ref[...].astype(F32) + two_ref[...]
    n = n_ref[...]
    grad = norm_back(e, n, scale_ref[:, 0:1], gain_ref[0:1, :])
    one_ref[...] = grad
    low_ref[...] = grad.astype(BF16)
    sums_ref[0:1, :] = jnp.sum(e * n, axis=0, keepdims=True)
    sums_ref[1:2, :] = jnp.sum(e, axis=0, keepdims=True)
    sums_ref[2:3, :] = jnp.sum(grad, axis=0, keepdims=True)


def attention_back_kernel(heads, scale, whole_ref, low_ref, qkv_ref, prob_ref, grads_ref, sums_ref, given):
    given[...] = dot(low_ref[...], whole_ref[3]).astype(BF16)
    lane = lax.broadcasted_iota(jnp.int32, (given.shape[0], PAIR), 1)
    for pair in range(heads // 2):
        columns = slice(pair * PAIR, (pair + 1) * PAIR)
        q = qkv_ref[0, :, columns]
        k = qkv_ref[1, :, columns]
        v = qkv_ref[2, :, columns]
        d = given[:, columns]
        parts = []
        for side in range(2):
            mine = (lane < HEAD) if side == 0 else (lane >= HEAD)
            prob = prob_ref[2 * pair + side]
            d_prob = dot(jnp.where(mine, d, jnp.zeros_like(d)), v, NT)
            wide = prob.astype(F32)
            center = jnp.sum(d_prob * wide, axis=-1, keepdims=True)
            score = (wide * (d_prob - center)).astype(BF16)
            parts.append((dot(score, k), dot(score, q, TN), dot(prob, d, TN)))
        for s in range(3):
            both = jnp.where(lane < HEAD, parts[0][s], parts[1][s])
            if s < 2:
                both = both * scale
            both = both.astype(BF16)
            grads_ref[s, :, columns] = both
            if s != 1:
                sums_ref[s // 2 : s // 2 + 1, columns] = jnp.sum(both.astype(F32), axis=0, keepdims=True)


def input_grad_kernel(whole_ref, grads_ref, out_ref):
    total = dot(grads_ref[0], whole_ref[0], NT)
    total = total + dot(grads_ref[1], whole_ref[1], NT)
    total = total + dot(grads_ref[2], whole_ref[2], NT)
    out_ref[...] = total.astype(BF16)


def project_grad_kernel(orders, tokens_ref, grads_ref, keep_ref, send_ref, whole):
    me = lax.axis_index("dp")
    rows = keep_ref.shape[2]
    for s in range(3):
        whole[...] = dot(tokens_ref[...], grads_ref[s], TN)
        for order, target in zip(orders, (keep_ref, send_ref)):
            for k, o in enumerate(order):
                start = pl.multiple_of((me ^ o) * rows, 16)
                target[k, s] = whole[pl.ds(start, rows), :].astype(BF16)


def plain_grad_kernel(left_ref, right_ref, out_ref):
    out_ref[...] = dot(left_ref[...], right_ref[...], TN)


def shards(
    dp,
    tokens,
    project_weight,
    project_bias,
    output_weight,
    output_bias,
    expand_weight,
    expand_bias,
    shrink_weight,
    norm_gain,
    norm_shift,
    doc_lengths,
    cluster_perm,
    masked,
    out_grad,
):
    rows, width = tokens.shape
    piece_rows, _, columns = project_weight.shape
    units = expand_weight.shape[1]
    heads = columns // HEAD
    scale = HEAD ** (-0.5)
    in_pieces = dp >= 4 and dp & (dp - 1) == 0 and piece_rows % 16 == 0

    mixer_shard = jnp.concatenate([project_weight.transpose(1, 0, 2), output_weight.T[None]])
    shrink_shard = shrink_weight.T
    (admit,) = call(
        functools.partial(admitted_kernel, heads, doc_lengths.shape[1]),
        [((heads, rows, rows), BF16)],
        [doc_lengths, cluster_perm[0]],
        "admitted",
        in_specs=[smem_spec(), vmem_spec()],
    )
    if in_pieces:
        mixer_first = {2: swap(mixer_shard, "dp", 2, dp)}
        mixer_far = gather_far(mixer_shard, dp, (), (mixer_first[2], admit))
        mixer_all = gather_near({**mixer_far, **mixer_first}, dp, ())
        expand_own = after(expand_weight, mixer_all[10])
        expand_first = {2: swap(after(expand_weight, mixer_all[14]), "dp", 2, dp)}
    else:
        mixer_all = [lax.all_gather(mixer_shard, "dp", axis=1, tiled=True)]
        expand_all = [lax.all_gather(expand_weight, "dp", axis=0, tiled=True)]
        shrink_all = [lax.all_gather(shrink_shard, "dp", axis=0, tiled=True)]
    count = len(mixer_all)

    def whole(*shape):
        return pltpu.VMEM(shape, BF16)

    def sems(*shape):
        return pltpu.SemaphoreType.DMA(shape)

    qkv, prob, attended, attention_own, mixer = call(
        functools.partial(attention_kernel, count, heads, scale),
        [
            ((3, rows, columns), BF16),
            ((heads, rows, rows), BF16),
            ((rows, columns), BF16),
            ((rows, width), BF16),
            ((4, width, columns), BF16),
        ],
        [*mixer_all, tokens, project_bias, admit],
        "attention",
        scratch=[sems(count)],
        in_specs=[any_spec()] * count + [vmem_spec()] * 3,
        us=7,
    )
    attention_got = other_half(attention_own)
    if in_pieces:
        expand_far = gather_far(expand_own, dp, (), (qkv,))
        expand_all = gather_near({**expand_far, **expand_first}, dp, (qkv,))
        ends = (expand_far[max(expand_far)],)
        shrink_far = gather_far(shrink_shard, dp, ends, ())
        shrink_all = gather_near(shrink_far, dp, ends)
    n_one, scale_one, first_low, active_low, slope, expand = call(
        functools.partial(expand_kernel, count),
        [
            ((rows, width), F32),
            ((rows, PAIR), F32),
            ((rows, width), BF16),
            ((rows, units), BF16),
            ((rows, units), BF16),
            ((width, units), BF16),
        ],
        [
            *expand_all, tokens, attention_own, attention_got, output_bias,
            norm_gain, norm_shift, expand_bias[None, :],
        ],
        "expand",
        scratch=[sems(count)],
        in_specs=[any_spec()] * count + [vmem_spec()] * 7,
        us=7,
    )
    feed_own, shrink = call(
        functools.partial(shrink_kernel, count),
        [((rows, width), BF16), ((width, units), BF16)],
        [*shrink_all, active_low],
        "shrink",
        scratch=[sems(count)],
        in_specs=[any_spec()] * count + [vmem_spec()],
    )
    feed_got = other_half(feed_own)
    layer_out, residual_two, feed_low, inner_low, first_own, sums_two, inner_sum = call(
        feed_back_kernel,
        [
            ((rows, width), BF16),
            ((rows, width), F32),
            ((rows, width), BF16),
            ((rows, units), BF16),
            ((rows, width), BF16),
            ((3, width), F32),
            ((1, units), F32),
        ],
        [
            expand, shrink, n_one, feed_own, feed_got, output_bias,
            norm_gain, norm_shift, out_grad, masked.astype(F32)[:, None], slope,
        ],
        "feed_backward",
        us=9,
    )
    first_got = other_half(first_own)

    far = far_steps(dp)[::-1]

    def weight_grad(left, right, name, steps):
        wide = right.shape[1]
        if in_pieces:
            keep, send = call(
                functools.partial(weight_grad_kernel, block_orders(dp, steps)),
                [((dp // 2, piece_rows, wide), BF16)] * 2,
                [left, right],
                name,
                scratch=[pltpu.VMEM((width, wide), F32)],
            )
            total, sends = scatter_sum(keep, send, dp, steps, name)
            return sends, total
        (grad,) = call(plain_grad_kernel, [((width, wide), F32)], [left, right], name)
        return [grad] * 4, lax.psum_scatter(grad, "dp", scatter_dimension=0, tiled=True)

    shrink_sends, shrink_part = weight_grad(feed_low, active_low, "shrink_grad", [1, 2, *far])
    expand_sends, expand_part = weight_grad(
        first_low, after(inner_low, shrink_sends[0]), "expand_grad", [1, 2, *far]
    )
    residual_one, attention_low, sums_one = call(
        norm_one_back_kernel,
        [((rows, width), F32), ((rows, width), BF16), ((3, width), F32)],
        [first_own, first_got, residual_two, n_one, scale_one, after(norm_gain, shrink_sends[1], expand_sends[1])],
        "norm_one_backward",
    )
    output_sends, output_part = weight_grad(attention_low, attended, "output_grad", [1, 2, *far])
    project_low, project_sums = call(
        functools.partial(attention_back_kernel, heads, scale),
        [((3, rows, columns), BF16), ((2, columns), F32)],
        [mixer, after(attention_low, output_sends[1], shrink_sends[2]), qkv, prob],
        "attention_backward",
        scratch=[whole(rows, columns)],
        us=5,
    )
    (tokens_own,) = call(
        input_grad_kernel,
        [((rows, width), BF16)],
        [mixer, project_low],
        "input_grad",
    )
    tokens_got = other_half(tokens_own)
    if in_pieces:
        steps = [1, 2, *far]
        keep, send = call(
            functools.partial(project_grad_kernel, block_orders(dp, steps)),
            [((dp // 2, 3, piece_rows, columns), BF16)] * 2,
            [tokens, project_low],
            "project_grad",
            scratch=[pltpu.VMEM((width, columns), F32)],
        )
        project_part, _ = scatter_sum(keep, send, dp, steps, "project_grad")
    else:
        project_part = jnp.stack(
            [weight_grad(tokens, project_low[s], "project_grad", [])[1] for s in range(3)]
        )
    tokens_grad = tokens_own.astype(F32) + tokens_got.astype(F32) + residual_one

    pieces = [sums_one, sums_two, inner_sum, project_sums]
    vector = jnp.concatenate([p.reshape(-1, PAIR) for p in pieces])
    vector = sum_all(vector, dp) if in_pieces else lax.psum(vector, "dp")
    ends, parts = 0, []
    for p in pieces:
        step = p.size // PAIR
        parts.append(vector[ends : ends + step].reshape(p.shape))
        ends += step
    one, two, inner_total, project_total = parts
    return (
        layer_out,
        tokens_grad,
        project_part.transpose(1, 0, 2),
        project_total,
        output_part.T,
        jnp.stack([one[2], two[2]]),
        expand_part,
        inner_total[0],
        shrink_part.T,
        jnp.stack([one[0], two[0]]),
        jnp.stack([one[1], two[1]]),
    )


def solution(mesh):
    in_specs = (
        P("dp", None),
        P("dp", None, "tensor"),
        P(None, "tensor"),
        P("tensor", "dp"),
        P(),
        P("dp", "tensor"),
        P("tensor"),
        P("tensor", "dp"),
        P(),
        P(),
        P("dp", None),
        P("dp", "tensor", None),
        P("dp"),
        P("dp", None),
    )
    out_specs = (
        P("dp", None),
        P("dp", None),
        P("dp", None, "tensor"),
        P(None, "tensor"),
        P("tensor", "dp"),
        P(),
        P("dp", "tensor"),
        P("tensor"),
        P("tensor", "dp"),
        P(),
        P(),
    )
    body = functools.partial(shards, mesh.shape["dp"])
    return jax.shard_map(body, mesh=mesh, in_specs=in_specs, out_specs=out_specs, check_vma=False)
```

time: 257 us -> 201 us (0.78)
  starting transfers between devices: 72.8 us -> 49.8 us
  waiting for transfers between devices: 103 us -> 81.3 us
  Pallas kernels: 55.3 us -> 43.3 us
  local copies, waits for them, and re-layouts: 13.3 us -> 17.3 us
  other arithmetic: 9.9 us -> 7.15 us
    ppermute x84 -> x65, starting transfers between devices: 66.4 us -> 43.6 us  [swap(): return lax.ppermute(array, axis, [(i, i ^ offset) for i in range(size)])]
    ppermute x84 -> x65, waiting for transfers between devices: 75.6 us -> 58.8 us  [swap(): return lax.ppermute(array, axis, [(i, i ^ offset) for i in range(size)])]
    pallas_call x12 -> x28, Pallas kernels: 55.3 us -> 43.3 us  [call(): pl.pallas_call(body, out_shape=tuple((jax.ShapeDtypeStruct(s, d) for s, d...]
    ppermute x4, waiting for transfers between devices: 27.6 us -> 22.5 us  [other_half(): return lax.ppermute(array, 'tensor', [(0, 1), (1, 0)])]
    add x5 -> x0, other arithmetic: 4.17 us -> none  [the longest x4 3.4 us: scatter_sum(): total = keep.astype(F32) + got.astype(F32)]
    unnamed x142 -> x72, local copies, waits for them, and re-layouts: 10.9 us -> 14.1 us
  transfers between devices with their start and end apart: 88 -> 69, of which waited for: 32 -> 25; matrix products, arithmetic and copies ran while one was open for 5% -> 5% of each run, Pallas kernels for 8% -> 16%
where the time goes in v2:
time: 201 us; the launch traced here: 200 us
  waiting for transfers between devices  81.3 us (40%)
  starting transfers between devices  49.8 us (25%)
  Pallas kernels  43.3 us (22%)
  local copies, waits for them, and re-layouts  17.3 us (9%)
  other arithmetic  7.15 us (4%)
    ppermute x65, waiting for transfers between devices, swap(): return lax.ppermute(array, axis, [(i, i ^ offset) for i in range(size)])  58.8 us
    ppermute x65, starting transfers between devices, swap(): return lax.ppermute(array, axis, [(i, i ^ offset) for i in range(size)])  43.6 us
    pallas_call x28, Pallas kernels, call(): pl.pallas_call(body, out_shape=tuple((jax.ShapeDtypeStruct(s, d) for s, d...  43.3 us
    ppermute x4, waiting for transfers between devices, other_half(): return lax.ppermute(array, 'tensor', [(0, 1), (1, 0)])  22.5 us
    unnamed x72, local copies, waits for them, and re-layouts  14.1 us
    ppermute x4, starting transfers between devices, other_half(): return lax.ppermute(array, 'tensor', [(0, 1), (1, 0)])  6.14 us
  transfers between devices with their start and end apart: 69, of which 25 were waited for; matrix products, arithmetic and copies ran while one was open for 5% of the time, Pallas kernels for 16%

profile of v2, /device:TPU:0, one launch (start us, length us, event | category | flops | bytes accessed | tf_op | source)
XLA Modules:
  0.0 200.1 jit_solution(1168899473488425095)
XLA Ops:
  1.7 3.0 %collective-permute-start.3 = (bf16[4,48,384]{2,1,0:T(8,128)(2,1)S(1)}, bf16[4,48,384]{2,1,0:T(8,128)(2,1)S(1)}, u32[]{:S(2)}, u32[]{:S(2)}) collective-permute-start(bf16[4,48,384]{2,1,0:T(8,128)(2,1)S(1)} %pad_maximum_fusion.refs_0_), channel_id=1, source_target_pairs={{0,4},{2,6},{4,0},{6,2},{8,12},{10,14},{12,8},{14,10},{16,20},{18,... | collective-permute-start | bytes 442376 | tf_op jit(solution)/shard_map/ppermute | solution.py:30
  4.7 2.6 %collective-permute-start = (bf16[4,48,384]{2,1,0:T(8,128)(2,1)S(1)}, bf16[4,48,384]{2,1,0:T(8,128)(2,1)S(1)}, u32[]{:S(2)}, u32[]{:S(2)}) collective-permute-start(bf16[4,48,384]{2,1,0:T(8,128)(2,1)S(1)} %pad_maximum_fusion.refs_0_), channel_id=1, source_target_pairs={{0,16},{2,18},{4,20},{6,22},{8,24},{10,26},{12,28},{14,30},{16,0},... | collective-permute-start | bytes 442376 | tf_op jit(solution)/shard_map/ppermute | solution.py:30
  10.2 2.4 %admitted.1.refs_18_ = bf16[6,384,384]{2,1,0:T(8,128)(2,1)S(1)} custom-call(s32[1,4]{1,0:T(1,128)S(1)} %copy-done.27, s32[6,384]{1,0:T(8,128)S(1)} %bitcast.49), custom_call_target="tpu_custom_call" | custom-call | flops 1000 | bytes 6000000 | tf_op jit(solution)/shard_map/admitted/pallas_call | solution.py:125
  21.5 3.2 %collective-permute-done.14.refs_6_ = bf16[4,48,384]{2,1,0:T(8,128)(2,1)S(1)} collective-permute-done((bf16[4,48,384]{2,1,0:T(8,128)(2,1)S(1)}, bf16[4,48,384]{2,1,0:T(8,128)(2,1)S(1)}, u32[]{:S(2)}, u32[]{:S(2)}) %collective-permute-start.14) | collective-permute-done | bytes 147488 | tf_op jit(solution)/shard_map/ppermute | solution.py:30
  26.6 3.4 %collective-permute-start.22 = (bf16[48,1536]{1,0:T(8,128)(2,1)S(1)}, bf16[48,1536]{1,0:T(8,128)(2,1)S(1)}, u32[]{:S(2)}, u32[]{:S(2)}) collective-permute-start(bf16[48,1536]{1,0:T(8,128)(2,1)S(1)} %copy-done.19), channel_id=1, source_target_pairs={{0,16},{2,18},{4,20},{6,22},{8,24},{10,26},{12,28},{14,30},{16,0},... | collective-permute-start | bytes 442376 | tf_op jit(solution)/shard_map/ppermute | solution.py:30
  30.8 5.3 %attention.1 = (bf16[3,384,384]{2,1,0:T(8,128)(2,1)S(1)}, bf16[6,384,384]{2,1,0:T(8,128)(2,1)S(1)}, bf16[384,384]{1,0:T(8,128)(2,1)S(1)}, bf16[384,768]{1,0:T(8,128)(2,1)S(1)}, bf16[4,768,384]{2,1,0:T(8,128)(2,1)S(1)}) custom-call(bf16[4,48,384]{2,1,0:T(8,128)(2,1)S(1)} %pad_maximum_fusion.refs_0_, bf16[4,48,384]{2,1,0:T(8,128)(2,1)S(1)} %collective-permute-done.10.refs_1_, ...), custom_call_target="tpu_custom_call" | custom-call | flops 1000 | bytes 21000000 | tf_op jit(solution)/shard_map/attention/pallas_call | solution.py:125
  53.5 4.1 %collective-permute-done.38.refs_8_ = bf16[48,1536]{1,0:T(8,128)(2,1)S(1)} collective-permute-done((bf16[48,1536]{1,0:T(8,128)(2,1)S(1)}, bf16[48,1536]{1,0:T(8,128)(2,1)S(1)}, u32[]{:S(2)}, u32[]{:S(2)}) %collective-permute-start.38) | collective-permute-done | bytes 147488 | tf_op jit(solution)/shard_map/ppermute | solution.py:30
  60.3 3.2 %collective-permute-done.42.refs_12_ = bf16[48,1536]{1,0:T(8,128)(2,1)S(1)} collective-permute-done((bf16[48,1536]{1,0:T(8,128)(2,1)S(1)}, bf16[48,1536]{1,0:T(8,128)(2,1)S(1)}, u32[]{:S(2)}, u32[]{:S(2)}) %collective-permute-start.42) | collective-permute-done | bytes 147488 | tf_op jit(solution)/shard_map/ppermute | solution.py:30
  66.4 3.6 %collective-permute-done.40.refs_10_ = bf16[48,1536]{1,0:T(8,128)(2,1)S(1)} collective-permute-done((bf16[48,1536]{1,0:T(8,128)(2,1)S(1)}, bf16[48,1536]{1,0:T(8,128)(2,1)S(1)}, u32[]{:S(2)}, u32[]{:S(2)}) %collective-permute-start.40) | collective-permute-done | bytes 147488 | tf_op jit(solution)/shard_map/ppermute | solution.py:30
  70.6 2.6 %collective-permute-done.36.refs_6_ = bf16[48,1536]{1,0:T(8,128)(2,1)S(1)} collective-permute-done((bf16[48,1536]{1,0:T(8,128)(2,1)S(1)}, bf16[48,1536]{1,0:T(8,128)(2,1)S(1)}, u32[]{:S(2)}, u32[]{:S(2)}) %collective-permute-start.36) | collective-permute-done | bytes 147488 | tf_op jit(solution)/shard_map/ppermute | solution.py:30
  73.2 2.8 %collective-permute-done.44.refs_14_ = bf16[48,1536]{1,0:T(8,128)(2,1)S(1)} collective-permute-done((bf16[48,1536]{1,0:T(8,128)(2,1)S(1)}, bf16[48,1536]{1,0:T(8,128)(2,1)S(1)}, u32[]{:S(2)}, u32[]{:S(2)}) %collective-permute-start.44) | collective-permute-done | bytes 147488 | tf_op jit(solution)/shard_map/ppermute | solution.py:30
  76.6 6.1 %expand.1 = (f32[384,768]{1,0:T(8,128)S(1)}, f32[384,128]{1,0:T(8,128)S(1)}, bf16[384,768]{1,0:T(8,128)(2,1)S(1)}, bf16[384,1536]{1,0:T(8,128)(2,1)S(1)}, bf16[3...) custom-call(bf16[48,1536]{1,0:T(8,128)(2,1)S(1)} %copy-done.19, ...), custom_call_target="tpu_custom_call" | custom-call | flops 1000 | bytes 21000000 | tf_op jit(solution)/shard_map/expand/pallas_call | solution.py:125
  82.7 4.7 %shrink.1 = (bf16[384,768]{1,0:T(8,128)(2,1)S(1)}, bf16[768,1536]{1,0:T(8,128)(2,1)S(1)}) custom-call(bf16[48,1536]{1,0:T(8,128)(2,1)S(1)} %bitcast.48, bf16[48,1536]{1,0:T(8,128)(2,1)S(1)} %collective-permute-done.31.refs_1_, bf16[48,1536]{1,0:T(8,128)(2,1)S(1)} %collective-permute-done.32.refs_2_, bf16[48,1536]{1,0:T(8,128)(2,1)S(1)} %collective-permute-done.33.refs_3_, ...), custom_call_target="tpu_custom_call" | custom-call | flops 1000 | bytes 6000000 | tf_op jit(solution)/shard_map/shrink/pallas_call | solution.py:125
  89.1 13.6 %collective-permute-done.46.got_ref = bf16[384,768]{1,0:T(8,128)(2,1)S(1)} collective-permute-done((bf16[384,768]{1,0:T(8,128)(2,1)S(1)}, bf16[384,768]{1,0:T(8,128)(2,1)S(1)}, u32[]{:S(2)}, u32[]{:S(2)}) %collective-permute-start.46) | collective-permute-done | bytes 589856 | tf_op jit(solution)/shard_map/ppermute | solution.py:107
  102.8 3.4 %feed_backward.1 = (bf16[384,768]{1,0:T(8,128)(2,1)}, f32[384,768]{1,0:T(8,128)S(1)}, bf16[384,768]{1,0:T(8,128)(2,1)S(1)}, bf16[384,1536]{1,0:T(8,128)(2,1)S(1)...) custom-call(bf16[768,1536]{1,0:T(8,128)(2,1)S(1)} %get-tuple-element.90.expand_all, ...), custom_call_target="tpu_custom_call" | custom-call | flops 1000 | bytes 27000000 | tf_op jit(solution)/shard_map/feed_backward/pallas_call | solution.py:125
  116.5 8.9 %collective-permute-done.47.got_ref = bf16[384,768]{1,0:T(8,128)(2,1)S(1)} collective-permute-done((bf16[384,768]{1,0:T(8,128)(2,1)S(1)}, bf16[384,768]{1,0:T(8,128)(2,1)S(1)}, u32[]{:S(2)}, u32[]{:S(2)}) %collective-permute-start.47) | collective-permute-done | bytes 589856 | tf_op jit(solution)/shard_map/ppermute | solution.py:107
  139.7 3.5 %attention_backward.1 = (bf16[3,384,384]{2,1,0:T(8,128)(2,1)S(1)}, f32[2,384]{1,0:T(2,128)S(1)}) custom-call(bf16[4,768,384]{2,1,0:T(8,128)(2,1)S(1)} %get-tuple-element.102.whole_ref, bf16[384,768]{1,0:T(8,128)(2,1)S(1)} %get-tuple-element.124.left_ref.low_ref, bf16[3,384,384]{2,1,0:T(8,128)(2,1)S(1)} %copy-done.13, bf16[6,384,384]{2,1,0:T(8,128)(2,1)S(1)} %copy-done.5), custom_call_target="tpu_custom_call" | custom-call | flops 1000 | bytes 15000000 | tf_op jit(solution)/shard_map/attention_backward/pallas_call | solution.py:125
  145.3 2.6 %collective-permute-done.61.refs_1_ = bf16[4,48,384]{2,1,0:T(8,128)(2,1)} collective-permute-done((bf16[4,48,384]{2,1,0:T(8,128)(2,1)}, bf16[4,48,384]{2,1,0:T(8,128)(2,1)}, u32[]{:S(2)}, u32[]{:S(2)}) %collective-permute-start.61) | collective-permute-done | bytes 147488 | tf_op jit(solution)/shard_map/ppermute | solution.py:30
  153.6 3.1 %collective-permute-done.58 = f32[54,128]{1,0:T(8,128)S(1)} collective-permute-done((f32[54,128]{1,0:T(8,128)S(1)}, f32[54,128]{1,0:T(8,128)S(1)}, u32[]{:S(2)}, u32[]{:S(2)}) %collective-permute-start.58) | collective-permute-done | bytes 27680 | tf_op jit(solution)/shard_map/ppermute | solution.py:30
  161.5 2.3 %collective-permute-done.63.refs_1_ = bf16[1,48,384]{2,1,0:T(8,128)(2,1)S(1)} collective-permute-done((bf16[1,48,384]{2,1,0:T(8,128)(2,1)S(1)}, bf16[1,48,384]{2,1,0:T(8,128)(2,1)S(1)}, u32[]{:S(2)}, u32[]{:S(2)}) %collective-permute-start.63) | collective-permute-done | bytes 36896 | tf_op jit(solution)/shard_map/ppermute | solution.py:30
  172.7 5.8 %collective-permute-done.65.refs_1_ = bf16[2,48,1536]{2,1,0:T(8,128)(2,1)S(1)} collective-permute-done((bf16[2,48,1536]{2,1,0:T(8,128)(2,1)S(1)}, bf16[2,48,1536]{2,1,0:T(8,128)(2,1)S(1)}, u32[]{:S(2)}, u32[]{:S(2)}) %collective-permute-start.65) | collective-permute-done | bytes 294944 | tf_op jit(solution)/shard_map/ppermute | solution.py:30
  180.6 2.2 %collective-permute-start.68 = (bf16[1,48,1536]{2,1,0:T(8,128)(2,1)}, bf16[1,48,1536]{2,1,0:T(8,128)(2,1)S(1)}, u32[]{:S(2)}, u32[]{:S(2)}) collective-permute-start(bf16[1,48,1536]{2,1,0:T(8,128)(2,1)} %get-tuple-element.152), channel_id=1, source_target_pairs={{0,16},{2,18},{4,20},{6,22},{8,24},{10,26},{12,28},{14,30},{16,0},... | collective-permute-start | bytes 442376 | tf_op jit(solution)/shard_map/ppermute | solution.py:30
  185.0 5.2 %collective-permute-done.66.refs_1_ = bf16[1,48,1536]{2,1,0:T(8,128)(2,1)S(1)} collective-permute-done((bf16[1,48,1536]{2,1,0:T(8,128)(2,1)}, bf16[1,48,1536]{2,1,0:T(8,128)(2,1)S(1)}, u32[]{:S(2)}, u32[]{:S(2)}) %collective-permute-start.66) | collective-permute-done | bytes 147488 | tf_op jit(solution)/shard_map/ppermute | solution.py:30
  195.5 3.9 %collective-permute-done.56.refs_1_ = bf16[1,3,48,384]{3,2,1,0:T(8,128)(2,1)S(1)} collective-permute-done((bf16[1,3,48,384]{3,2,1,0:T(8,128)(2,1)S(1)}, bf16[1,3,48,384]{3,2,1,0:T(8,128)(2,1)S(1)}, u32[]{:S(2)}, u32[]{:S(2)}) %collective-permute-start.56) | collective-permute-done | bytes 110624 | tf_op jit(solution)/shard_map/ppermute | solution.py:30
  (236 shorter events, 97.3 us)
Async XLA Ops:
  1.7 11.0 %collective-permute-start.3 = (bf16[4,48,384]{2,1,0:T(8,128)(2,1)S(1)}, bf16[4,48,384]{2,1,0:T(8,128)(2,1)S(1)}, u32[]{:S(2)}, u32[]{:S(2)}) collective-permute-start(bf16[4,48,384]{2,1,0:T(8,128)(2,1)S(1)} %pad_maximum_fusion.refs_0_), channel_id=1, source_target_pairs={{0,4},{2,6},{4,0},{6,2},{8,12},{10,14},{12,8},{14,10},{16,20},{18,... | collective-permute-start | bytes 442376 | tf_op jit(solution)/shard_map/ppermute | solution.py:30
  4.7 9.5 %collective-permute-start = (bf16[4,48,384]{2,1,0:T(8,128)(2,1)S(1)}, bf16[4,48,384]{2,1,0:T(8,128)(2,1)S(1)}, u32[]{:S(2)}, u32[]{:S(2)}) collective-permute-start(bf16[4,48,384]{2,1,0:T(8,128)(2,1)S(1)} %pad_maximum_fusion.refs_0_), channel_id=1, source_target_pairs={{0,16},{2,18},{4,20},{6,22},{8,24},{10,26},{12,28},{14,30},{16,0},... | collective-permute-start | bytes 442376 | tf_op jit(solution)/shard_map/ppermute | solution.py:30
  26.6 11.7 %collective-permute-start.22 = (bf16[48,1536]{1,0:T(8,128)(2,1)S(1)}, bf16[48,1536]{1,0:T(8,128)(2,1)S(1)}, u32[]{:S(2)}, u32[]{:S(2)}) collective-permute-start(bf16[48,1536]{1,0:T(8,128)(2,1)S(1)} %copy-done.19), channel_id=1, source_target_pairs={{0,16},{2,18},{4,20},{6,22},{8,24},{10,26},{12,28},{14,30},{16,0},... | collective-permute-start | bytes 442376 | tf_op jit(solution)/shard_map/ppermute | solution.py:30
  30.0 10.0 %collective-permute-start.8 = (bf16[48,1536]{1,0:T(8,128)(2,1)S(1)}, bf16[48,1536]{1,0:T(8,128)(2,1)S(1)}, u32[]{:S(2)}, u32[]{:S(2)}) collective-permute-start(bf16[48,1536]{1,0:T(8,128)(2,1)S(1)} %copy-done.19), channel_id=1, source_target_pairs={{0,8},{2,10},{4,12},{6,14},{8,0},{10,2},{12,4},{14,6},{16,24},{18,... | collective-permute-start | bytes 442376 | tf_op jit(solution)/shard_map/ppermute | solution.py:30
  30.3 11.5 %collective-permute-start.6 = (bf16[48,1536]{1,0:T(8,128)(2,1)S(1)}, bf16[48,1536]{1,0:T(8,128)(2,1)S(1)}, u32[]{:S(2)}, u32[]{:S(2)}) collective-permute-start(bf16[48,1536]{1,0:T(8,128)(2,1)S(1)} %copy-done.19), channel_id=1, source_target_pairs={{0,4},{2,6},{4,0},{6,2},{8,12},{10,14},{12,8},{14,10},{16,20},{18,... | collective-permute-start | bytes 442376 | tf_op jit(solution)/shard_map/ppermute | solution.py:30
  47.8 9.9 %collective-permute-start.38 = (bf16[48,1536]{1,0:T(8,128)(2,1)S(1)}, bf16[48,1536]{1,0:T(8,128)(2,1)S(1)}, u32[]{:S(2)}, u32[]{:S(2)}) collective-permute-start(bf16[48,1536]{1,0:T(8,128)(2,1)S(1)} %bitcast.44), channel_id=1, source_target_pairs={{0,16},{2,18},{4,20},{6,22},{8,24},{10,26},{12,28},{14,30},{16,0},... | collective-permute-start | bytes 442376 | tf_op jit(solution)/shard_map/ppermute | solution.py:30
  47.9 28.1 %collective-permute-start.30 = (bf16[384,768]{1,0:T(8,128)(2,1)S(1)}, bf16[384,768]{1,0:T(8,128)(2,1)S(1)}, u32[]{:S(2)}, u32[]{:S(2)}) collective-permute-start(bf16[384,768]{1,0:T(8,128)(2,1)S(1)} %get-tuple-element.89.refs_17_), channel_id=1, source_target_pairs={{0,1},{1,0},{2,3},{3,2},{4,5},{5,4},{6,7},{7,6},{8,9},{9,8},{10,11... | collective-permute-start | bytes 1769480 | tf_op jit(solution)/shard_map/ppermute | solution.py:107
  65.7 10.3 %collective-permute-start.44 = (bf16[48,1536]{1,0:T(8,128)(2,1)S(1)}, bf16[48,1536]{1,0:T(8,128)(2,1)S(1)}, u32[]{:S(2)}, u32[]{:S(2)}) collective-permute-start(bf16[48,1536]{1,0:T(8,128)(2,1)S(1)} %collective-permute-done.42.refs_12_), channel_id=1, source_target_pairs={{0,4},{2,6},{4,0},{6,2},{8,12},{10,14},{12,8},{14,10},{16,20},{18,... | collective-permute-start | bytes 442376 | tf_op jit(solution)/shard_map/ppermute | solution.py:30
  70.1 12.6 %collective-permute-start.35 = (bf16[48,1536]{1,0:T(8,128)(2,1)S(1)}, bf16[48,1536]{1,0:T(8,128)(2,1)S(1)}, u32[]{:S(2)}, u32[]{:S(2)}) collective-permute-start(bf16[48,1536]{1,0:T(8,128)(2,1)S(1)} %collective-permute-done.34.refs_4_), channel_id=1, source_target_pairs={{0,2},{2,0},{4,6},{6,4},{8,10},{10,8},{12,14},{14,12},{16,18},{18,... | collective-permute-start | bytes 442376 | tf_op jit(solution)/shard_map/ppermute | solution.py:30
  70.1 12.6 %collective-permute-start.43 = (bf16[48,1536]{1,0:T(8,128)(2,1)S(1)}, bf16[48,1536]{1,0:T(8,128)(2,1)S(1)}, u32[]{:S(2)}, u32[]{:S(2)}) collective-permute-start(bf16[48,1536]{1,0:T(8,128)(2,1)S(1)} %collective-permute-done.42.refs_12_), channel_id=1, source_target_pairs={{0,2},{2,0},{4,6},{6,4},{8,10},{10,8},{12,14},{14,12},{16,18},{18,... | collective-permute-start | bytes 442376 | tf_op jit(solution)/shard_map/ppermute | solution.py:30
  87.4 15.3 %collective-permute-start.46 = (bf16[384,768]{1,0:T(8,128)(2,1)S(1)}, bf16[384,768]{1,0:T(8,128)(2,1)S(1)}, u32[]{:S(2)}, u32[]{:S(2)}) collective-permute-start(bf16[384,768]{1,0:T(8,128)(2,1)S(1)} %get-tuple-element.99.own_ref), channel_id=1, source_target_pairs={{0,1},{1,0},{2,3},{3,2},{4,5},{5,4},{6,7},{7,6},{8,9},{9,8},{10,11... | collective-permute-start | bytes 1769480 | tf_op jit(solution)/shard_map/ppermute | solution.py:107
  110.1 15.3 %collective-permute-start.47 = (bf16[384,768]{1,0:T(8,128)(2,1)S(1)}, bf16[384,768]{1,0:T(8,128)(2,1)S(1)}, u32[]{:S(2)}, u32[]{:S(2)}) collective-permute-start(bf16[384,768]{1,0:T(8,128)(2,1)S(1)} %get-tuple-element.103.own_ref), channel_id=1, source_target_pairs={{0,1},{1,0},{2,3},{3,2},{4,5},{5,4},{6,7},{7,6},{8,9},{9,8},{10,11... | collective-permute-start | bytes 1769480 | tf_op jit(solution)/shard_map/ppermute | solution.py:107
  113.7 21.9 %collective-permute-start.51 = (bf16[4,48,1536]{2,1,0:T(8,128)(2,1)}, bf16[4,48,1536]{2,1,0:T(8,128)(2,1)}, u32[]{:S(2)}, u32[]{:S(2)}) collective-permute-start(bf16[4,48,1536]{2,1,0:T(8,128)(2,1)} %get-tuple-element.109), channel_id=1, source_target_pairs={{0,4},{2,6},{4,0},{6,2},{8,12},{10,14},{12,8},{14,10},{16,20},{18,... | collective-permute-start | bytes 1769480 | tf_op jit(solution)/shard_map/ppermute | solution.py:30
  128.6 37.0 %collective-permute-start.64 = (bf16[4,48,1536]{2,1,0:T(8,128)(2,1)}, bf16[4,48,1536]{2,1,0:T(8,128)(2,1)}, u32[]{:S(2)}, u32[]{:S(2)}) collective-permute-start(bf16[4,48,1536]{2,1,0:T(8,128)(2,1)} %get-tuple-element.115), channel_id=1, source_target_pairs={{0,4},{2,6},{4,0},{6,2},{8,12},{10,14},{12,8},{14,10},{16,20},{18,... | collective-permute-start | bytes 1769480 | tf_op jit(solution)/shard_map/ppermute | solution.py:30
  131.6 16.2 %collective-permute-start.61 = (bf16[4,48,384]{2,1,0:T(8,128)(2,1)}, bf16[4,48,384]{2,1,0:T(8,128)(2,1)}, u32[]{:S(2)}, u32[]{:S(2)}) collective-permute-start(bf16[4,48,384]{2,1,0:T(8,128)(2,1)} %get-tuple-element.121), channel_id=1, source_target_pairs={{0,4},{2,6},{4,0},{6,2},{8,12},{10,14},{12,8},{14,10},{16,20},{18,... | collective-permute-start | bytes 442376 | tf_op jit(solution)/shard_map/ppermute | solution.py:30
  152.6 17.8 %collective-permute-start.53 = (bf16[8,3,48,384]{3,2,1,0:T(8,128)(2,1)S(1)}, bf16[8,3,48,384]{3,2,1,0:T(8,128)(2,1)S(1)}, u32[]{:S(2)}, u32[]{:S(2)}) collective-permute-start(bf16[8,3,48,384]{3,2,1,0:T(8,128)(2,1)S(1)} %get-tuple-element.129), channel_id=1, source_target_pairs={{0,2},{2,0},{4,6},{6,4},{8,10},{10,8},{12,14},{14,12},{16,18},{18,... | collective-permute-start | bytes 2654216 | tf_op jit(solution)/shard_map/ppermute | solution.py:30
  160.6 9.8 %collective-permute-start.60 = (f32[54,128]{1,0:T(8,128)S(1)}, f32[54,128]{1,0:T(8,128)S(1)}, u32[]{:S(2)}, u32[]{:S(2)}) collective-permute-start(f32[54,128]{1,0:T(8,128)S(1)} %add.22), channel_id=1, source_target_pairs={{0,16},{2,18},{4,20},{6,22},{8,24},{10,26},{12,28},{14,30},{16,0},... | collective-permute-start | bytes 82952 | tf_op jit(solution)/shard_map/ppermute | solution.py:30
  165.6 14.3 %collective-permute-start.67 = (bf16[2,48,1536]{2,1,0:T(8,128)(2,1)S(1)}, bf16[2,48,1536]{2,1,0:T(8,128)(2,1)S(1)}, u32[]{:S(2)}, u32[]{:S(2)}) collective-permute-start(bf16[2,48,1536]{2,1,0:T(8,128)(2,1)S(1)} %copy-done.29), channel_id=1, source_target_pairs={{0,8},{2,10},{4,12},{6,14},{8,0},{10,2},{12,4},{14,6},{16,24},{18,... | collective-permute-start | bytes 884744 | tf_op jit(solution)/shard_map/ppermute | solution.py:30
  167.0 11.5 %collective-permute-start.65 = (bf16[2,48,1536]{2,1,0:T(8,128)(2,1)S(1)}, bf16[2,48,1536]{2,1,0:T(8,128)(2,1)S(1)}, u32[]{:S(2)}, u32[]{:S(2)}) collective-permute-start(bf16[2,48,1536]{2,1,0:T(8,128)(2,1)S(1)} %get-tuple-element.147), channel_id=1, source_target_pairs={{0,8},{2,10},{4,12},{6,14},{8,0},{10,2},{12,4},{14,6},{16,24},{18,... | collective-permute-start | bytes 884744 | tf_op jit(solution)/shard_map/ppermute | solution.py:30
  168.9 24.4 %collective-permute-start.52 = (bf16[384,768]{1,0:T(8,128)(2,1)S(1)}, bf16[384,768]{1,0:T(8,128)(2,1)}, u32[]{:S(2)}, u32[]{:S(2)}) collective-permute-start(bf16[384,768]{1,0:T(8,128)(2,1)S(1)} %input_grad.1), channel_id=1, source_target_pairs={{0,1},{1,0},{2,3},{3,2},{4,5},{5,4},{6,7},{7,6},{8,9},{9,8},{10,11... | collective-permute-start | bytes 1769480 | tf_op jit(solution)/shard_map/ppermute | solution.py:107
  170.7 12.1 %collective-permute-start.54 = (bf16[4,3,48,384]{3,2,1,0:T(8,128)(2,1)S(1)}, bf16[4,3,48,384]{3,2,1,0:T(8,128)(2,1)S(1)}, u32[]{:S(2)}, u32[]{:S(2)}) collective-permute-start(bf16[4,3,48,384]{3,2,1,0:T(8,128)(2,1)S(1)} %get-tuple-element.131), channel_id=1, source_target_pairs={{0,4},{2,6},{4,0},{6,2},{8,12},{10,14},{12,8},{14,10},{16,20},{18,... | collective-permute-start | bytes 1327112 | tf_op jit(solution)/shard_map/ppermute | solution.py:30
  179.2 11.0 %collective-permute-start.66 = (bf16[1,48,1536]{2,1,0:T(8,128)(2,1)}, bf16[1,48,1536]{2,1,0:T(8,128)(2,1)S(1)}, u32[]{:S(2)}, u32[]{:S(2)}) collective-permute-start(bf16[1,48,1536]{2,1,0:T(8,128)(2,1)} %get-tuple-element.149), channel_id=1, source_target_pairs={{0,16},{2,18},{4,20},{6,22},{8,24},{10,26},{12,28},{14,30},{16,0},... | collective-permute-start | bytes 442376 | tf_op jit(solution)/shard_map/ppermute | solution.py:30
  180.6 11.8 %collective-permute-start.68 = (bf16[1,48,1536]{2,1,0:T(8,128)(2,1)}, bf16[1,48,1536]{2,1,0:T(8,128)(2,1)S(1)}, u32[]{:S(2)}, u32[]{:S(2)}) collective-permute-start(bf16[1,48,1536]{2,1,0:T(8,128)(2,1)} %get-tuple-element.152), channel_id=1, source_target_pairs={{0,16},{2,18},{4,20},{6,22},{8,24},{10,26},{12,28},{14,30},{16,0},... | collective-permute-start | bytes 442376 | tf_op jit(solution)/shard_map/ppermute | solution.py:30
  182.9 10.3 %collective-permute-start.55 = (bf16[2,3,48,384]{3,2,1,0:T(8,128)(2,1)S(1)}, bf16[2,3,48,384]{3,2,1,0:T(8,128)(2,1)S(1)}, u32[]{:S(2)}, u32[]{:S(2)}) collective-permute-start(bf16[2,3,48,384]{3,2,1,0:T(8,128)(2,1)S(1)} %get-tuple-element.133), channel_id=1, source_target_pairs={{0,8},{2,10},{4,12},{6,14},{8,0},{10,2},{12,4},{14,6},{16,24},{18,... | collective-permute-start | bytes 663560 | tf_op jit(solution)/shard_map/ppermute | solution.py:30
  (80 other events, 760.5 us)

commit v3 on v2

v3 whole, which is shorter than its diff:
```python
import functools

import jax
import jax.numpy as jnp
from jax import lax
from jax.experimental import pallas as pl
from jax.experimental.pallas import tpu as pltpu
from jax.sharding import PartitionSpec as P

HEAD = 64
CLUSTER = 128
PAIR = 128
NORM_EPS = 1e-05
EXCLUDED = -1e30
VMEM_BYTES = 24 * 1024 * 1024

F32 = jnp.float32
BF16 = jnp.bfloat16

NN = (((1,), (0,)), ((), ()))
NT = (((1,), (1,)), ((), ()))
TN = (((0,), (0,)), ((), ()))


def dot(a, b, dims=NN):
    return lax.dot_general(a, b, dims, preferred_element_type=F32)


def swap(array, axis, offset, size):
    return lax.ppermute(array, axis, [(i, i ^ offset) for i in range(size)])


def after(array, *earlier):
    return lax.optimization_barrier((array, *earlier))[0]


def block_orders(dp, steps):
    offsets = [0]
    for step in reversed(steps[1:]):
        offsets = offsets + [o ^ step for o in offsets]
    return offsets, [o ^ steps[0] for o in offsets]


def halve_kernel(*refs):
    (keep_ref, got_ref), outs = refs[:2], refs[2:]
    total = keep_ref[...].astype(F32) + got_ref[...].astype(F32)
    if total.shape[0] == 1:
        for out in outs:
            if len(outs) == 1:
                out[...] = total[0]
            elif len(out.shape) == 3:
                out[...] = total[0, : out.shape[0]]
            else:
                out[...] = total[0, -1]
    else:
        half = total.shape[0] // 2
        outs[0][...] = total[:half]
        outs[1][...] = total[half:].astype(BF16)


def halve(keep, got, name):
    shape, half = keep.shape[1:], keep.shape[0] // 2
    if half == 0 and len(shape) == 3:
        parts = [((shape[0] - 1, *shape[1:]), F32, "free"), (shape[1:], F32, "free")]
        return call(halve_kernel, parts, [keep, got], name)
    if half == 0:
        return call(halve_kernel, [(shape, F32, "free")], [keep, got], name)[0]
    return call(halve_kernel, [((half, *shape), F32), ((half, *shape), BF16)], [keep, got], name)


def rows_of(shapes):
    places = []
    for i, (height, width) in enumerate(shapes):
        places += [(i, r, slice(c, c + PAIR)) for r in range(height) for c in range(0, width, PAIR)]
    return places


def pack_kernel(*refs):
    ins, out_ref = refs[:-1], refs[-1]
    out_ref[...] = jnp.zeros(out_ref.shape, F32)
    for k, (i, r, columns) in enumerate(rows_of([ref.shape for ref in ins])):
        out_ref[k : k + 1, :] = ins[i][r : r + 1, columns]


def unpack_kernel(order, shapes, in_ref, *outs):
    for k, (i, r, columns) in enumerate(rows_of(shapes)):
        out, row = order[i][r]
        if outs[out].shape[1] == PAIR:
            row, columns = columns.start // PAIR, slice(0, PAIR)
        outs[out][row : row + 1, columns] = in_ref[k : k + 1, :]


def other_half(array):
    return lax.ppermute(array, "tensor", [(0, 1), (1, 0)])


def call(body, outs, ins, name, scratch=()):
    kinds = [o[2] if len(o) > 2 else "vmem" for o in outs]
    make = {"vmem": pltpu.VMEM, "hbm": pltpu.HBM, "free": jax.ShapeDtypeStruct}
    in_specs, values = [], []
    for x in ins:
        away = isinstance(x, Away)
        in_specs.append(pl.BlockSpec(memory_space=pl.ANY if away else pltpu.VMEM))
        values.append(pltpu.with_memory_space_constraint(x.array, pltpu.HBM) if away else x)
    return pl.pallas_call(
        body,
        out_shape=tuple(make[k](o[0], o[1]) for o, k in zip(outs, kinds)),
        in_specs=in_specs,
        out_specs=tuple(
            pl.BlockSpec(memory_space=pl.ANY if k == "hbm" else pltpu.VMEM) for k in kinds
        ),
        scratch_shapes=list(scratch),
        compiler_params=pltpu.CompilerParams(vmem_limit_bytes=VMEM_BYTES),
        name=name,
    )(*values)


class Away:
    def __init__(self, array):
        self.array = array


def assemble(pieces, whole):
    count = len(pieces)
    me = lax.axis_index("dp") if count > 1 else 0
    for o, piece in enumerate(pieces):
        rows = piece.shape[-2]
        start = pl.multiple_of((me ^ o) * rows, 16) if count > 1 else 0
        if len(piece.shape) == 3:
            whole[:, pl.ds(start, rows), :] = piece[...]
        else:
            whole[pl.ds(start, rows), :] = piece[...]


def norm_rows(v):
    center = jnp.mean(v, axis=-1, keepdims=True)
    offset = v - center
    spread = jnp.mean(offset * offset, axis=-1, keepdims=True)
    scale = lax.rsqrt(spread + NORM_EPS)
    return offset * scale, scale


def norm_back(e, n, scale, gain):
    ea = e * gain
    return scale * (
        ea
        - jnp.mean(ea, axis=-1, keepdims=True)
        - n * jnp.mean(ea * n, axis=-1, keepdims=True)
    )


def admitted_kernel(heads, docs, lengths_ref, perm_ref, bias_ref):
    rows = bias_ref.shape[1]
    spot = lax.broadcasted_iota(jnp.int32, (rows, PAIR), 0)
    lane = lax.broadcasted_iota(jnp.int32, (rows, PAIR), 1)
    doc = jnp.zeros((rows, PAIR), jnp.int32)
    bound = jnp.int32(0)
    for k in range(docs):
        bound = bound + lengths_ref[0, k]
        doc = doc + (spot >= bound).astype(jnp.int32)
    doc_hot = (lane == doc + PAIR // 2).astype(F32)
    cluster_hot = (lane == spot // CLUSTER).astype(BF16)
    place = lax.broadcasted_iota(jnp.int32, (rows, rows), 0)
    for h in range(heads):
        here = (place == perm_ref[h]).astype(BF16)
        key = (dot(here, cluster_hot) + doc_hot).astype(BF16)
        same = dot(key, key, NT)
        bias_ref[h] = jnp.where(same > 1.5, 0.0, EXCLUDED).astype(BF16)


def attention_kernel(count, heads, scale, *refs):
    pieces, refs = refs[:count], refs[count:]
    (tokens_ref, bias_ref, admit_ref, qkv_out, prob_out, attended_ref, out_ref, whole,
     qkv_ref, prob_ref, sems) = refs
    assemble(pieces, whole)
    tokens = tokens_ref[...]
    copies = []

    def away(source, target):
        copies.append(pltpu.make_async_copy(source, target, sems.at[len(copies)]))
        copies[-1].start()

    for s in range(3):
        part = dot(tokens, whole[s])
        if s == 0:
            part = part + bias_ref[0:1, :]
        if s == 2:
            part = part + bias_ref[1:2, :]
        qkv_ref[s] = part.astype(BF16)
        away(qkv_ref.at[s], qkv_out.at[s])
    lane = lax.broadcasted_iota(jnp.int32, (tokens.shape[0], PAIR), 1)
    for pair in range(heads // 2):
        columns = slice(pair * PAIR, (pair + 1) * PAIR)
        q = qkv_ref[0, :, columns]
        k = qkv_ref[1, :, columns]
        v = qkv_ref[2, :, columns]
        mixed = []
        for side in range(2):
            mine = (lane < HEAD) if side == 0 else (lane >= HEAD)
            scores = dot(jnp.where(mine, q, jnp.zeros_like(q)), k, NT) * scale
            scores = scores + admit_ref[2 * pair + side].astype(F32)
            top = jnp.max(scores, axis=-1, keepdims=True)
            terms = jnp.exp(scores - top)
            total = jnp.sum(terms, axis=-1, keepdims=True)
            prob = (terms * (1.0 / total)).astype(BF16)
            prob_ref[2 * pair + side] = prob
            away(prob_ref.at[2 * pair + side], prob_out.at[2 * pair + side])
            mixed.append(dot(prob, v))
        attended_ref[:, columns] = jnp.where(lane < HEAD, mixed[0], mixed[1]).astype(BF16)
    out_ref[...] = dot(attended_ref[...], whole[3], NT).astype(BF16)
    for copy in copies:
        copy.wait()


def feed_kernel(count, *refs):
    pieces, refs = refs[:count], refs[count:]
    (tokens_ref, own_ref, got_ref, out_bias_ref, gain_ref, shift_ref, bias_ref,
     n_ref, scale_ref, low_ref, active_ref, slope_ref, out_ref, whole) = refs
    assemble(pieces, whole)
    attention = own_ref[...].astype(F32) + got_ref[...].astype(F32) + out_bias_ref[0:1, :]
    n, scale = norm_rows(tokens_ref[...].astype(F32) + attention)
    n_ref[...] = n
    scale_ref[...] = jnp.broadcast_to(scale, scale_ref.shape)
    low_ref[...] = (n * gain_ref[0:1, :] + shift_ref[0:1, :]).astype(BF16)
    units = whole.shape[2]
    step = 256
    for start in range(0, units, step):
        part = slice(start, start + step)
        pre = dot(low_ref[...], whole[0, :, part]) + bias_ref[:, part]
        half = 0.5 * (1.0 + lax.erf(pre * (2.0**-0.5)))
        active_ref[:, part] = (pre * half).astype(BF16)
        bell = jnp.exp(-0.5 * pre * pre) * 0.3989422804014327
        slope_ref[:, part] = (half + pre * bell).astype(BF16)
    out_ref[...] = dot(active_ref[...], whole[1], NT).astype(BF16)


def feed_back_kernel(
    whole, n_ref, own_ref, got_ref, out_bias_ref, gain_ref, shift_ref, seed_ref,
    masked_ref, slope_ref, layer_ref, two_ref, low_ref, inner_ref, first_ref, sums_ref, inner_sum_ref,
):
    first = n_ref[...] * gain_ref[0:1, :] + shift_ref[0:1, :]
    feed = own_ref[...].astype(F32) + got_ref[...].astype(F32) + out_bias_ref[1:2, :]
    n, scale = norm_rows(first + feed)
    gain = gain_ref[1:2, :]
    layer_ref[...] = (n * gain + shift_ref[1:2, :]).astype(BF16)
    e = seed_ref[...].astype(F32) * masked_ref[...]
    grad = norm_back(e, n, scale, gain)
    two_ref[...] = grad
    low_ref[...] = grad.astype(BF16)
    sums_ref[0:1, :] = jnp.sum(e * n, axis=0, keepdims=True)
    sums_ref[1:2, :] = jnp.sum(e, axis=0, keepdims=True)
    sums_ref[2:3, :] = jnp.sum(grad, axis=0, keepdims=True)
    units = whole.shape[2]
    step = 256
    for start in range(0, units, step):
        part = slice(start, start + step)
        inner = (dot(low_ref[...], whole[1, :, part]) * slope_ref[:, part].astype(F32)).astype(BF16)
        inner_ref[:, part] = inner
        inner_sum_ref[:, part] = jnp.sum(inner.astype(F32), axis=0, keepdims=True)
    first_ref[...] = dot(inner_ref[...], whole[0], NT).astype(BF16)


def weight_grad_kernel(orders, left_ref, right_ref, keep_ref, send_ref, whole):
    whole[...] = dot(left_ref[...], right_ref[...], TN)
    me = lax.axis_index("dp")
    rows = keep_ref.shape[1]
    for order, target in zip(orders, (keep_ref, send_ref)):
        for k, o in enumerate(order):
            start = pl.multiple_of((me ^ o) * rows, 16)
            target[k] = whole[pl.ds(start, rows), :].astype(BF16)


def norm_one_back_kernel(own_ref, got_ref, two_ref, n_ref, scale_ref, gain_ref, one_ref, low_ref, sums_ref):
    e = own_ref[...].astype(F32) + got_ref[...].astype(F32) + two_ref[...]
    n = n_ref[...]
    grad = norm_back(e, n, scale_ref[:, 0:1], gain_ref[0:1, :])
    one_ref[...] = grad
    low_ref[...] = grad.astype(BF16)
    sums_ref[0:1, :] = jnp.sum(e * n, axis=0, keepdims=True)
    sums_ref[1:2, :] = jnp.sum(e, axis=0, keepdims=True)
    sums_ref[2:3, :] = jnp.sum(grad, axis=0, keepdims=True)


def attention_back_kernel(
    heads, scale, whole_ref, low_ref, qkv_in, prob_in, grads_ref, sums_ref, given, qkv_ref, prob_ref, sems
):
    copies = [pltpu.make_async_copy(qkv_in, qkv_ref, sems.at[heads])]
    for h in range(heads):
        copies.append(pltpu.make_async_copy(prob_in.at[h], prob_ref.at[h], sems.at[h]))
    for copy in copies:
        copy.start()
    given[...] = dot(low_ref[...], whole_ref[3]).astype(BF16)
    lane = lax.broadcasted_iota(jnp.int32, (given.shape[0], PAIR), 1)
    copies[0].wait()
    for pair in range(heads // 2):
        columns = slice(pair * PAIR, (pair + 1) * PAIR)
        q = qkv_ref[0, :, columns]
        k = qkv_ref[1, :, columns]
        v = qkv_ref[2, :, columns]
        d = given[:, columns]
        parts = []
        for side in range(2):
            mine = (lane < HEAD) if side == 0 else (lane >= HEAD)
            copies[1 + 2 * pair + side].wait()
            prob = prob_ref[2 * pair + side]
            d_prob = dot(jnp.where(mine, d, jnp.zeros_like(d)), v, NT)
            wide = prob.astype(F32)
            center = jnp.sum(d_prob * wide, axis=-1, keepdims=True)
            score = (wide * (d_prob - center)).astype(BF16)
            parts.append((dot(score, k), dot(score, q, TN), dot(prob, d, TN)))
        for s in range(3):
            both = jnp.where(lane < HEAD, parts[0][s], parts[1][s])
            if s < 2:
                both = both * scale
            both = both.astype(BF16)
            grads_ref[s, :, columns] = both
            if s != 1:
                sums_ref[s // 2 : s // 2 + 1, columns] = jnp.sum(both.astype(F32), axis=0, keepdims=True)


def input_grad_kernel(whole_ref, grads_ref, out_ref):
    total = dot(grads_ref[0], whole_ref[0], NT)
    total = total + dot(grads_ref[1], whole_ref[1], NT)
    total = total + dot(grads_ref[2], whole_ref[2], NT)
    out_ref[...] = total.astype(BF16)


def mixer_grad_kernel(orders, tokens_ref, grads_ref, low_ref, attended_ref, keep_ref, send_ref, whole):
    me = lax.axis_index("dp")
    rows = keep_ref.shape[2]
    for s in range(4):
        if s < 3:
            whole[...] = dot(tokens_ref[...], grads_ref[s], TN)
        else:
            whole[...] = dot(low_ref[...], attended_ref[...], TN)
        for order, target in zip(orders, (keep_ref, send_ref)):
            for k, o in enumerate(order):
                start = pl.multiple_of((me ^ o) * rows, 16)
                target[k, s] = whole[pl.ds(start, rows), :].astype(BF16)


def add_kernel(own_ref, got_ref, rest_ref, out_ref):
    out_ref[...] = own_ref[...].astype(F32) + got_ref[...].astype(F32) + rest_ref[...]


def plain_grad_kernel(left_ref, right_ref, out_ref):
    out_ref[...] = dot(left_ref[...], right_ref[...], TN)


def shards(
    dp,
    tokens,
    project_weight,
    project_bias,
    output_weight,
    output_bias,
    expand_weight,
    expand_bias,
    shrink_weight,
    norm_gain,
    norm_shift,
    doc_lengths,
    cluster_perm,
    masked,
    out_grad,
):
    rows, width = tokens.shape
    piece_rows, _, columns = project_weight.shape
    units = expand_weight.shape[1]
    heads = columns // HEAD
    scale = HEAD ** (-0.5)
    in_pieces = dp == 16 and piece_rows % 16 == 0

    mixer_shard = jnp.concatenate([project_weight.transpose(1, 0, 2), output_weight.T[None]])
    feed_shard = jnp.stack([expand_weight, shrink_weight.T])
    (admit,) = call(
        functools.partial(admitted_kernel, heads, doc_lengths.shape[1]),
        [((heads, rows, rows), BF16)],
        [doc_lengths, cluster_perm.transpose(1, 0, 2)],
        "admitted",
    )
    if in_pieces:

        def go(array, step, *gate):
            return swap(after(array, *gate) if gate else array, "dp", step, dp)

        def cross(pieces):
            return [go(pieces[o ^ 1], 1) if o & 1 else pieces[o] for o in range(dp)]

        m = {0: mixer_shard}
        m[2] = go(m[0], 2)
        m[8] = go(m[0], 8)
        m[4] = go(m[0], 4)
        m[12] = go(m[8], 4, m[2], admit)
        m[6] = go(m[4], 2)
        m[10] = go(m[8], 2)
        m[14] = go(m[12], 2)
        mixer_all = cross(m)
        f = {0: feed_shard}
        f[8] = go(f[0], 8, m[8])
        f[4] = go(f[0], 4, m[12])
        f[2] = go(f[0], 2, m[14])
        gate = ()
    else:
        gate = ()
        mixer_all = [lax.all_gather(mixer_shard, "dp", axis=1, tiled=True)]
        feed_all = [lax.all_gather(feed_shard, "dp", axis=1, tiled=True)]
    count = len(mixer_all)

    def whole(*shape):
        return pltpu.VMEM(shape, BF16)

    qkv, prob, attended, attention_own, mixer = call(
        functools.partial(attention_kernel, count, heads, scale),
        [
            ((3, rows, columns), BF16, "hbm"),
            ((heads, rows, rows), BF16, "hbm"),
            ((rows, columns), BF16),
            ((rows, width), BF16),
            ((4, width, columns), BF16),
        ],
        [*mixer_all, tokens, after(project_bias, *gate), admit],
        "attention",
        scratch=[
            whole(3, rows, columns), whole(heads, rows, rows), pltpu.SemaphoreType.DMA((3 + heads,)),
        ],
    )
    attention_got = other_half(attention_own)
    if in_pieces:
        f[12] = go(f[8], 4, mixer)
        f[6] = go(f[4], 2, mixer)
        f[10] = go(f[8], 2, mixer)
        f[14] = go(f[12], 2)
        feed_all = cross(f)
    n_one, scale_one, first_low, active_low, slope, feed_own, feed = call(
        functools.partial(feed_kernel, count),
        [
            ((rows, width), F32),
            ((rows, PAIR), F32),
            ((rows, width), BF16),
            ((rows, units), BF16),
            ((rows, units), BF16),
            ((rows, width), BF16),
            ((2, width, units), BF16),
        ],
        [
            *feed_all, tokens, attention_own, attention_got, output_bias,
            norm_gain, norm_shift, expand_bias[None, :],
        ],
        "feed_forward",
    )
    feed_got = other_half(feed_own)
    layer_out, residual_two, feed_low, inner_low, first_own, sums_two, inner_sum = call(
        feed_back_kernel,
        [
            ((rows, width), BF16, "free"),
            ((rows, width), F32),
            ((rows, width), BF16),
            ((rows, units), BF16),
            ((rows, width), BF16),
            ((3, width), F32),
            ((1, units), F32),
        ],
        [
            feed, n_one, feed_own, feed_got, output_bias,
            norm_gain, norm_shift, out_grad, masked.astype(F32)[:, None], slope,
        ],
        "feed_backward",
    )
    first_got = other_half(first_own)

    far = [4, 8]

    def weight_grad(left, right, name, steps=()):
        wide = right.shape[1]
        if in_pieces:
            return call(
                functools.partial(weight_grad_kernel, block_orders(dp, steps)),
                [((dp // 2, piece_rows, wide), BF16)] * 2,
                [left, right],
                name,
                scratch=[pltpu.VMEM((width, wide), F32)],
            )
        (grad,) = call(plain_grad_kernel, [((width, wide), F32, "free")], [left, right], name)
        return lax.psum_scatter(grad, "dp", scatter_dimension=0, tiled=True), grad

    shrink_keep, shrink_send = weight_grad(feed_low, active_low, "shrink_grad", [1, 4, 8, 2])
    expand_keep, expand_send = weight_grad(
        first_low, after(inner_low, shrink_send), "expand_grad", [1, 2, 4, 8]
    )
    gate_one, gate_two = (), ()
    if in_pieces:
        shrink_keep, shrink_send = halve(shrink_keep, swap(shrink_send, "dp", 1, dp), "shrink_sum_core")
        expand_keep, expand_send = halve(expand_keep, swap(expand_send, "dp", 1, dp), "expand_sum_core")
        shrink_got = swap(shrink_send, "dp", 4, dp)
        expand_got = swap(expand_send, "dp", 2, dp)
        gate_one, gate_two = (shrink_send, expand_send), (shrink_got, expand_got)
    residual_one, attention_low, sums_one = call(
        norm_one_back_kernel,
        [((rows, width), F32), ((rows, width), BF16), ((3, width), F32)],
        [first_own, first_got, residual_two, n_one, scale_one, after(norm_gain, *gate_one)],
        "norm_one_backward",
    )
    project_low, project_sums = call(
        functools.partial(attention_back_kernel, heads, scale),
        [((3, rows, columns), BF16), ((2, columns), F32)],
        [mixer, after(attention_low, *gate_two), Away(qkv), Away(prob)],
        "attention_backward",
        scratch=[
            whole(rows, columns), whole(3, rows, columns), whole(heads, rows, rows),
            pltpu.SemaphoreType.DMA((heads + 1,)),
        ],
    )
    vectors = [sums_one, sums_two, inner_sum, project_sums]
    shapes = [v.shape for v in vectors]
    height = -(-sum(v.size for v in vectors) // PAIR // 8) * 8
    (packed,) = call(pack_kernel, [((height, PAIR), F32)], vectors, "pack")

    def input_grad():
        (own,) = call(
            input_grad_kernel, [((rows, width), BF16)], [mixer, project_low], "input_grad"
        )
        return call(
            add_kernel,
            [((rows, width), F32, "free")],
            [own, other_half(own), residual_one],
            "tokens_grad",
        )[0]

    if in_pieces:
        keep, send = call(
            functools.partial(mixer_grad_kernel, block_orders(dp, [1, 2, *far])),
            [((dp // 2, 4, piece_rows, columns), BF16)] * 2,
            [tokens, project_low, attention_low, attended],
            "mixer_grad",
            scratch=[pltpu.VMEM((width, columns), F32)],
        )
        got = swap(send, "dp", 1, dp)
        packed = packed + swap(packed, "dp", 1, dp)
        keep, send = halve(keep, after(got, packed), "mixer_sum_core")
        got = swap(send, "dp", 2, dp)
        packed = packed + swap(packed, "dp", 2, dp)
        tokens_grad = input_grad()
        shrink_keep, shrink_send = halve(shrink_keep, shrink_got, "shrink_sum_4")
        shrink_got = swap(shrink_send, "dp", 8, dp)
        expand_keep, expand_send = halve(expand_keep, expand_got, "expand_sum_2")
        expand_got = swap(expand_send, "dp", 4, dp)
        keep, send = halve(keep, after(got, packed, expand_got), "mixer_sum_2")
        got = swap(send, "dp", 4, dp)
        packed = packed + swap(packed, "dp", 4, dp)
        expand_keep, expand_send = halve(expand_keep, expand_got, "expand_sum_4")
        expand_got = swap(expand_send, "dp", 8, dp)
        shrink_keep, shrink_send = halve(shrink_keep, shrink_got, "shrink_sum_8")
        shrink_got = swap(shrink_send, "dp", 2, dp)
        keep, send = halve(keep, after(got, packed, tokens_grad), "mixer_sum_4")
        got = swap(send, "dp", 8, dp)
        packed = packed + swap(packed, "dp", 8, dp)
        expand_part = halve(expand_keep, expand_got, "expand_sum_8")
        shrink_part = halve(shrink_keep, shrink_got, "shrink_sum_2")
        got = after(got, packed, expand_part, shrink_part)
        project_part, output_part = halve(keep, got, "mixer_sum_8")
    else:
        tokens_grad = input_grad()
        packed = lax.psum(packed, "dp")
        shrink_part, expand_part = shrink_keep, expand_keep
        lefts = [tokens, tokens, tokens, attention_low]
        rights = [project_low[0], project_low[1], project_low[2], attended]
        parts = [weight_grad(l, r, "mixer_grad")[0] for l, r in zip(lefts, rights)]
        project_part, output_part = jnp.stack(parts[:3]), parts[3]
    order = [[(2, 0), (3, 0), (1, 0)], [(2, 1), (3, 1), (1, 1)], [(4, 0)], [(0, 0), (0, 1)]]
    project_total, output_total, gain_total, shift_total, inner_total = call(
        functools.partial(unpack_kernel, order, shapes),
        [
            ((2, columns), F32, "free"),
            ((2, width), F32, "free"),
            ((2, width), F32, "free"),
            ((2, width), F32, "free"),
            ((units // PAIR, PAIR), F32, "free"),
        ],
        [packed],
        "unpack",
    )
    return (
        layer_out,
        tokens_grad,
        project_part.transpose(1, 0, 2),
        project_total,
        output_part.T,
        output_total,
        expand_part,
        inner_total.reshape(units),
        shrink_part.T,
        gain_total,
        shift_total,
    )


def solution(mesh):
    in_specs = (
        P("dp", None),
        P("dp", None, "tensor"),
        P(None, "tensor"),
        P("tensor", "dp"),
        P(),
        P("dp", "tensor"),
        P("tensor"),
        P("tensor", "dp"),
        P(),
        P(),
        P("dp", None),
        P("dp", "tensor", None),
        P("dp"),
        P("dp", None),
    )
    out_specs = (
        P("dp", None),
        P("dp", None),
        P("dp", None, "tensor"),
        P(None, "tensor"),
        P("tensor", "dp"),
        P(),
        P("dp", "tensor"),
        P("tensor"),
        P("tensor", "dp"),
        P(),
        P(),
    )
    body = functools.partial(shards, mesh.shape["dp"])
    return jax.shard_map(body, mesh=mesh, in_specs=in_specs, out_specs=out_specs, check_vma=False)
```

time: 201 us -> 171 us (0.85)
  local copies, waits for them, and re-layouts: 17.3 us -> 1.52 us
  Pallas kernels: 43.3 us -> 31.5 us
  waiting for transfers between devices: 81.3 us -> 88.3 us
  other arithmetic: 7.15 us -> 1.04 us
  starting transfers between devices: 49.8 us -> 47 us
    unnamed x72 -> x24, local copies, waits for them, and re-layouts: 14.1 us -> 1.41 us
    pallas_call x28 -> x25, Pallas kernels: 43.3 us -> 31.5 us  [call(): pl.pallas_call(body, out_shape=tuple((make[k](o[0], o[1]) for o, k in zip...]
    ppermute x65 -> x46, waiting for transfers between devices: 58.8 us -> 62.3 us  [swap(): return lax.ppermute(array, axis, [(i, i ^ offset) for i in range(size)])]
    ppermute x4, waiting for transfers between devices: 22.5 us -> 26 us  [other_half(): return lax.ppermute(array, 'tensor', [(0, 1), (1, 0)])]
    ppermute x65 -> x46, starting transfers between devices: 43.6 us -> 40.8 us  [swap(): return lax.ppermute(array, axis, [(i, i ^ offset) for i in range(size)])]
    reshape x4 -> x0, local copies, waits for them, and re-layouts: 2.51 us -> none  [the longest x3 1.92 us: shards(): vector = jnp.concatenate([p.reshape(-1, PAIR) for p in pieces])]
    add x5 -> x4, other arithmetic: 2.26 us -> 0.02 us  [the longest x1 0.01 us: shards(): packed = packed + swap(packed, 'dp', 2, dp)]
  transfers between devices with their start and end apart: 69 -> 50, of which waited for: 25 -> 18; matrix products, arithmetic and copies ran while one was open for 5% -> 0% of each run, Pallas kernels for 16% -> 9%
where the time goes in v3:
time: 171 us; the launch traced here: 170 us
  waiting for transfers between devices  88.3 us (52%)
  starting transfers between devices  47 us (27%)
  Pallas kernels  31.5 us (18%)
    ppermute x46, waiting for transfers between devices, swap(): return lax.ppermute(array, axis, [(i, i ^ offset) for i in range(size)])  62.3 us
    ppermute x46, starting transfers between devices, swap(): return lax.ppermute(array, axis, [(i, i ^ offset) for i in range(size)])  40.8 us
    pallas_call x25, Pallas kernels, call(): pl.pallas_call(body, out_shape=tuple((make[k](o[0], o[1]) for o, k in zip...  31.5 us
    ppermute x4, waiting for transfers between devices, other_half(): return lax.ppermute(array, 'tensor', [(0, 1), (1, 0)])  26 us
    ppermute x4, starting transfers between devices, other_half(): return lax.ppermute(array, 'tensor', [(0, 1), (1, 0)])  6.21 us
  transfers between devices with their start and end apart: 50, of which 18 were waited for; matrix products, arithmetic and copies ran while one was open for 0% of the time, Pallas kernels for 9%

profile of v3, /device:TPU:0, one launch (start us, length us, event | category | flops | bytes accessed | tf_op | source)
XLA Modules:
  0.0 170.4 jit_solution(5940551403870254999)
XLA Ops:
  1.6 4.1 %collective-permute-start.1 = (bf16[4,48,384]{2,1,0:T(8,128)(2,1)S(1)}, bf16[4,48,384]{2,1,0:T(8,128)(2,1)S(1)}, u32[]{:S(2)}, u32[]{:S(2)}) collective-permute-start(bf16[4,48,384]{2,1,0:T(8,128)(2,1)S(1)} %pad_maximum_fusion.1.refs_0_), channel_id=1, source_target_pairs={{0,16},{2,18},{4,20},{6,22},{8,24},{10,26},{12,28},{14,30},{16,0},... | collective-permute-start | bytes 442376 | tf_op jit(solution)/shard_map/ppermute | solution.py:30
  10.2 1.9 %admitted.1.refs_18_ = bf16[6,384,384]{2,1,0:T(8,128)(2,1)S(1)} custom-call(s32[1,4]{1,0:T(1,128)S(1)} %copy-done.7, s32[6,1,384]{2,1,0:T(1,128)S(1)} %bitcast.13), custom_call_target="tpu_custom_call" | custom-call | tf_op jit(solution)/shard_map/admitted/pallas_call | solution.py:105
  15.5 2.5 %collective-permute-done.3.refs_12_ = bf16[4,48,384]{2,1,0:T(8,128)(2,1)S(1)} collective-permute-done((bf16[4,48,384]{2,1,0:T(8,128)(2,1)S(1)}, bf16[4,48,384]{2,1,0:T(8,128)(2,1)S(1)}, u32[]{:S(2)}, u32[]{:S(2)}) %collective-permute-start.3) | collective-permute-done | bytes 147488 | tf_op jit(solution)/shard_map/ppermute | solution.py:30
  21.6 3.1 %collective-permute-start.22 = (bf16[2,48,1536]{2,1,0:T(8,128)(2,1)S(1)}, bf16[2,48,1536]{2,1,0:T(8,128)(2,1)S(1)}, u32[]{:S(2)}, u32[]{:S(2)}) collective-permute-start(bf16[2,48,1536]{2,1,0:T(8,128)(2,1)S(1)} %pad_maximum_fusion.refs_0_), channel_id=1, source_target_pairs={{0,16},{2,18},{4,20},{6,22},{8,24},{10,26},{12,28},{14,30},{16,0},... | collective-permute-start | bytes 884744 | tf_op jit(solution)/shard_map/ppermute | solution.py:30
  29.2 8.4 %collective-permute-done.22.refs_8_ = bf16[2,48,1536]{2,1,0:T(8,128)(2,1)S(1)} collective-permute-done((bf16[2,48,1536]{2,1,0:T(8,128)(2,1)S(1)}, bf16[2,48,1536]{2,1,0:T(8,128)(2,1)S(1)}, u32[]{:S(2)}, u32[]{:S(2)}) %collective-permute-start.22) | collective-permute-done | bytes 294944 | tf_op jit(solution)/shard_map/ppermute | solution.py:30
  37.7 5.1 %attention.1 = (bf16[3,384,384]{2,1,0:T(8,128)(2,1)}, bf16[6,384,384]{2,1,0:T(8,128)(2,1)}, bf16[384,384]{1,0:T(8,128)(2,1)S(1)}, bf16[384,768]{1,0:T(8,128)(2,1)S(1)}, bf16[4,768,384]{2,1,0:T(8,128)(2,1)S(1)}) custom-call(bf16[4,48,384]{2,1,0:T(8,128)(2,1)S(1)} %pad_maximum_fusion.1.refs_0_, bf16[4,48,384]{2,1,0:T(8,128)(2,1)S(1)} %collective-permute-done.9.refs_1_, ...), custom_call_target="tpu_custom_call" | custom-call | tf_op jit(solution)/shard_map/attention/pallas_call | solution.py:105
  45.7 6.6 %collective-permute-done.26.refs_12_ = bf16[2,48,1536]{2,1,0:T(8,128)(2,1)S(1)} collective-permute-done((bf16[2,48,1536]{2,1,0:T(8,128)(2,1)S(1)}, bf16[2,48,1536]{2,1,0:T(8,128)(2,1)S(1)}, u32[]{:S(2)}, u32[]{:S(2)}) %collective-permute-start.26) | collective-permute-done | bytes 294944 | tf_op jit(solution)/shard_map/ppermute | solution.py:30
  54.5 4.7 %collective-permute-done.24.refs_10_ = bf16[2,48,1536]{2,1,0:T(8,128)(2,1)S(1)} collective-permute-done((bf16[2,48,1536]{2,1,0:T(8,128)(2,1)S(1)}, bf16[2,48,1536]{2,1,0:T(8,128)(2,1)S(1)}, u32[]{:S(2)}, u32[]{:S(2)}) %collective-permute-start.24) | collective-permute-done | bytes 294944 | tf_op jit(solution)/shard_map/ppermute | solution.py:30
  59.9 5.1 %collective-permute-done.28.refs_14_ = bf16[2,48,1536]{2,1,0:T(8,128)(2,1)S(1)} collective-permute-done((bf16[2,48,1536]{2,1,0:T(8,128)(2,1)S(1)}, bf16[2,48,1536]{2,1,0:T(8,128)(2,1)S(1)}, u32[]{:S(2)}, u32[]{:S(2)}) %collective-permute-start.28) | collective-permute-done | bytes 294944 | tf_op jit(solution)/shard_map/ppermute | solution.py:30
  65.1 2.6 %collective-permute-done.30.refs_18_ = bf16[384,768]{1,0:T(8,128)(2,1)S(1)} collective-permute-done((bf16[384,768]{1,0:T(8,128)(2,1)S(1)}, bf16[384,768]{1,0:T(8,128)(2,1)S(1)}, u32[]{:S(2)}, u32[]{:S(2)}) %collective-permute-start.30) | collective-permute-done | bytes 589856 | tf_op jit(solution)/shard_map/ppermute | solution.py:94
  67.7 3.3 %feed_forward.1 = (f32[384,768]{1,0:T(8,128)S(1)}, f32[384,128]{1,0:T(8,128)S(1)}, bf16[384,768]{1,0:T(8,128)(2,1)S(1)}, bf16[384,1536]{1,0:T(8,128)(2,1)S(1)}, ...) custom-call(bf16[2,48,1536]{2,1,0:T(8,128)(2,1)S(1)} %pad_maximum_fusion.refs_0_, ...), custom_call_target="tpu_custom_call" | custom-call | tf_op jit(solution)/shard_map/feed_forward/pallas_call | solution.py:105
  72.7 12.6 %collective-permute-done.31.got_ref = bf16[384,768]{1,0:T(8,128)(2,1)S(1)} collective-permute-done((bf16[384,768]{1,0:T(8,128)(2,1)S(1)}, bf16[384,768]{1,0:T(8,128)(2,1)S(1)}, u32[]{:S(2)}, u32[]{:S(2)}) %collective-permute-start.31) | collective-permute-done | bytes 589856 | tf_op jit(solution)/shard_map/ppermute | solution.py:94
  85.3 3.5 %feed_backward.1 = (bf16[384,768]{1,0:T(8,128)(2,1)}, f32[384,768]{1,0:T(8,128)S(1)}, bf16[384,768]{1,0:T(8,128)(2,1)S(1)}, bf16[384,1536]{1,0:T(8,128)(2,1)S(1)...) custom-call(bf16[2,768,1536]{2,1,0:T(8,128)(2,1)S(1)} %get-tuple-element.87.whole, ...), custom_call_target="tpu_custom_call" | custom-call | tf_op jit(solution)/shard_map/feed_backward/pallas_call | solution.py:105
  94.6 1.7 %collective-permute-start.35 = (bf16[4,48,1536]{2,1,0:T(8,128)(2,1)S(1)}, bf16[4,48,1536]{2,1,0:T(8,128)(2,1)S(1)}, u32[]{:S(2)}, u32[]{:S(2)}) collective-permute-start(bf16[4,48,1536]{2,1,0:T(8,128)(2,1)S(1)} %get-tuple-element.99), channel_id=1, source_target_pairs={{0,8},{2,10},{4,12},{6,14},{8,0},{10,2},{12,4},{14,6},{16,24},{18,... | collective-permute-start | bytes 1769480 | tf_op jit(solution)/shard_map/ppermute | solution.py:30
  97.3 10.7 %collective-permute-done.32.got_ref = bf16[384,768]{1,0:T(8,128)(2,1)S(1)} collective-permute-done((bf16[384,768]{1,0:T(8,128)(2,1)S(1)}, bf16[384,768]{1,0:T(8,128)(2,1)S(1)}, u32[]{:S(2)}, u32[]{:S(2)}) %collective-permute-start.32) | collective-permute-done | bytes 589856 | tf_op jit(solution)/shard_map/ppermute | solution.py:94
  111.3 5.6 %attention_backward.1 = (bf16[3,384,384]{2,1,0:T(8,128)(2,1)S(1)}, f32[2,384]{1,0:T(2,128)S(1)}) custom-call(bf16[4,768,384]{2,1,0:T(8,128)(2,1)S(1)} %get-tuple-element.82.whole_ref, bf16[384,768]{1,0:T(8,128)(2,1)S(1)} %get-tuple-element.108.low_ref, bf16[3,384,384]{2,1,0:T(8,128)(2,1)} %get-tuple-element.109.qkv_in, ...), custom_call_target="tpu_custom_call" | custom-call | tf_op jit(solution)/shard_map/attention_backward/pallas_call | solution.py:105
  116.9 1.7 %mixer_grad.1 = (bf16[8,4,48,384]{3,2,1,0:T(8,128)(2,1)S(1)}, bf16[8,4,48,384]{3,2,1,0:T(8,128)(2,1)S(1)}) custom-call(bf16[384,768]{1,0:T(8,128)(2,1)S(1)} %copy-done, bf16[3,384,384]{2,1,0:T(8,128)(2,1)S(1)} %get-tuple-element.111.grads_ref, bf16[384,768]{1,0:T(8,128)(2,1)S(1)} %get-tuple-element.108.low_ref, ...), custom_call_target="tpu_custom_call" | custom-call | tf_op jit(solution)/shard_map/mixer_grad/pallas_call | solution.py:105
  119.3 2.3 %collective-permute-done.39 = f32[56,128]{1,0:T(8,128)S(1)} collective-permute-done((f32[56,128]{1,0:T(8,128)S(1)}, f32[56,128]{1,0:T(8,128)S(1)}, u32[]{:S(2)}, u32[]{:S(2)}) %collective-permute-start.39) | collective-permute-done | bytes 28704 | tf_op jit(solution)/shard_map/ppermute | solution.py:30
  128.4 2.1 %collective-permute-start.48 = (bf16[2,48,1536]{2,1,0:T(8,128)(2,1)S(1)}, bf16[2,48,1536]{2,1,0:T(8,128)(2,1)S(1)}, u32[]{:S(2)}, u32[]{:S(2)}) collective-permute-start(bf16[2,48,1536]{2,1,0:T(8,128)(2,1)S(1)} %get-tuple-element.136), channel_id=1, source_target_pairs={{0,16},{2,18},{4,20},{6,22},{8,24},{10,26},{12,28},{14,30},{16,0},... | collective-permute-start | bytes 884744 | tf_op jit(solution)/shard_map/ppermute | solution.py:30
  130.5 7.4 %collective-permute-done.41 = f32[56,128]{1,0:T(8,128)S(1)} collective-permute-done((f32[56,128]{1,0:T(8,128)S(1)}, f32[56,128]{1,0:T(8,128)S(1)}, u32[]{:S(2)}, u32[]{:S(2)}) %collective-permute-start.41) | collective-permute-done | bytes 28704 | tf_op jit(solution)/shard_map/ppermute | solution.py:30
  140.2 9.4 %collective-permute-done.44 = f32[56,128]{1,0:T(8,128)S(1)} collective-permute-done((f32[56,128]{1,0:T(8,128)S(1)}, f32[56,128]{1,0:T(8,128)S(1)}, u32[]{:S(2)}, u32[]{:S(2)}) %collective-permute-start.44) | collective-permute-done | bytes 28704 | tf_op jit(solution)/shard_map/ppermute | solution.py:30
  150.5 2.6 %collective-permute-start.47 = (bf16[1,48,1536]{2,1,0:T(8,128)(2,1)S(1)}, bf16[1,48,1536]{2,1,0:T(8,128)(2,1)S(1)}, u32[]{:S(2)}, u32[]{:S(2)}) collective-permute-start(bf16[1,48,1536]{2,1,0:T(8,128)(2,1)S(1)} %get-tuple-element.133), channel_id=1, source_target_pairs={{0,16},{2,18},{4,20},{6,22},{8,24},{10,26},{12,28},{14,30},{16,0},... | collective-permute-start | bytes 442376 | tf_op jit(solution)/shard_map/ppermute | solution.py:30
  154.8 2.5 %collective-permute-start.46 = (f32[56,128]{1,0:T(8,128)S(1)}, f32[56,128]{1,0:T(8,128)S(1)}, u32[]{:S(2)}, u32[]{:S(2)}) collective-permute-start(f32[56,128]{1,0:T(8,128)S(1)} %add.14), channel_id=1, source_target_pairs={{0,16},{2,18},{4,20},{6,22},{8,24},{10,26},{12,28},{14,30},{16,0},... | collective-permute-start | bytes 86024 | tf_op jit(solution)/shard_map/ppermute | solution.py:30
  157.3 10.2 %collective-permute-done.46 = f32[56,128]{1,0:T(8,128)S(1)} collective-permute-done((f32[56,128]{1,0:T(8,128)S(1)}, f32[56,128]{1,0:T(8,128)S(1)}, u32[]{:S(2)}, u32[]{:S(2)}) %collective-permute-start.46) | collective-permute-done | bytes 28704 | tf_op jit(solution)/shard_map/ppermute | solution.py:30
  (134 shorter events, 49.5 us)
Async XLA Ops:
  1.6 11.2 %collective-permute-start.1 = (bf16[4,48,384]{2,1,0:T(8,128)(2,1)S(1)}, bf16[4,48,384]{2,1,0:T(8,128)(2,1)S(1)}, u32[]{:S(2)}, u32[]{:S(2)}) collective-permute-start(bf16[4,48,384]{2,1,0:T(8,128)(2,1)S(1)} %pad_maximum_fusion.1.refs_0_), channel_id=1, source_target_pairs={{0,16},{2,18},{4,20},{6,22},{8,24},{10,26},{12,28},{14,30},{16,0},... | collective-permute-start | bytes 442376 | tf_op jit(solution)/shard_map/ppermute | solution.py:30
  21.6 16.0 %collective-permute-start.22 = (bf16[2,48,1536]{2,1,0:T(8,128)(2,1)S(1)}, bf16[2,48,1536]{2,1,0:T(8,128)(2,1)S(1)}, u32[]{:S(2)}, u32[]{:S(2)}) collective-permute-start(bf16[2,48,1536]{2,1,0:T(8,128)(2,1)S(1)} %pad_maximum_fusion.refs_0_), channel_id=1, source_target_pairs={{0,16},{2,18},{4,20},{6,22},{8,24},{10,26},{12,28},{14,30},{16,0},... | collective-permute-start | bytes 884744 | tf_op jit(solution)/shard_map/ppermute | solution.py:30
  24.7 18.1 %collective-permute-start.7 = (bf16[2,48,1536]{2,1,0:T(8,128)(2,1)S(1)}, bf16[2,48,1536]{2,1,0:T(8,128)(2,1)S(1)}, u32[]{:S(2)}, u32[]{:S(2)}) collective-permute-start(bf16[2,48,1536]{2,1,0:T(8,128)(2,1)S(1)} %pad_maximum_fusion.refs_0_), channel_id=1, source_target_pairs={{0,8},{2,10},{4,12},{6,14},{8,0},{10,2},{12,4},{14,6},{16,24},{18,... | collective-permute-start | bytes 884744 | tf_op jit(solution)/shard_map/ppermute | solution.py:30
  26.3 11.4 %collective-permute-start.19 = (bf16[4,48,384]{2,1,0:T(8,128)(2,1)S(1)}, bf16[4,48,384]{2,1,0:T(8,128)(2,1)S(1)}, u32[]{:S(2)}, u32[]{:S(2)}) collective-permute-start(bf16[4,48,384]{2,1,0:T(8,128)(2,1)S(1)} %collective-permute-done.4.refs_14_), channel_id=1, source_target_pairs={{0,2},{2,0},{4,6},{6,4},{8,10},{10,8},{12,14},{14,12},{16,18},{18,... | collective-permute-start | bytes 442376 | tf_op jit(solution)/shard_map/ppermute | solution.py:30
  26.8 17.5 %collective-permute-start = (bf16[2,48,1536]{2,1,0:T(8,128)(2,1)S(1)}, bf16[2,48,1536]{2,1,0:T(8,128)(2,1)S(1)}, u32[]{:S(2)}, u32[]{:S(2)}) collective-permute-start(bf16[2,48,1536]{2,1,0:T(8,128)(2,1)S(1)} %pad_maximum_fusion.refs_0_), channel_id=1, source_target_pairs={{0,2},{2,0},{4,6},{6,4},{8,10},{10,8},{12,14},{14,12},{16,18},{18,... | collective-permute-start | bytes 884744 | tf_op jit(solution)/shard_map/ppermute | solution.py:30
  27.7 17.5 %collective-permute-start.5 = (bf16[2,48,1536]{2,1,0:T(8,128)(2,1)S(1)}, bf16[2,48,1536]{2,1,0:T(8,128)(2,1)S(1)}, u32[]{:S(2)}, u32[]{:S(2)}) collective-permute-start(bf16[2,48,1536]{2,1,0:T(8,128)(2,1)S(1)} %pad_maximum_fusion.refs_0_), channel_id=1, source_target_pairs={{0,4},{2,6},{4,0},{6,2},{8,12},{10,14},{12,8},{14,10},{16,20},{18,... | collective-permute-start | bytes 884744 | tf_op jit(solution)/shard_map/ppermute | solution.py:30
  44.3 15.0 %collective-permute-start.24 = (bf16[2,48,1536]{2,1,0:T(8,128)(2,1)S(1)}, bf16[2,48,1536]{2,1,0:T(8,128)(2,1)S(1)}, u32[]{:S(2)}, u32[]{:S(2)}) collective-permute-start(bf16[2,48,1536]{2,1,0:T(8,128)(2,1)S(1)} %collective-permute-done.22.refs_8_), channel_id=1, source_target_pairs={{0,4},{2,6},{4,0},{6,2},{8,12},{10,14},{12,8},{14,10},{16,20},{18,... | collective-permute-start | bytes 884744 | tf_op jit(solution)/shard_map/ppermute | solution.py:30
  45.1 14.1 %collective-permute-start.8 = (bf16[2,48,1536]{2,1,0:T(8,128)(2,1)S(1)}, bf16[2,48,1536]{2,1,0:T(8,128)(2,1)S(1)}, u32[]{:S(2)}, u32[]{:S(2)}) collective-permute-start(bf16[2,48,1536]{2,1,0:T(8,128)(2,1)S(1)} %collective-permute-done.7.refs_4_), channel_id=1, source_target_pairs={{0,2},{2,0},{4,6},{6,4},{8,10},{10,8},{12,14},{14,12},{16,18},{18,... | collective-permute-start | bytes 884744 | tf_op jit(solution)/shard_map/ppermute | solution.py:30
  45.2 14.6 %collective-permute-start.6 = (bf16[2,48,1536]{2,1,0:T(8,128)(2,1)S(1)}, bf16[2,48,1536]{2,1,0:T(8,128)(2,1)S(1)}, u32[]{:S(2)}, u32[]{:S(2)}) collective-permute-start(bf16[2,48,1536]{2,1,0:T(8,128)(2,1)S(1)} %collective-permute-done.5.refs_2_), channel_id=1, source_target_pairs={{0,2},{2,0},{4,6},{6,4},{8,10},{10,8},{12,14},{14,12},{16,18},{18,... | collective-permute-start | bytes 884744 | tf_op jit(solution)/shard_map/ppermute | solution.py:30
  52.3 12.7 %collective-permute-start.28 = (bf16[2,48,1536]{2,1,0:T(8,128)(2,1)S(1)}, bf16[2,48,1536]{2,1,0:T(8,128)(2,1)S(1)}, u32[]{:S(2)}, u32[]{:S(2)}) collective-permute-start(bf16[2,48,1536]{2,1,0:T(8,128)(2,1)S(1)} %collective-permute-done.26.refs_12_), channel_id=1, source_target_pairs={{0,4},{2,6},{4,0},{6,2},{8,12},{10,14},{12,8},{14,10},{16,20},{18,... | collective-permute-start | bytes 884744 | tf_op jit(solution)/shard_map/ppermute | solution.py:30
  53.0 14.7 %collective-permute-start.30 = (bf16[384,768]{1,0:T(8,128)(2,1)S(1)}, bf16[384,768]{1,0:T(8,128)(2,1)S(1)}, u32[]{:S(2)}, u32[]{:S(2)}) collective-permute-start(bf16[384,768]{1,0:T(8,128)(2,1)S(1)} %get-tuple-element.86.refs_17_), channel_id=1, source_target_pairs={{0,1},{1,0},{2,3},{3,2},{4,5},{5,4},{6,7},{7,6},{8,9},{9,8},{10,11... | collective-permute-start | bytes 1769480 | tf_op jit(solution)/shard_map/ppermute | solution.py:94
  71.0 14.3 %collective-permute-start.31 = (bf16[384,768]{1,0:T(8,128)(2,1)S(1)}, bf16[384,768]{1,0:T(8,128)(2,1)S(1)}, u32[]{:S(2)}, u32[]{:S(2)}) collective-permute-start(bf16[384,768]{1,0:T(8,128)(2,1)S(1)} %get-tuple-element.89.own_ref), channel_id=1, source_target_pairs={{0,1},{1,0},{2,3},{3,2},{4,5},{5,4},{6,7},{7,6},{8,9},{9,8},{10,11... | collective-permute-start | bytes 1769480 | tf_op jit(solution)/shard_map/ppermute | solution.py:94
  92.8 15.3 %collective-permute-start.32 = (bf16[384,768]{1,0:T(8,128)(2,1)S(1)}, bf16[384,768]{1,0:T(8,128)(2,1)S(1)}, u32[]{:S(2)}, u32[]{:S(2)}) collective-permute-start(bf16[384,768]{1,0:T(8,128)(2,1)S(1)} %get-tuple-element.92.own_ref), channel_id=1, source_target_pairs={{0,1},{1,0},{2,3},{3,2},{4,5},{5,4},{6,7},{7,6},{8,9},{9,8},{10,11... | collective-permute-start | bytes 1769480 | tf_op jit(solution)/shard_map/ppermute | solution.py:94
  94.6 15.1 %collective-permute-start.35 = (bf16[4,48,1536]{2,1,0:T(8,128)(2,1)S(1)}, bf16[4,48,1536]{2,1,0:T(8,128)(2,1)S(1)}, u32[]{:S(2)}, u32[]{:S(2)}) collective-permute-start(bf16[4,48,1536]{2,1,0:T(8,128)(2,1)S(1)} %get-tuple-element.99), channel_id=1, source_target_pairs={{0,8},{2,10},{4,12},{6,14},{8,0},{10,2},{12,4},{14,6},{16,24},{18,... | collective-permute-start | bytes 1769480 | tf_op jit(solution)/shard_map/ppermute | solution.py:30
  96.5 14.8 %collective-permute-start.36 = (bf16[4,48,1536]{2,1,0:T(8,128)(2,1)S(1)}, bf16[4,48,1536]{2,1,0:T(8,128)(2,1)S(1)}, u32[]{:S(2)}, u32[]{:S(2)}) collective-permute-start(bf16[4,48,1536]{2,1,0:T(8,128)(2,1)S(1)} %get-tuple-element.105), channel_id=1, source_target_pairs={{0,4},{2,6},{4,0},{6,2},{8,12},{10,14},{12,8},{14,10},{16,20},{18,... | collective-permute-start | bytes 1769480 | tf_op jit(solution)/shard_map/ppermute | solution.py:30
  121.9 16.1 %collective-permute-start.40 = (bf16[4,4,48,384]{3,2,1,0:T(8,128)(2,1)S(1)}, bf16[4,4,48,384]{3,2,1,0:T(8,128)(2,1)S(1)}, u32[]{:S(2)}, u32[]{:S(2)}) collective-permute-start(bf16[4,4,48,384]{3,2,1,0:T(8,128)(2,1)S(1)} %get-tuple-element.122), channel_id=1, source_target_pairs={{0,4},{2,6},{4,0},{6,2},{8,12},{10,14},{12,8},{14,10},{16,20},{18,... | collective-permute-start | bytes 1769480 | tf_op jit(solution)/shard_map/ppermute | solution.py:30
  122.9 15.0 %collective-permute-start.42 = (bf16[2,48,1536]{2,1,0:T(8,128)(2,1)S(1)}, bf16[2,48,1536]{2,1,0:T(8,128)(2,1)S(1)}, u32[]{:S(2)}, u32[]{:S(2)}) collective-permute-start(bf16[2,48,1536]{2,1,0:T(8,128)(2,1)S(1)} %get-tuple-element.124), channel_id=1, source_target_pairs={{0,8},{2,10},{4,12},{6,14},{8,0},{10,2},{12,4},{14,6},{16,24},{18,... | collective-permute-start | bytes 884744 | tf_op jit(solution)/shard_map/ppermute | solution.py:30
  125.5 27.7 %collective-permute-start.37 = (bf16[384,768]{1,0:T(8,128)(2,1)S(1)}, bf16[384,768]{1,0:T(8,128)(2,1)S(1)}, u32[]{:S(2)}, u32[]{:S(2)}) collective-permute-start(bf16[384,768]{1,0:T(8,128)(2,1)S(1)} %input_grad.1.own_ref), channel_id=1, source_target_pairs={{0,1},{1,0},{2,3},{3,2},{4,5},{5,4},{6,7},{7,6},{8,9},{9,8},{10,11... | collective-permute-start | bytes 1769480 | tf_op jit(solution)/shard_map/ppermute | solution.py:94
  128.4 21.2 %collective-permute-start.48 = (bf16[2,48,1536]{2,1,0:T(8,128)(2,1)S(1)}, bf16[2,48,1536]{2,1,0:T(8,128)(2,1)S(1)}, u32[]{:S(2)}, u32[]{:S(2)}) collective-permute-start(bf16[2,48,1536]{2,1,0:T(8,128)(2,1)S(1)} %get-tuple-element.136), channel_id=1, source_target_pairs={{0,16},{2,18},{4,20},{6,22},{8,24},{10,26},{12,28},{14,30},{16,0},... | collective-permute-start | bytes 884744 | tf_op jit(solution)/shard_map/ppermute | solution.py:30
  138.1 16.2 %collective-permute-start.43 = (bf16[2,4,48,384]{3,2,1,0:T(8,128)(2,1)S(1)}, bf16[2,4,48,384]{3,2,1,0:T(8,128)(2,1)S(1)}, u32[]{:S(2)}, u32[]{:S(2)}) collective-permute-start(bf16[2,4,48,384]{3,2,1,0:T(8,128)(2,1)S(1)} %get-tuple-element.127), channel_id=1, source_target_pairs={{0,8},{2,10},{4,12},{6,14},{8,0},{10,2},{12,4},{14,6},{16,24},{18,... | collective-permute-start | bytes 884744 | tf_op jit(solution)/shard_map/ppermute | solution.py:30
  149.7 18.5 %collective-permute-start.49 = (bf16[1,48,1536]{2,1,0:T(8,128)(2,1)S(1)}, bf16[1,48,1536]{2,1,0:T(8,128)(2,1)S(1)}, u32[]{:S(2)}, u32[]{:S(2)}) collective-permute-start(bf16[1,48,1536]{2,1,0:T(8,128)(2,1)S(1)} %get-tuple-element.138), channel_id=1, source_target_pairs={{0,4},{2,6},{4,0},{6,2},{8,12},{10,14},{12,8},{14,10},{16,20},{18,... | collective-permute-start | bytes 442376 | tf_op jit(solution)/shard_map/ppermute | solution.py:30
  150.5 18.4 %collective-permute-start.47 = (bf16[1,48,1536]{2,1,0:T(8,128)(2,1)S(1)}, bf16[1,48,1536]{2,1,0:T(8,128)(2,1)S(1)}, u32[]{:S(2)}, u32[]{:S(2)}) collective-permute-start(bf16[1,48,1536]{2,1,0:T(8,128)(2,1)S(1)} %get-tuple-element.133), channel_id=1, source_target_pairs={{0,16},{2,18},{4,20},{6,22},{8,24},{10,26},{12,28},{14,30},{16,0},... | collective-permute-start | bytes 442376 | tf_op jit(solution)/shard_map/ppermute | solution.py:30
  154.3 15.4 %collective-permute-start.45 = (bf16[1,4,48,384]{3,2,1,0:T(8,128)(2,1)S(1)}, bf16[1,4,48,384]{3,2,1,0:T(8,128)(2,1)S(1)}, u32[]{:S(2)}, u32[]{:S(2)}) collective-permute-start(bf16[1,4,48,384]{3,2,1,0:T(8,128)(2,1)S(1)} %get-tuple-element.130), channel_id=1, source_target_pairs={{0,16},{2,18},{4,20},{6,22},{8,24},{10,26},{12,28},{14,30},{16,0},... | collective-permute-start | bytes 442376 | tf_op jit(solution)/shard_map/ppermute | solution.py:30
  154.8 12.7 %collective-permute-start.46 = (f32[56,128]{1,0:T(8,128)S(1)}, f32[56,128]{1,0:T(8,128)S(1)}, u32[]{:S(2)}, u32[]{:S(2)}) collective-permute-start(f32[56,128]{1,0:T(8,128)S(1)} %add.14), channel_id=1, source_target_pairs={{0,16},{2,18},{4,20},{6,22},{8,24},{10,26},{12,28},{14,30},{16,0},... | collective-permute-start | bytes 86024 | tf_op jit(solution)/shard_map/ppermute | solution.py:30
  (38 other events, 464.7 us)

commit v4 on v3

v4 whole, which is shorter than its diff:
```python
import functools

import jax
import jax.numpy as jnp
from jax import lax
from jax.experimental import pallas as pl
from jax.experimental.pallas import tpu as pltpu
from jax.sharding import PartitionSpec as P

HEAD = 64
CLUSTER = 128
PAIR = 128
NORM_EPS = 1e-05
EXCLUDED = -1e30
VMEM_BYTES = 24 * 1024 * 1024
CUTS = {"y4": 96}

HOPS = {o: (o, o & 12, 2) if o & 2 else (o, 0, o) for o in range(2, 16, 2)}
HOPS.update({o + 1: (o + 1, o, 1) for o in range(0, 16, 2)})
FAR = {"m": 8, "f": 8}
ORDER_BEFORE = (
    "m12", "m6", "m10", "m1", "m3", "m5", "m9", "f8", "f4", "m14", "m7", "f5",
    "m11", "m13", "m15", "f2",
)
ORDER_AFTER = (
    "f12", "f6", "f10", "f1", "f3", "f9", "f14", "f7", "f11", "f13", "f15",
)
SHRINK_STEPS = ((1, 4, 8, 2), (0, 0, 0, 0))
EXPAND_STEPS = ((1, 2, 4, 8), (0, 0, 0, 0))
MIXER_STEPS = ((1, 2, 4, 8), (0, 1, 1, 0))
ORDER_TAIL = (
    "x", "sf", "s", "ef", "e", "xf", "ef", "x", "input", "sf", "s", "e",
    "xf", "x", "s_end", "e_end", "xf", "x",
)
WAITS = {
    "back": ("e2", "s4",),
    "e": ("m15",),
    "e2": ("e",),
    "e8": ("x2b",),
    "f10": ("attention",),
    "f12": ("attention",),
    "f7": ("f12",),
    "f9": ("attention",),
    "m9": ("m8",),
    "x4a": ("x_to_4",),
    "x4b": ("e8",),
    "x_to_2": ("s4", "e2",),
    "y21": ("feed0",),
}

F32 = jnp.float32
BF16 = jnp.bfloat16

NN = (((1,), (0,)), ((), ()))
NT = (((1,), (1,)), ((), ()))
TN = (((0,), (0,)), ((), ()))


def dot(a, b, dims=NN):
    return lax.dot_general(a, b, dims, preferred_element_type=F32)


def swap(array, axis, offset, size):
    return lax.ppermute(array, axis, [(i, i ^ offset) for i in range(size)])


def after(array, *earlier):
    return lax.optimization_barrier((array, *earlier))[0]


class Plan:
    def __init__(self):
        self.made = {}

    def hold(self, name, array):
        gates = [self.made[g] for g in WAITS.get(name, ()) if g in self.made]
        return after(array, *gates) if gates else array

    def note(self, name, array):
        self.made[name] = array
        return array

    def swap(self, name, array, offset):
        return self.note(name, swap(self.hold(name, array), "dp", offset, 16))

    def other(self, name, array, part=None):
        cut = CUTS.get(name, 0)
        if not cut:
            return self.note(name, other_half(self.hold(name, array))) if part != 1 else None
        rows = array[:cut] if part == 0 else array[cut:]
        name = name + "ab"[part]
        return self.note(name, other_half(self.hold(name, rows)))


def offsets_of(steps):
    offsets = [0]
    for step in reversed(steps):
        offsets = offsets + [o ^ step for o in offsets]
    return offsets


def hop(key):
    o, source, step = HOPS[int(key[1:])]
    if o == 12 and FAR[key[0]]:
        source, step = FAR[key[0]], 12 ^ FAR[key[0]]
    return o, source, step


class Reduction:
    def __init__(self, plan, name, kept, sends, steps, split, rider=None):
        self.plan, self.name, self.kept, self.sends = plan, name, kept, sends
        self.steps, self.split, self.rider = list(steps), list(split), rider
        self.arrived = []
        self.count = 8

    def send(self):
        step = self.steps.pop(0)
        count, got = self.count, []
        pieces = len(self.sends)
        for i, array in enumerate(self.sends):
            name = f"{self.name}{step}" + ("ab"[i] if pieces > 1 else "")
            got.append(self.plan.swap(name, array, step))
        if pieces > 1:
            half = count // 2
            self.arrived.append((half, half, got[0], self.rider is not None))
            self.arrived.append((0, half, got[1], False))
        else:
            self.arrived.append((0, count, got[0], self.rider is not None))
        self.step = step
        self.count = count // 2

    def forward(self):
        count = self.count
        split = self.split.pop(0) and count > 1
        ranges = [(count + count // 2, count // 2), (count, count // 2)] if split else [(count, count)]
        needed = [a for a in self.arrived if a[0] + a[1] > count]
        name = f"{self.name}_to_{self.steps[0]}"
        self.sends = self.total(name, ranges, needed)

    def total(self, name, ranges, needed):
        mats = 1 if self.rider is None else 4
        block = self.kept.shape[1:]
        outs = []
        for i, (_, blocks) in enumerate(ranges):
            extra = 1 if self.rider is not None and i == 0 else 0
            outs.append(((blocks * mats + extra, *block), BF16))
        ins = [self.kept, *(a[2] for a in needed)]
        if self.rider is not None:
            outs.append((self.rider.shape, F32))
            ins.append(self.rider)
        ins[1] = self.plan.hold(name, ins[1])
        body = functools.partial(forward_kernel, mats, tuple(ranges), tuple((a[0], a[1], a[3]) for a in needed))
        result = list(call(body, outs, ins, name))
        self.plan.note(name, result[0])
        for i, a in enumerate(self.arrived):
            self.arrived[i] = (a[0], a[1], a[2], False)
        if self.rider is not None:
            self.rider = result.pop()
        return result

    def finish(self, body, outs):
        name = f"{self.name}_end"
        ins = [self.kept, *(a[2] for a in self.arrived)]
        if self.rider is not None:
            ins.append(self.rider)
        ins[1] = self.plan.hold(name, ins[1])
        mats = 1 if self.rider is None else 4
        body = functools.partial(body, mats, tuple((a[0], a[1], a[3]) for a in self.arrived))
        result = call(body, outs, ins, name)
        self.plan.note(name, result[0])
        return result


def ride(vector):
    high = vector.astype(BF16)
    low = (vector - high.astype(F32)).astype(BF16)
    return jnp.concatenate([high, low]), high.astype(F32) + low.astype(F32)


def unride(block):
    half = block.shape[0] // 2
    return block[:half].astype(F32) + block[half:].astype(F32)


def sum_blocks(mats, first, count, kept, gots, places):
    total = kept[first * mats : (first + count) * mats].astype(F32)
    for ref, (start, blocks, _) in zip(gots, places):
        low, high = max(start, first), min(start + blocks, first + count)
        if low < high:
            part = ref[(low - start) * mats : (high - start) * mats].astype(F32)
            pieces = [total[: (low - first) * mats]] if low > first else []
            pieces.append(total[(low - first) * mats : (high - first) * mats] + part)
            if high < first + count:
                pieces.append(total[(high - first) * mats :])
            total = jnp.concatenate(pieces) if len(pieces) > 1 else pieces[0]
    return total


def next_vector(mats, gots, places, rider_ref):
    vector = rider_ref[...]
    for ref, (_, blocks, rides) in zip(gots, places):
        if rides:
            vector = vector + unride(ref[blocks * mats])
    return vector


def forward_kernel(mats, ranges, places, kept, *refs):
    gots, refs = refs[: len(places)], refs[len(places) :]
    if mats > 1:
        rider_ref, outs, rider_out = refs[0], refs[1:-1], refs[-1]
        coded, rider_out[...] = ride(next_vector(mats, gots, places, rider_ref))
        outs[0][ranges[0][1] * mats] = coded
    else:
        outs = refs
    for out, (first, count) in zip(outs, ranges):
        out[: count * mats] = sum_blocks(mats, first, count, kept, gots, places).astype(BF16)


def last_kernel(mats, places, kept, *refs):
    gots, out_ref = refs[:-1], refs[-1]
    out_ref[...] = sum_blocks(mats, 0, 1, kept, gots, places)[0]


def last_mixer_kernel(order, shapes, mats, places, kept, *refs):
    gots, rider_ref, outs = refs[: len(places)], refs[len(places)], refs[len(places) + 1 :]
    total = sum_blocks(mats, 0, 1, kept, gots, places)
    outs[0][...] = total[:-1]
    outs[1][...] = total[-1]
    vector = next_vector(mats, gots, places, rider_ref)
    unpack(order, shapes, vector, outs[2:])


def rows_of(shapes, wide):
    places = []
    for i, (height, width) in enumerate(shapes):
        places += [(i, r, slice(c, c + wide)) for r in range(height) for c in range(0, width, wide)]
    return places


def pack(refs, out_ref):
    wide = out_ref.shape[1]
    out_ref[...] = jnp.zeros(out_ref.shape, F32)
    for k, (i, r, columns) in enumerate(rows_of([ref.shape for ref in refs], wide)):
        out_ref[k : k + 1, :] = refs[i][r : r + 1, columns]


def unpack(order, shapes, vector, outs):
    wide = vector.shape[1]
    for k, (i, r, columns) in enumerate(rows_of(shapes, wide)):
        out, row = order[i][r]
        part = vector[k : k + 1, :]
        if outs[out].shape[1] == PAIR:
            for j in range(wide // PAIR):
                at = columns.start // PAIR + j
                outs[out][at : at + 1, :] = part[:, j * PAIR : (j + 1) * PAIR]
        else:
            outs[out][row : row + 1, columns] = part


def pack_kernel(*refs):
    pack(refs[:-1], refs[-1])


def unpack_kernel(order, shapes, in_ref, *outs):
    unpack(order, shapes, in_ref[...], outs)


def other_half(array):
    return lax.ppermute(array, "tensor", [(0, 1), (1, 0)])


def call(body, outs, ins, name, scratch=()):
    kinds = [o[2] if len(o) > 2 else "vmem" for o in outs]
    make = {"vmem": pltpu.VMEM, "hbm": pltpu.HBM, "free": jax.ShapeDtypeStruct}
    in_specs, values = [], []
    for x in ins:
        away = isinstance(x, Away)
        in_specs.append(pl.BlockSpec(memory_space=pl.ANY if away else pltpu.VMEM))
        values.append(pltpu.with_memory_space_constraint(x.array, pltpu.HBM) if away else x)
    return pl.pallas_call(
        body,
        out_shape=tuple(make[k](o[0], o[1]) for o, k in zip(outs, kinds)),
        in_specs=in_specs,
        out_specs=tuple(
            pl.BlockSpec(memory_space=pl.ANY if k == "hbm" else pltpu.VMEM) for k in kinds
        ),
        scratch_shapes=list(scratch),
        compiler_params=pltpu.CompilerParams(vmem_limit_bytes=VMEM_BYTES),
        name=name,
    )(*values)


class Away:
    def __init__(self, array):
        self.array = array


def assemble(pieces, whole):
    count = len(pieces)
    me = lax.axis_index("dp") if count > 1 else 0
    for o, piece in enumerate(pieces):
        rows = piece.shape[-2]
        start = pl.multiple_of((me ^ o) * rows, 16) if count > 1 else 0
        if len(piece.shape) == 3:
            whole[:, pl.ds(start, rows), :] = piece[...]
        else:
            whole[pl.ds(start, rows), :] = piece[...]


def norm_rows(v):
    center = jnp.mean(v, axis=-1, keepdims=True)
    offset = v - center
    spread = jnp.mean(offset * offset, axis=-1, keepdims=True)
    scale = lax.rsqrt(spread + NORM_EPS)
    return offset * scale, scale


def norm_back(e, n, scale, gain):
    ea = e * gain
    return scale * (
        ea
        - jnp.mean(ea, axis=-1, keepdims=True)
        - n * jnp.mean(ea * n, axis=-1, keepdims=True)
    )


def bundle_kernel(project_ref, output_ref, out_ref, sems):
    one = pltpu.make_async_copy(project_ref, out_ref.at[pl.ds(0, 3)], sems.at[0])
    two = pltpu.make_async_copy(output_ref, out_ref.at[3], sems.at[1])
    one.start()
    two.start()
    one.wait()
    two.wait()


def prepare_kernel(heads, docs, lengths_ref, perm_ref, expand_ref, shrink_ref, bias_ref, feed_ref, sems):
    one = pltpu.make_async_copy(expand_ref, feed_ref.at[0], sems.at[0])
    two = pltpu.make_async_copy(shrink_ref, feed_ref.at[1], sems.at[1])
    one.start()
    two.start()
    rows = bias_ref.shape[1]
    spot = lax.broadcasted_iota(jnp.int32, (rows, PAIR), 0)
    lane = lax.broadcasted_iota(jnp.int32, (rows, PAIR), 1)
    doc = jnp.zeros((rows, PAIR), jnp.int32)
    bound = jnp.int32(0)
    for k in range(docs):
        bound = bound + lengths_ref[0, k]
        doc = doc + (spot >= bound).astype(jnp.int32)
    doc_hot = (lane == doc + PAIR // 2).astype(F32)
    cluster_hot = (lane == spot // CLUSTER).astype(BF16)
    place = lax.broadcasted_iota(jnp.int32, (rows, rows), 0)
    for h in range(heads):
        here = (place == perm_ref[h]).astype(BF16)
        key = (dot(here, cluster_hot) + doc_hot).astype(BF16)
        same = dot(key, key, NT)
        bias_ref[h] = jnp.where(same > 1.5, 0.0, EXCLUDED).astype(BF16)
    one.wait()
    two.wait()


def apart(pair):
    lane = lax.broadcasted_iota(jnp.int32, pair.shape, 1)
    zeros = jnp.zeros_like(pair)
    return jnp.concatenate([jnp.where(lane < HEAD, pair, zeros), jnp.where(lane < HEAD, zeros, pair)])


def attention_kernel(count, heads, scale, *refs):
    pieces, refs = refs[:count], refs[count:]
    (tokens_in, bias_in, admit_ref, qkv_out, prob_out, attended_ref, out_ref, whole,
     qkv_ref, prob_ref, tokens_ref, bias_ref, sems) = refs
    last = sems.shape[0]
    copies = [
        pltpu.make_async_copy(tokens_in, tokens_ref, sems.at[last - 2]),
        pltpu.make_async_copy(bias_in, bias_ref, sems.at[last - 1]),
    ]
    for copy in copies:
        copy.start()
    assemble(pieces, whole)
    for copy in copies:
        copy.wait()
    tokens = tokens_ref[...]
    rows = tokens.shape[0]
    copies = []

    def away(source, target):
        copies.append(pltpu.make_async_copy(source, target, sems.at[len(copies)]))
        copies[-1].start()

    for s in range(3):
        part = dot(tokens, whole[s])
        if s == 0:
            part = part + bias_ref[0:1, :]
        if s == 2:
            part = part + bias_ref[1:2, :]
        qkv_ref[s] = part.astype(BF16)
        away(qkv_ref.at[s], qkv_out.at[s])
    for pair in range(heads // 2):
        columns = slice(pair * PAIR, (pair + 1) * PAIR)
        keys = apart(qkv_ref[1, :, columns])
        scores = dot(keys, qkv_ref[0, :, columns] * scale, NT)
        probs = []
        for side in range(2):
            h = 2 * pair + side
            terms = scores[side * rows : (side + 1) * rows] + admit_ref[h].astype(F32)
            terms = jnp.exp(terms - jnp.max(terms, axis=0, keepdims=True))
            prob = (terms * (1.0 / jnp.sum(terms, axis=0, keepdims=True))).astype(BF16)
            prob_ref[h] = prob
            away(prob_ref.at[h], prob_out.at[h])
            probs.append(prob)
        mixed = dot(apart(qkv_ref[2, :, columns]), jnp.concatenate(probs), TN)
        attended_ref[:, columns] = mixed.T.astype(BF16)
    out_ref[...] = dot(attended_ref[...], whole[3], NT).astype(BF16)
    for copy in copies:
        copy.wait()


def feed_kernel(count, part, gather, *refs):
    if gather:
        pieces, refs = refs[:count], refs[count:]
        whole, refs = refs[-1], refs[:-1]
        assemble(pieces, whole)
    else:
        whole, refs = refs[0], refs[1:]
    (got_ref, tokens_ref, own_ref, out_bias_ref, gain_ref, shift_ref, bias_ref,
     n_ref, scale_ref, low_ref, active_ref, slope_ref, out_ref) = refs
    rows = n_ref.shape[0]
    mine = slice(part * rows, (part + 1) * rows)
    got = got_ref[...] if got_ref.shape[0] == rows else got_ref[mine]
    attention = own_ref[mine].astype(F32) + got.astype(F32) + out_bias_ref[0:1, :]
    n, scale = norm_rows(tokens_ref[mine].astype(F32) + attention)
    n_ref[...] = n
    scale_ref[...] = jnp.broadcast_to(scale, scale_ref.shape)
    low_ref[...] = (n * gain_ref[0:1, :] + shift_ref[0:1, :]).astype(BF16)
    units = whole.shape[2]
    step = 256
    for start in range(0, units, step):
        columns = slice(start, start + step)
        pre = dot(low_ref[...], whole[0, :, columns]) + bias_ref[:, columns]
        half = 0.5 * (1.0 + lax.erf(pre * (2.0**-0.5)))
        active_ref[:, columns] = (pre * half).astype(BF16)
        bell = jnp.exp(-0.5 * pre * pre) * 0.3989422804014327
        slope_ref[:, columns] = (half + pre * bell).astype(BF16)
    out_ref[...] = dot(active_ref[...], whole[1], NT).astype(BF16)


def feed_back_kernel(part, *refs):
    (whole, n_ref, own_ref, got_ref, out_bias_ref, gain_ref, shift_ref, seed_ref, masked_ref, slope_ref,
     *refs) = refs
    if part:
        layer_first, sums_first, inner_first, *refs = refs
    layer_ref, two_ref, low_ref, inner_ref, first_ref, sums_ref, inner_sum_ref = refs
    rows = n_ref.shape[0]
    mine = slice(part * rows, (part + 1) * rows)
    first = n_ref[...] * gain_ref[0:1, :] + shift_ref[0:1, :]
    feed = own_ref[...].astype(F32) + got_ref[...].astype(F32) + out_bias_ref[1:2, :]
    n, scale = norm_rows(first + feed)
    gain = gain_ref[1:2, :]
    layer = (n * gain + shift_ref[1:2, :]).astype(BF16)
    if part:
        layer_ref[:rows] = layer_first[...]
        layer_ref[mine] = layer
    else:
        layer_ref[...] = layer
    e = seed_ref[mine].astype(F32) * masked_ref[mine]
    grad = norm_back(e, n, scale, gain)
    two_ref[...] = grad
    low_ref[...] = grad.astype(BF16)
    for row, values in enumerate((e * n, e, grad)):
        total = jnp.sum(values, axis=0, keepdims=True)
        sums_ref[row : row + 1, :] = total + sums_first[row : row + 1, :] if part else total
    units = whole.shape[2]
    step = 256
    for start in range(0, units, step):
        columns = slice(start, start + step)
        slope = slope_ref[:, columns].astype(F32)
        inner = (dot(low_ref[...], whole[1, :, columns]) * slope).astype(BF16)
        inner_ref[:, columns] = inner
        total = jnp.sum(inner.astype(F32), axis=0, keepdims=True)
        inner_sum_ref[:, columns] = total + inner_first[:, columns] if part else total
    first_ref[...] = dot(inner_ref[...], whole[0], NT).astype(BF16)


def hand_out(offsets, rows, whole, kept_ref, sends, mats=1, mat=0):
    me = lax.axis_index("dp")
    per = 8 // len(sends)
    for k, offset in enumerate(offsets):
        start = pl.multiple_of((me ^ offset) * rows, 16)
        block = whole[pl.ds(start, rows), :]
        if k < 8:
            kept_ref[k * mats + mat] = block
        else:
            part = len(sends) - 1 - (k - 8) // per
            sends[part][(k - 8) % per * mats + mat] = block


def weight_grad_kernel(offsets, left_a, left_b, right_a, right_b, kept_ref, *refs):
    sends, whole = refs[:-1], refs[-1]
    left = jnp.concatenate([left_a[...], left_b[...]])
    right = jnp.concatenate([right_a[...], right_b[...]])
    whole[...] = dot(left, right, TN).astype(BF16)
    hand_out(offsets, kept_ref.shape[1], whole, kept_ref, sends)


def norm_one_back(halves, gain_ref, one_ref, low_ref, sums_ref):
    totals = []
    for part, (own_ref, got_ref, two_ref, n_ref, scale_ref) in enumerate(halves):
        rows = own_ref.shape[0]
        mine = slice(part * rows, (part + 1) * rows)
        e = own_ref[...].astype(F32) + got_ref[...].astype(F32) + two_ref[...]
        n = n_ref[...]
        grad = norm_back(e, n, scale_ref[:, 0:1], gain_ref[0:1, :])
        one_ref[mine] = grad
        low_ref[mine] = grad.astype(BF16)
        totals.append([jnp.sum(values, axis=0, keepdims=True) for values in (e * n, e, grad)])
    for row in range(3):
        sums_ref[row : row + 1, :] = totals[0][row] + totals[1][row]


def attention_back_kernel(heads, scale, *refs):
    halves, refs = (refs[:5], refs[5:10]), refs[10:]
    (gain_ref, whole_ref, qkv_in, prob_in, one_ref, low_ref, norm_sums_ref, grads_ref, sums_ref,
     given, qkv_ref, prob_ref, sems) = refs
    copies = [pltpu.make_async_copy(qkv_in, qkv_ref, sems.at[heads])]
    for h in range(heads):
        copies.append(pltpu.make_async_copy(prob_in.at[h], prob_ref.at[h], sems.at[h]))
    for copy in copies:
        copy.start()
    norm_one_back(halves, gain_ref, one_ref, low_ref, norm_sums_ref)
    given[...] = dot(low_ref[...], whole_ref[3]).astype(BF16)
    rows = given.shape[0]
    lane = lax.broadcasted_iota(jnp.int32, (rows, PAIR), 1)
    copies[0].wait()
    for pair in range(heads // 2):
        columns = slice(pair * PAIR, (pair + 1) * PAIR)
        q = qkv_ref[0, :, columns]
        d = given[:, columns]
        keys = apart(qkv_ref[1, :, columns])
        d_probs = dot(apart(qkv_ref[2, :, columns]), d, NT)
        probs, scores = [], []
        for side in range(2):
            copies[1 + 2 * pair + side].wait()
            prob = prob_ref[2 * pair + side]
            wide = prob.astype(F32)
            d_prob = d_probs[side * rows : (side + 1) * rows]
            center = jnp.sum(d_prob * wide, axis=0, keepdims=True)
            probs.append(prob)
            scores.append((wide * (d_prob - center)).astype(BF16))
        score = jnp.concatenate(scores)
        d_keys = dot(score, q)
        d_values = dot(jnp.concatenate(probs), d)
        d_queries = dot(keys, score, TN).T
        for s, both in enumerate(
            (
                d_queries * scale,
                jnp.where(lane < HEAD, d_keys[:rows], d_keys[rows:]) * scale,
                jnp.where(lane < HEAD, d_values[:rows], d_values[rows:]),
            )
        ):
            both = both.astype(BF16)
            grads_ref[s, :, columns] = both
            if s != 1:
                sums_ref[s // 2 : s // 2 + 1, columns] = jnp.sum(both.astype(F32), axis=0, keepdims=True)


def input_grad_kernel(whole_ref, grads_ref, out_ref):
    total = dot(grads_ref[0], whole_ref[0], NT)
    total = total + dot(grads_ref[1], whole_ref[1], NT)
    total = total + dot(grads_ref[2], whole_ref[2], NT)
    out_ref[...] = total.astype(BF16)


def mixer_grad_kernel(offsets, vectors, tokens_ref, grads_ref, low_ref, attended_ref, *refs):
    vector_refs, (kept_ref, *sends, rider_ref, whole, packed) = refs[:vectors], refs[vectors:]
    pack(vector_refs, packed)
    coded, rider_ref[...] = ride(packed[...])
    sends[0][8 // len(sends) * 4] = coded
    for mat in range(4):
        if mat < 3:
            whole[...] = dot(tokens_ref[...], grads_ref[mat], TN).astype(BF16)
        else:
            whole[...] = dot(low_ref[...], attended_ref[...], TN).astype(BF16)
        hand_out(offsets, kept_ref.shape[1], whole, kept_ref, sends, 4, mat)


def add_kernel(cuts, *refs):
    gots, (own_ref, rest_ref, out_ref) = refs[:cuts], refs[cuts:]
    out_ref[...] = own_ref[...].astype(F32) + joined(gots) + rest_ref[...]


def joined(refs):
    parts = [ref[...].astype(F32) for ref in refs]
    return jnp.concatenate(parts) if len(parts) > 1 else parts[0]


def plain_grad_kernel(left_ref, right_ref, out_ref):
    out_ref[...] = dot(left_ref[...], right_ref[...], TN)


def shards(
    dp,
    tokens,
    project_weight,
    project_bias,
    output_weight,
    output_bias,
    expand_weight,
    expand_bias,
    shrink_weight,
    norm_gain,
    norm_shift,
    doc_lengths,
    cluster_perm,
    masked,
    out_grad,
):
    rows, width = tokens.shape
    piece_rows, _, columns = project_weight.shape
    units = expand_weight.shape[1]
    heads = columns // HEAD
    scale = HEAD**-0.5
    in_pieces = dp == 16 and piece_rows % 16 == 0 and piece_rows == 48 and columns == 384
    plan = Plan()
    note, hold = plan.note, plan.hold

    def whole(*shape):
        return pltpu.VMEM(shape, BF16)

    def sems(count):
        return pltpu.SemaphoreType.DMA((count,))

    (mixer_shard,) = call(
        bundle_kernel,
        [((4, piece_rows, columns), BF16)],
        [Away(project_weight.transpose(1, 0, 2)), Away(output_weight.T)],
        "bundle",
        scratch=[sems(2)],
    )
    m = {0: mixer_shard}
    if in_pieces:
        for o, source, step in ((8, 0, 8), (2, 0, 2), (4, 0, 4)):
            m[o] = plan.swap(f"m{o}", m[source], step)
    admit, feed_shard = call(
        functools.partial(prepare_kernel, heads, doc_lengths.shape[1]),
        [((heads, rows, rows), BF16), ((2, piece_rows, units), BF16)],
        [hold("prepare", doc_lengths), cluster_perm.transpose(1, 0, 2), Away(expand_weight), Away(shrink_weight.T)],
        "prepare",
        scratch=[sems(2)],
    )
    note("prepare", admit)
    f = {0: feed_shard}
    if in_pieces:
        for key in ORDER_BEFORE:
            pieces = m if key[0] == "m" else f
            o, source, step = hop(key)
            pieces[o] = plan.swap(key, pieces[source], step)
        mixer_all = [m[o] for o in range(dp)]
    else:
        mixer_all = [lax.all_gather(mixer_shard, "dp", axis=1, tiled=True)]
        feed_all = [lax.all_gather(feed_shard, "dp", axis=1, tiled=True)]
    count = len(mixer_all)

    qkv, prob, attended, attention_own, mixer = call(
        functools.partial(attention_kernel, count, heads, scale),
        [
            ((3, rows, columns), BF16, "hbm"),
            ((heads, rows, rows), BF16, "hbm"),
            ((rows, columns), BF16),
            ((rows, width), BF16),
            ((4, width, columns), BF16),
        ],
        [*mixer_all, Away(tokens), Away(project_bias), hold("attention", admit)],
        "attention",
        scratch=[
            whole(3, rows, columns), whole(heads, rows, rows), whole(rows, width),
            pltpu.VMEM((2, columns), F32), sems(5 + heads),
        ],
    )
    note("attention", mixer)
    attention_got = [plan.other("y1", attention_own, 0)]
    attention_got.append(plan.other("y1", attention_own, 1))
    attention_got = [x for x in attention_got if x is not None]
    if in_pieces:
        for key in ORDER_AFTER:
            o, source, step = hop(key)
            f[o] = plan.swap(key, f[source], step)
        feed_all = [f[o] for o in range(dp)]
    half_rows = rows // 2
    forward, feed = [], None
    for part in range(2):
        got = attention_got[part] if len(attention_got) == 2 else attention_got[0]
        outs = [
            ((half_rows, width), F32),
            ((half_rows, PAIR), F32),
            ((half_rows, width), BF16),
            ((half_rows, units), BF16),
            ((half_rows, units), BF16),
            ((half_rows, width), BF16),
        ]
        bias = hold(f"feed{part}", output_bias)
        weights = [feed] if part else feed_all
        result = call(
            functools.partial(feed_kernel, count, part, not part),
            outs if part else [*outs, ((2, width, units), BF16)],
            [*weights, got, tokens, attention_own, bias, norm_gain, norm_shift, expand_bias[None, :]],
            f"feed_forward_{part}",
        )
        if not part:
            *result, feed = result
        note(f"feed{part}", result[5])
        forward.append((*result, plan.other(f"y2{part}", result[5])))
    back, seed = [], masked.astype(F32)[:, None]
    for part in range(2):
        n_one, scale_one, first_low, active_low, slope, feed_own, feed_got = forward[part]
        result = call(
            functools.partial(feed_back_kernel, part),
            [
                ((rows, width), BF16, "free") if part else ((half_rows, width), BF16),
                ((half_rows, width), F32),
                ((half_rows, width), BF16),
                ((half_rows, units), BF16),
                ((half_rows, width), BF16),
                ((3, width), F32),
                ((1, units), F32),
            ],
            [
                feed, n_one, feed_own, feed_got, hold(f"feed_back{part}", output_bias), norm_gain, norm_shift,
                out_grad, seed, slope, *((back[0][0], *back[0][5:7]) if part else ()),
            ],
            f"feed_backward_{part}",
        )
        note(f"feed_back{part}", result[4])
        back.append((*result, plan.other(f"y3{part}", result[4])))
    layer_out, sums_two, inner_sum = back[1][0], back[1][5], back[1][6]

    def plain_grad(left, right, name):
        (grad,) = call(plain_grad_kernel, [((width, right.shape[1]), F32, "free")], [left, right], name)
        return lax.psum_scatter(grad, "dp", scatter_dimension=0, tiled=True)

    grads_of = (
        ([x[2] for x in back], [x[3] for x in forward]),
        ([x[2] for x in forward], [x[3] for x in back]),
    )

    def weight_grad(left, right, name, steps, split):
        wide = right[0].shape[1]
        parts = 2 if split[0] else 1
        outs = [((8, piece_rows, wide), BF16)] + [((8 // parts, piece_rows, wide), BF16)] * parts
        kept, *sends = call(
            functools.partial(weight_grad_kernel, offsets_of(steps)),
            outs,
            [*left, right[0], hold(name, right[1])],
            name,
            scratch=[whole(width, wide)],
        )
        note(name, kept)
        return Reduction(plan, name, kept, sends, steps, split[1:])

    if in_pieces:
        shrink = weight_grad(*grads_of[0], "s", *SHRINK_STEPS)
        expand = weight_grad(*grads_of[1], "e", *EXPAND_STEPS)
        shrink.send()
        expand.send()
        shrink.forward()
        shrink.send()
        expand.forward()
        expand.send()
    residual_one, attention_low, sums_one, project_low, project_sums = call(
        functools.partial(attention_back_kernel, heads, scale),
        [
            ((rows, width), F32),
            ((rows, width), BF16),
            ((3, width), F32),
            ((3, rows, columns), BF16),
            ((2, columns), F32),
        ],
        [
            *(x for p in range(2) for x in (back[p][4], back[p][7], back[p][1], *forward[p][:2])),
            hold("back", norm_gain), mixer, Away(qkv), Away(prob),
        ],
        "attention_backward",
        scratch=[
            whole(rows, columns), whole(3, rows, columns), whole(heads, rows, rows), sems(heads + 1),
        ],
    )
    note("back", project_low)
    vectors = [sums_one, sums_two, inner_sum, project_sums]
    shapes = [v.shape for v in vectors]
    order = [[(2, 0), (3, 0), (1, 0)], [(2, 1), (3, 1), (1, 1)], [(4, 0)], [(0, 0), (0, 1)]]
    vector_outs = [
        ((2, columns), F32, "free"),
        ((2, width), F32, "free"),
        ((2, width), F32, "free"),
        ((2, width), F32, "free"),
        ((units // PAIR, PAIR), F32, "free"),
    ]

    def input_grad():
        (own,) = call(
            input_grad_kernel,
            [((rows, width), BF16)],
            [mixer, hold("input", project_low)],
            "input_grad",
        )
        note("input", own)
        gots = [plan.other("y4", own, 0)]
        gots.append(plan.other("y4", own, 1))
        gots = [x for x in gots if x is not None]
        (result,) = call(
            functools.partial(add_kernel, len(gots)),
            [((rows, width), F32, "free")],
            [*gots, own, hold("tokens", residual_one)],
            "tokens_grad",
        )
        return note("tokens", result)

    if in_pieces:
        steps, split = MIXER_STEPS
        parts = 2 if split[0] else 1
        half = piece_rows // 2
        kept, *sends, rider = call(
            functools.partial(mixer_grad_kernel, offsets_of(steps), len(vectors)),
            [((32, piece_rows, columns), BF16)]
            + [((8 // parts * 4 + (i == 0), piece_rows, columns), BF16) for i in range(parts)]
            + [((half, columns), F32)],
            [tokens, hold("x", project_low), attention_low, attended, *vectors],
            "mixer_grad",
            scratch=[whole(width, columns), pltpu.VMEM((half, columns), F32)],
        )
        note("x", kept)
        mixed = Reduction(plan, "x", kept, sends, steps, split[1:], rider)
        parts_of = {"s": shrink, "e": expand, "x": mixed}
        block = (piece_rows, units)
        for key in ORDER_TAIL:
            if key == "input":
                tokens_grad = input_grad()
            elif key == "s_end":
                (shrink_part,) = shrink.finish(last_kernel, [(block, F32, "free")])
            elif key == "e_end":
                (expand_part,) = expand.finish(last_kernel, [(block, F32, "free")])
            elif key[1:] == "f":
                parts_of[key[0]].forward()
            else:
                parts_of[key[0]].send()
        project_part, output_part, *totals = mixed.finish(
            functools.partial(last_mixer_kernel, order, shapes),
            [((3, piece_rows, columns), F32, "free"), ((piece_rows, columns), F32, "free"), *vector_outs],
        )
    else:
        tokens_grad = input_grad()
        height = -(-sum(v.size for v in vectors) // PAIR // 8) * 8
        (packed,) = call(pack_kernel, [((height, PAIR), F32)], vectors, "pack")
        totals = call(
            functools.partial(unpack_kernel, order, shapes), vector_outs, [lax.psum(packed, "dp")], "unpack"
        )
        shrink_part, expand_part = (
            plain_grad(jnp.concatenate(left), jnp.concatenate(right), name)
            for (left, right), name in zip(grads_of, ("shrink_grad", "expand_grad"))
        )
        project_part = jnp.stack([plain_grad(tokens, project_low[s], "project_grad") for s in range(3)])
        output_part = plain_grad(attention_low, attended, "output_grad")
    project_total, output_total, gain_total, shift_total, inner_total = totals
    return (
        layer_out,
        tokens_grad,
        project_part.transpose(1, 0, 2),
        project_total,
        output_part.T,
        output_total,
        expand_part,
        inner_total.reshape(units),
        shrink_part.T,
        gain_total,
        shift_total,
    )


def solution(mesh):
    in_specs = (
        P("dp", None),
        P("dp", None, "tensor"),
        P(None, "tensor"),
        P("tensor", "dp"),
        P(),
        P("dp", "tensor"),
        P("tensor"),
        P("tensor", "dp"),
        P(),
        P(),
        P("dp", None),
        P("dp", "tensor", None),
        P("dp"),
        P("dp", None),
    )
    out_specs = (
        P("dp", None),
        P("dp", None),
        P("dp", None, "tensor"),
        P(None, "tensor"),
        P("tensor", "dp"),
        P(),
        P("dp", "tensor"),
        P("tensor"),
        P("tensor", "dp"),
        P(),
        P(),
    )
    body = functools.partial(shards, mesh.shape["dp"])
    return jax.shard_map(body, mesh=mesh, in_specs=in_specs, out_specs=out_specs, check_vma=False)
```

time: 171 us -> 150 us (0.88)
  waiting for transfers between devices: 88.3 us -> 73.2 us
  starting transfers between devices: 47 us -> 41.6 us
    ppermute x4 -> x7, waiting for transfers between devices: 26 us -> 13.7 us  [other_half(): return lax.ppermute(array, 'tensor', [(0, 1), (1, 0)])]
    ppermute x46 -> x44, starting transfers between devices: 40.8 us -> 32.7 us  [swap(): return lax.ppermute(array, axis, [(i, i ^ offset) for i in range(size)])]
    ppermute x46 -> x44, waiting for transfers between devices: 62.3 us -> 59.4 us  [swap(): return lax.ppermute(array, axis, [(i, i ^ offset) for i in range(size)])]
    ppermute x4 -> x7, starting transfers between devices: 6.21 us -> 8.81 us  [other_half(): return lax.ppermute(array, 'tensor', [(0, 1), (1, 0)])]
  transfers between devices with their start and end apart: 50 -> 51, of which waited for: 18 -> 24; matrix products, arithmetic and copies ran while one was open for 0% -> 0% of each run, Pallas kernels for 9% -> 11%
where the time goes in v4:
time: 150 us
  waiting for transfers between devices  73.2 us (49%)
  starting transfers between devices  41.6 us (28%)
  Pallas kernels  32.8 us (22%)
  local copies, waits for them, and re-layouts  1.54 us (1%)
    ppermute x44, waiting for transfers between devices, swap(): return lax.ppermute(array, axis, [(i, i ^ offset) for i in range(size)])  59.4 us
    pallas_call x25, Pallas kernels, call(): pl.pallas_call(body, out_shape=tuple((make[k](o[0], o[1]) for o, k in zip...  32.8 us
    ppermute x44, starting transfers between devices, swap(): return lax.ppermute(array, axis, [(i, i ^ offset) for i in range(size)])  32.7 us
    ppermute x7, waiting for transfers between devices, other_half(): return lax.ppermute(array, 'tensor', [(0, 1), (1, 0)])  13.7 us
    ppermute x7, starting transfers between devices, other_half(): return lax.ppermute(array, 'tensor', [(0, 1), (1, 0)])  8.81 us
  transfers between devices with their start and end apart: 51, of which 24 were waited for; matrix products, arithmetic and copies ran while one was open for 0% of the time, Pallas kernels for 11%

profile of v4, /device:TPU:0, one launch (start us, length us, event | category | flops | bytes accessed | tf_op | source)
XLA Modules:
  0.0 150.0 jit_solution(7959750207450575738)
XLA Ops:
  1.6 4.1 %collective-permute-start.14 = (bf16[4,48,384]{2,1,0:T(8,128)(2,1)S(1)}, bf16[4,48,384]{2,1,0:T(8,128)(2,1)S(1)}, u32[]{:S(2)}, u32[]{:S(2)}) collective-permute-start(bf16[4,48,384]{2,1,0:T(8,128)(2,1)S(1)} %bundle.1.refs_0_), channel_id=1, source_target_pairs={{0,16},{2,18},{4,20},{6,22},{8,24},{10,26},{12,28},{14,30},{16,0},... | collective-permute-start | bytes 442376 | tf_op jit(solution)/shard_map/ppermute | solution.py:64
  10.1 1.9 %prepare.1 = (bf16[6,384,384]{2,1,0:T(8,128)(2,1)S(1)}, bf16[2,48,1536]{2,1,0:T(8,128)(2,1)S(1)}) custom-call(s32[1,4]{1,0:T(1,128)S(1)} %copy-done.6, s32[6,1,384]{2,1,0:T(1,128)S(1)} %bitcast.8, bf16[48,1536]{1,0:T(8,128)(2,1)} %expand_ref.1, bf16[48,1536]{1,0:T(8,128)(2,1)} %bitcast.10), custom_call_target="tpu_custom_call" | custom-call | tf_op jit(solution)/shard_map/prepare/pallas_call | solution.py:280
  16.9 2.7 %collective-permute-done.18.refs_12_ = bf16[4,48,384]{2,1,0:T(8,128)(2,1)S(1)} collective-permute-done((bf16[4,48,384]{2,1,0:T(8,128)(2,1)S(1)}, bf16[4,48,384]{2,1,0:T(8,128)(2,1)S(1)}, u32[]{:S(2)}, u32[]{:S(2)}) %collective-permute-start.18) | collective-permute-done | bytes 147488 | tf_op jit(solution)/shard_map/ppermute | solution.py:64
  23.5 3.4 %collective-permute-start.6 = (bf16[2,48,1536]{2,1,0:T(8,128)(2,1)S(1)}, bf16[2,48,1536]{2,1,0:T(8,128)(2,1)S(1)}, u32[]{:S(2)}, u32[]{:S(2)}) collective-permute-start(bf16[2,48,1536]{2,1,0:T(8,128)(2,1)S(1)} %get-tuple-element.82.refs_0_), channel_id=1, source_target_pairs={{0,16},{2,18},{4,20},{6,22},{8,24},{10,26},{12,28},{14,30},{16,0},... | collective-permute-start | bytes 884744 | tf_op jit(solution)/shard_map/ppermute | solution.py:64
  30.4 5.0 %attention.1 = (bf16[3,384,384]{2,1,0:T(8,128)(2,1)}, bf16[6,384,384]{2,1,0:T(8,128)(2,1)}, bf16[384,384]{1,0:T(8,128)(2,1)S(1)}, bf16[384,768]{1,0:T(8,128)(2,1)S(1)}, bf16[4,768,384]{2,1,0:T(8,128)(2,1)S(1)}) custom-call(bf16[4,48,384]{2,1,0:T(8,128)(2,1)S(1)} %bundle.1.refs_0_, bf16[4,48,384]{2,1,0:T(8,128)(2,1)S(1)} %collective-permute-done.7.refs_1_, ...), custom_call_target="tpu_custom_call" | custom-call | tf_op jit(solution)/shard_map/attention/pallas_call | solution.py:280
  35.5 3.5 %collective-permute-done.6.refs_8_ = bf16[2,48,1536]{2,1,0:T(8,128)(2,1)S(1)} collective-permute-done((bf16[2,48,1536]{2,1,0:T(8,128)(2,1)S(1)}, bf16[2,48,1536]{2,1,0:T(8,128)(2,1)S(1)}, u32[]{:S(2)}, u32[]{:S(2)}) %collective-permute-start.6) | collective-permute-done | bytes 294944 | tf_op jit(solution)/shard_map/ppermute | solution.py:64
  40.0 4.4 %collective-permute-done.5.refs_6_ = bf16[2,48,1536]{2,1,0:T(8,128)(2,1)S(1)} collective-permute-done((bf16[2,48,1536]{2,1,0:T(8,128)(2,1)S(1)}, bf16[2,48,1536]{2,1,0:T(8,128)(2,1)S(1)}, u32[]{:S(2)}, u32[]{:S(2)}) %collective-permute-start.5) | collective-permute-done | bytes 294944 | tf_op jit(solution)/shard_map/ppermute | solution.py:64
  44.5 3.2 %collective-permute-done.22.refs_12_ = bf16[2,48,1536]{2,1,0:T(8,128)(2,1)S(1)} collective-permute-done((bf16[2,48,1536]{2,1,0:T(8,128)(2,1)S(1)}, bf16[2,48,1536]{2,1,0:T(8,128)(2,1)S(1)}, u32[]{:S(2)}, u32[]{:S(2)}) %collective-permute-start.22) | collective-permute-done | bytes 294944 | tf_op jit(solution)/shard_map/ppermute | solution.py:64
  51.2 5.1 %collective-permute-done.28.refs_14_ = bf16[2,48,1536]{2,1,0:T(8,128)(2,1)S(1)} collective-permute-done((bf16[2,48,1536]{2,1,0:T(8,128)(2,1)S(1)}, bf16[2,48,1536]{2,1,0:T(8,128)(2,1)S(1)}, u32[]{:S(2)}, u32[]{:S(2)}) %collective-permute-start.28) | collective-permute-done | bytes 294944 | tf_op jit(solution)/shard_map/ppermute | solution.py:64
  56.4 5.5 %collective-permute-done.30.refs_16_.refs_1_ = bf16[384,768]{1,0:T(8,128)(2,1)S(1)} collective-permute-done((bf16[384,768]{1,0:T(8,128)(2,1)S(1)}, bf16[384,768]{1,0:T(8,128)(2,1)S(1)}, u32[]{:S(2)}, u32[]{:S(2)}) %collective-permute-start.30) | collective-permute-done | bytes 589856 | tf_op jit(solution)/shard_map/ppermute | solution.py:269
  61.9 2.1 %feed_forward_0.1 = (f32[192,768]{1,0:T(8,128)S(1)}, f32[192,128]{1,0:T(8,128)S(1)}, bf16[192,768]{1,0:T(8,128)(2,1)S(1)}, bf16[192,1536]{1,0:T(8,128)(2,1)S(1)}...) custom-call(bf16[2,48,1536]{2,1,0:T(8,128)(2,1)S(1)} %get-tuple-element.82.refs_0_, ...), custom_call_target="tpu_custom_call" | custom-call | tf_op jit(solution)/shard_map/feed_forward_0/pallas_call | solution.py:280
  68.0 6.0 %collective-permute-done.32.refs_3_ = bf16[192,768]{1,0:T(8,128)(2,1)S(1)} collective-permute-done((bf16[192,768]{1,0:T(8,128)(2,1)S(1)}, bf16[192,768]{1,0:T(8,128)(2,1)S(1)}, u32[]{:S(2)}, u32[]{:S(2)}) %collective-permute-start.32) | collective-permute-done | bytes 294944 | tf_op jit(solution)/shard_map/ppermute | solution.py:269
  74.0 2.2 %feed_backward_0.1 = (bf16[192,768]{1,0:T(8,128)(2,1)S(1)}, f32[192,768]{1,0:T(8,128)S(1)}, bf16[192,768]{1,0:T(8,128)(2,1)S(1)}, bf16[192,1536]{1,0:T(8,128)(2,...) custom-call(bf16[2,768,1536]{2,1,0:T(8,128)(2,1)S(1)} %get-tuple-element.89.refs_0_, ...), custom_call_target="tpu_custom_call" | custom-call | tf_op jit(solution)/shard_map/feed_backward_0/pallas_call | solution.py:280
  77.3 2.7 %feed_backward_1.1 = (bf16[384,768]{1,0:T(8,128)(2,1)}, f32[192,768]{1,0:T(8,128)S(1)}, bf16[192,768]{1,0:T(8,128)(2,1)S(1)}, bf16[192,1536]{1,0:T(8,128)(2,1)S(...) custom-call(bf16[2,768,1536]{2,1,0:T(8,128)(2,1)S(1)} %get-tuple-element.89.refs_0_, ...), custom_call_target="tpu_custom_call" | custom-call | tf_op jit(solution)/shard_map/feed_backward_1/pallas_call | solution.py:280
  90.0 10.1 %collective-permute-done.38.refs_1_ = bf16[4,48,1536]{2,1,0:T(8,128)(2,1)S(1)} collective-permute-done((bf16[4,48,1536]{2,1,0:T(8,128)(2,1)S(1)}, bf16[4,48,1536]{2,1,0:T(8,128)(2,1)S(1)}, u32[]{:S(2)}, u32[]{:S(2)}) %collective-permute-start.38) | collective-permute-done | bytes 589856 | tf_op jit(solution)/shard_map/ppermute | solution.py:64
  100.1 2.0 %collective-permute-done.36.refs_1_ = bf16[4,48,1536]{2,1,0:T(8,128)(2,1)S(1)} collective-permute-done((bf16[4,48,1536]{2,1,0:T(8,128)(2,1)S(1)}, bf16[4,48,1536]{2,1,0:T(8,128)(2,1)S(1)}, u32[]{:S(2)}, u32[]{:S(2)}) %collective-permute-start.36) | collective-permute-done | bytes 589856 | tf_op jit(solution)/shard_map/ppermute | solution.py:64
  103.3 5.5 %attention_backward.1 = (f32[384,768]{1,0:T(8,128)S(1)}, bf16[384,768]{1,0:T(8,128)(2,1)S(1)}, f32[3,768]{1,0:T(4,128)S(1)}, bf16[3,384,384]{2,1,0:T(8,128)(2,1)S(1)}, f32[2,384]{1,0:T(2,128)S(1)}) custom-call(bf16[192,768]{1,0:T(8,128)(2,1)S(1)} %get-tuple-element.101.refs_0_, bf16[192,768]{1,0:T(8,128)(2,1)S(1)} %collective-permute-done.33.refs_1_, ...), custom_call_target="tpu_custom_call" | custom-call | tf_op jit(solution)/shard_map/attention_backward/pallas_call | solution.py:280
  110.6 2.9 %collective-permute-done.41.refs_0_ = bf16[33,48,384]{2,1,0:T(8,128)(2,1)S(1)} collective-permute-done((bf16[33,48,384]{2,1,0:T(8,128)(2,1)S(1)}, bf16[33,48,384]{2,1,0:T(8,128)(2,1)S(1)}, u32[]{:S(2)}, u32[]{:S(2)}) %collective-permute-start.41) | collective-permute-done | bytes 1216544 | tf_op jit(solution)/shard_map/ppermute | solution.py:64
  120.6 3.8 %collective-permute-done.42.refs_1_ = bf16[9,48,384]{2,1,0:T(8,128)(2,1)S(1)} collective-permute-done((bf16[9,48,384]{2,1,0:T(8,128)(2,1)S(1)}, bf16[9,48,384]{2,1,0:T(8,128)(2,1)S(1)}, u32[]{:S(2)}, u32[]{:S(2)}) %collective-permute-start.42) | collective-permute-done | bytes 331808 | tf_op jit(solution)/shard_map/ppermute | solution.py:64
  125.5 4.5 %collective-permute-done.45.refs_2_ = bf16[2,48,1536]{2,1,0:T(8,128)(2,1)S(1)} collective-permute-done((bf16[2,48,1536]{2,1,0:T(8,128)(2,1)S(1)}, bf16[2,48,1536]{2,1,0:T(8,128)(2,1)S(1)}, u32[]{:S(2)}, u32[]{:S(2)}) %collective-permute-start.45) | collective-permute-done | bytes 294944 | tf_op jit(solution)/shard_map/ppermute | solution.py:64
  131.6 4.0 %collective-permute-done.44.refs_3_ = bf16[5,48,384]{2,1,0:T(8,128)(2,1)S(1)} collective-permute-done((bf16[5,48,384]{2,1,0:T(8,128)(2,1)S(1)}, bf16[5,48,384]{2,1,0:T(8,128)(2,1)S(1)}, u32[]{:S(2)}, u32[]{:S(2)}) %collective-permute-start.44) | collective-permute-done | bytes 184352 | tf_op jit(solution)/shard_map/ppermute | solution.py:64
  135.7 2.0 %collective-permute-start.48 = (bf16[5,48,384]{2,1,0:T(8,128)(2,1)S(1)}, bf16[5,48,384]{2,1,0:T(8,128)(2,1)S(1)}, u32[]{:S(2)}, u32[]{:S(2)}) collective-permute-start(bf16[5,48,384]{2,1,0:T(8,128)(2,1)S(1)} %get-tuple-element.144), channel_id=1, source_target_pairs={{0,16},{2,18},{4,20},{6,22},{8,24},{10,26},{12,28},{14,30},{16,0},... | collective-permute-start | bytes 552968 | tf_op jit(solution)/shard_map/ppermute | solution.py:64
  139.7 4.4 %collective-permute-done.46.refs_3_ = bf16[1,48,1536]{2,1,0:T(8,128)(2,1)S(1)} collective-permute-done((bf16[1,48,1536]{2,1,0:T(8,128)(2,1)S(1)}, bf16[1,48,1536]{2,1,0:T(8,128)(2,1)S(1)}, u32[]{:S(2)}, u32[]{:S(2)}) %collective-permute-start.46) | collective-permute-done | bytes 147488 | tf_op jit(solution)/shard_map/ppermute | solution.py:64
  146.9 2.3 %collective-permute-done.47.refs_4_ = bf16[4,48,384]{2,1,0:T(8,128)(2,1)S(1)} collective-permute-done((bf16[4,48,384]{2,1,0:T(8,128)(2,1)S(1)}, bf16[4,48,384]{2,1,0:T(8,128)(2,1)S(1)}, u32[]{:S(2)}, u32[]{:S(2)}) %collective-permute-start.47) | collective-permute-done | bytes 147488 | tf_op jit(solution)/shard_map/ppermute | solution.py:64
  (126 shorter events, 55.7 us)
Async XLA Ops:
  1.6 11.2 %collective-permute-start.14 = (bf16[4,48,384]{2,1,0:T(8,128)(2,1)S(1)}, bf16[4,48,384]{2,1,0:T(8,128)(2,1)S(1)}, u32[]{:S(2)}, u32[]{:S(2)}) collective-permute-start(bf16[4,48,384]{2,1,0:T(8,128)(2,1)S(1)} %bundle.1.refs_0_), channel_id=1, source_target_pairs={{0,16},{2,18},{4,20},{6,22},{8,24},{10,26},{12,28},{14,30},{16,0},... | collective-permute-start | bytes 442376 | tf_op jit(solution)/shard_map/ppermute | solution.py:64
  5.7 9.2 %collective-permute-start.10 = (bf16[4,48,384]{2,1,0:T(8,128)(2,1)S(1)}, bf16[4,48,384]{2,1,0:T(8,128)(2,1)S(1)}, u32[]{:S(2)}, u32[]{:S(2)}) collective-permute-start(bf16[4,48,384]{2,1,0:T(8,128)(2,1)S(1)} %bundle.1.refs_0_), channel_id=1, source_target_pairs={{0,8},{2,10},{4,12},{6,14},{8,0},{10,2},{12,4},{14,6},{16,24},{18,... | collective-permute-start | bytes 442376 | tf_op jit(solution)/shard_map/ppermute | solution.py:64
  14.9 12.6 %collective-permute-start.3 = (bf16[2,48,1536]{2,1,0:T(8,128)(2,1)S(1)}, bf16[2,48,1536]{2,1,0:T(8,128)(2,1)S(1)}, u32[]{:S(2)}, u32[]{:S(2)}) collective-permute-start(bf16[2,48,1536]{2,1,0:T(8,128)(2,1)S(1)} %get-tuple-element.82.refs_0_), channel_id=1, source_target_pairs={{0,8},{2,10},{4,12},{6,14},{8,0},{10,2},{12,4},{14,6},{16,24},{18,... | collective-permute-start | bytes 884744 | tf_op jit(solution)/shard_map/ppermute | solution.py:64
  23.5 15.4 %collective-permute-start.6 = (bf16[2,48,1536]{2,1,0:T(8,128)(2,1)S(1)}, bf16[2,48,1536]{2,1,0:T(8,128)(2,1)S(1)}, u32[]{:S(2)}, u32[]{:S(2)}) collective-permute-start(bf16[2,48,1536]{2,1,0:T(8,128)(2,1)S(1)} %get-tuple-element.82.refs_0_), channel_id=1, source_target_pairs={{0,16},{2,18},{4,20},{6,22},{8,24},{10,26},{12,28},{14,30},{16,0},... | collective-permute-start | bytes 884744 | tf_op jit(solution)/shard_map/ppermute | solution.py:64
  28.3 10.7 %collective-permute-start.1 = (bf16[2,48,1536]{2,1,0:T(8,128)(2,1)S(1)}, bf16[2,48,1536]{2,1,0:T(8,128)(2,1)S(1)}, u32[]{:S(2)}, u32[]{:S(2)}) collective-permute-start(bf16[2,48,1536]{2,1,0:T(8,128)(2,1)S(1)} %get-tuple-element.82.refs_0_), channel_id=1, source_target_pairs={{0,4},{2,6},{4,0},{6,2},{8,12},{10,14},{12,8},{14,10},{16,20},{18,... | collective-permute-start | bytes 884744 | tf_op jit(solution)/shard_map/ppermute | solution.py:64
  28.9 10.7 %collective-permute-start = (bf16[2,48,1536]{2,1,0:T(8,128)(2,1)S(1)}, bf16[2,48,1536]{2,1,0:T(8,128)(2,1)S(1)}, u32[]{:S(2)}, u32[]{:S(2)}) collective-permute-start(bf16[2,48,1536]{2,1,0:T(8,128)(2,1)S(1)} %get-tuple-element.82.refs_0_), channel_id=1, source_target_pairs={{0,2},{2,0},{4,6},{6,4},{8,10},{10,8},{12,14},{14,12},{16,18},{18,... | collective-permute-start | bytes 884744 | tf_op jit(solution)/shard_map/ppermute | solution.py:64
  28.9 15.5 %collective-permute-start.5 = (bf16[2,48,1536]{2,1,0:T(8,128)(2,1)S(1)}, bf16[2,48,1536]{2,1,0:T(8,128)(2,1)S(1)}, u32[]{:S(2)}, u32[]{:S(2)}) collective-permute-start(bf16[2,48,1536]{2,1,0:T(8,128)(2,1)S(1)} %collective-permute-done.3.refs_4_), channel_id=1, source_target_pairs={{0,4},{2,6},{4,0},{6,2},{8,12},{10,14},{12,8},{14,10},{16,20},{18,... | collective-permute-start | bytes 884744 | tf_op jit(solution)/shard_map/ppermute | solution.py:64
  39.0 10.2 %collective-permute-start.2 = (bf16[2,48,1536]{2,1,0:T(8,128)(2,1)S(1)}, bf16[2,48,1536]{2,1,0:T(8,128)(2,1)S(1)}, u32[]{:S(2)}, u32[]{:S(2)}) collective-permute-start(bf16[2,48,1536]{2,1,0:T(8,128)(2,1)S(1)} %collective-permute-done.1.refs_2_), channel_id=1, source_target_pairs={{0,2},{2,0},{4,6},{6,4},{8,10},{10,8},{12,14},{14,12},{16,18},{18,... | collective-permute-start | bytes 884744 | tf_op jit(solution)/shard_map/ppermute | solution.py:64
  39.5 11.2 %collective-permute-start.25 = (bf16[2,48,1536]{2,1,0:T(8,128)(2,1)S(1)}, bf16[2,48,1536]{2,1,0:T(8,128)(2,1)S(1)}, u32[]{:S(2)}, u32[]{:S(2)}) collective-permute-start(bf16[2,48,1536]{2,1,0:T(8,128)(2,1)S(1)} %collective-permute-done.6.refs_8_), channel_id=1, source_target_pairs={{0,4},{2,6},{4,0},{6,2},{8,12},{10,14},{12,8},{14,10},{16,20},{18,... | collective-permute-start | bytes 884744 | tf_op jit(solution)/shard_map/ppermute | solution.py:64
  47.7 14.2 %collective-permute-start.30 = (bf16[384,768]{1,0:T(8,128)(2,1)S(1)}, bf16[384,768]{1,0:T(8,128)(2,1)S(1)}, u32[]{:S(2)}, u32[]{:S(2)}) collective-permute-start(bf16[384,768]{1,0:T(8,128)(2,1)S(1)} %get-tuple-element.88.refs_18_.refs_3_), channel_id=1, source_target_pairs={{0,1},{1,0},{2,3},{3,2},{4,5},{5,4},{6,7},{7,6},{8,9},{9,8},{10,11... | collective-permute-start | bytes 1769480 | tf_op jit(solution)/shard_map/ppermute | solution.py:269
  64.0 10.0 %collective-permute-start.32 = (bf16[192,768]{1,0:T(8,128)(2,1)S(1)}, bf16[192,768]{1,0:T(8,128)(2,1)S(1)}, u32[]{:S(2)}, u32[]{:S(2)}) collective-permute-start(bf16[192,768]{1,0:T(8,128)(2,1)S(1)} %get-tuple-element.92.refs_2_), channel_id=1, source_target_pairs={{0,1},{1,0},{2,3},{3,2},{4,5},{5,4},{6,7},{7,6},{8,9},{9,8},{10,11... | collective-permute-start | bytes 884744 | tf_op jit(solution)/shard_map/ppermute | solution.py:269
  67.3 10.0 %collective-permute-start.31 = (bf16[192,768]{1,0:T(8,128)(2,1)S(1)}, bf16[192,768]{1,0:T(8,128)(2,1)S(1)}, u32[]{:S(2)}, u32[]{:S(2)}) collective-permute-start(bf16[192,768]{1,0:T(8,128)(2,1)S(1)} %get-tuple-element.93.refs_2_), channel_id=1, source_target_pairs={{0,1},{1,0},{2,3},{3,2},{4,5},{5,4},{6,7},{7,6},{8,9},{9,8},{10,11... | collective-permute-start | bytes 884744 | tf_op jit(solution)/shard_map/ppermute | solution.py:269
  84.6 15.4 %collective-permute-start.38 = (bf16[4,48,1536]{2,1,0:T(8,128)(2,1)S(1)}, bf16[4,48,1536]{2,1,0:T(8,128)(2,1)S(1)}, u32[]{:S(2)}, u32[]{:S(2)}) collective-permute-start(bf16[4,48,1536]{2,1,0:T(8,128)(2,1)S(1)} %s_to_4.1), channel_id=1, source_target_pairs={{0,8},{2,10},{4,12},{6,14},{8,0},{10,2},{12,4},{14,6},{16,24},{18,... | collective-permute-start | bytes 1769480 | tf_op jit(solution)/shard_map/ppermute | solution.py:64
  86.4 15.7 %collective-permute-start.36 = (bf16[4,48,1536]{2,1,0:T(8,128)(2,1)S(1)}, bf16[4,48,1536]{2,1,0:T(8,128)(2,1)S(1)}, u32[]{:S(2)}, u32[]{:S(2)}) collective-permute-start(bf16[4,48,1536]{2,1,0:T(8,128)(2,1)S(1)} %e_to_2.1), channel_id=1, source_target_pairs={{0,4},{2,6},{4,0},{6,2},{8,12},{10,14},{12,8},{14,10},{16,20},{18,... | collective-permute-start | bytes 1769480 | tf_op jit(solution)/shard_map/ppermute | solution.py:64
  88.0 14.1 %collective-permute-start.34 = (bf16[192,768]{1,0:T(8,128)(2,1)S(1)}, bf16[192,768]{1,0:T(8,128)(2,1)S(1)}, u32[]{:S(2)}, u32[]{:S(2)}) collective-permute-start(bf16[192,768]{1,0:T(8,128)(2,1)S(1)} %get-tuple-element.104.refs_5_), channel_id=1, source_target_pairs={{0,1},{1,0},{2,3},{3,2},{4,5},{5,4},{6,7},{7,6},{8,9},{9,8},{10,11... | collective-permute-start | bytes 884744 | tf_op jit(solution)/shard_map/ppermute | solution.py:269
  89.5 13.8 %collective-permute-start.33 = (bf16[192,768]{1,0:T(8,128)(2,1)S(1)}, bf16[192,768]{1,0:T(8,128)(2,1)S(1)}, u32[]{:S(2)}, u32[]{:S(2)}) collective-permute-start(bf16[192,768]{1,0:T(8,128)(2,1)S(1)} %get-tuple-element.101.refs_0_), channel_id=1, source_target_pairs={{0,1},{1,0},{2,3},{3,2},{4,5},{5,4},{6,7},{7,6},{8,9},{9,8},{10,11... | collective-permute-start | bytes 884744 | tf_op jit(solution)/shard_map/ppermute | solution.py:269
  113.7 10.7 %collective-permute-start.42 = (bf16[9,48,384]{2,1,0:T(8,128)(2,1)S(1)}, bf16[9,48,384]{2,1,0:T(8,128)(2,1)S(1)}, u32[]{:S(2)}, u32[]{:S(2)}) collective-permute-start(bf16[9,48,384]{2,1,0:T(8,128)(2,1)S(1)} %get-tuple-element.136), channel_id=1, source_target_pairs={{0,4},{2,6},{4,0},{6,2},{8,12},{10,14},{12,8},{14,10},{16,20},{18,... | collective-permute-start | bytes 995336 | tf_op jit(solution)/shard_map/ppermute | solution.py:64
  114.4 15.6 %collective-permute-start.45 = (bf16[2,48,1536]{2,1,0:T(8,128)(2,1)S(1)}, bf16[2,48,1536]{2,1,0:T(8,128)(2,1)S(1)}, u32[]{:S(2)}, u32[]{:S(2)}) collective-permute-start(bf16[2,48,1536]{2,1,0:T(8,128)(2,1)S(1)} %e_to_4.1), channel_id=1, source_target_pairs={{0,8},{2,10},{4,12},{6,14},{8,0},{10,2},{12,4},{14,6},{16,24},{18,... | collective-permute-start | bytes 884744 | tf_op jit(solution)/shard_map/ppermute | solution.py:64
  115.4 14.7 %collective-permute-start.43 = (bf16[8,48,384]{2,1,0:T(8,128)(2,1)S(1)}, bf16[8,48,384]{2,1,0:T(8,128)(2,1)S(1)}, u32[]{:S(2)}, u32[]{:S(2)}) collective-permute-start(bf16[8,48,384]{2,1,0:T(8,128)(2,1)S(1)} %get-tuple-element.137), channel_id=1, source_target_pairs={{0,4},{2,6},{4,0},{6,2},{8,12},{10,14},{12,8},{14,10},{16,20},{18,... | collective-permute-start | bytes 884744 | tf_op jit(solution)/shard_map/ppermute | solution.py:64
  117.0 20.7 %collective-permute-start.49 = (bf16[2,48,1536]{2,1,0:T(8,128)(2,1)S(1)}, bf16[2,48,1536]{2,1,0:T(8,128)(2,1)S(1)}, u32[]{:S(2)}, u32[]{:S(2)}) collective-permute-start(bf16[2,48,1536]{2,1,0:T(8,128)(2,1)S(1)} %s_to_8.1), channel_id=1, source_target_pairs={{0,16},{2,18},{4,20},{6,22},{8,24},{10,26},{12,28},{14,30},{16,0},... | collective-permute-start | bytes 884744 | tf_op jit(solution)/shard_map/ppermute | solution.py:64
  119.0 25.9 %collective-permute-start.40 = (bf16[288,768]{1,0:T(8,128)(2,1)S(1)}, bf16[288,768]{1,0:T(8,128)(2,1)S(1)}, u32[]{:S(2)}, u32[]{:S(2)}) collective-permute-start(bf16[288,768]{1,0:T(8,128)(2,1)S(1)} %slice.9), channel_id=1, source_target_pairs={{0,1},{1,0},{2,3},{3,2},{4,5},{5,4},{6,7},{7,6},{8,9},{9,8},{10,11... | collective-permute-start | bytes 1327112 | tf_op jit(solution)/shard_map/ppermute | solution.py:269
  124.5 11.0 %collective-permute-start.44 = (bf16[5,48,384]{2,1,0:T(8,128)(2,1)S(1)}, bf16[5,48,384]{2,1,0:T(8,128)(2,1)S(1)}, u32[]{:S(2)}, u32[]{:S(2)}) collective-permute-start(bf16[5,48,384]{2,1,0:T(8,128)(2,1)S(1)} %get-tuple-element.139), channel_id=1, source_target_pairs={{0,8},{2,10},{4,12},{6,14},{8,0},{10,2},{12,4},{14,6},{16,24},{18,... | collective-permute-start | bytes 552968 | tf_op jit(solution)/shard_map/ppermute | solution.py:64
  130.2 13.9 %collective-permute-start.46 = (bf16[1,48,1536]{2,1,0:T(8,128)(2,1)S(1)}, bf16[1,48,1536]{2,1,0:T(8,128)(2,1)S(1)}, u32[]{:S(2)}, u32[]{:S(2)}) collective-permute-start(bf16[1,48,1536]{2,1,0:T(8,128)(2,1)S(1)} %e_to_8.1), channel_id=1, source_target_pairs={{0,16},{2,18},{4,20},{6,22},{8,24},{10,26},{12,28},{14,30},{16,0},... | collective-permute-start | bytes 442376 | tf_op jit(solution)/shard_map/ppermute | solution.py:64
  135.7 13.5 %collective-permute-start.48 = (bf16[5,48,384]{2,1,0:T(8,128)(2,1)S(1)}, bf16[5,48,384]{2,1,0:T(8,128)(2,1)S(1)}, u32[]{:S(2)}, u32[]{:S(2)}) collective-permute-start(bf16[5,48,384]{2,1,0:T(8,128)(2,1)S(1)} %get-tuple-element.144), channel_id=1, source_target_pairs={{0,16},{2,18},{4,20},{6,22},{8,24},{10,26},{12,28},{14,30},{16,0},... | collective-permute-start | bytes 552968 | tf_op jit(solution)/shard_map/ppermute | solution.py:64
  (36 other events, 317.5 us)

commit v5 on v4

--- a/solution.py
+++ b/solution.py
@@ -13,7 +13,7 @@
 NORM_EPS = 1e-05
 EXCLUDED = -1e30
 VMEM_BYTES = 24 * 1024 * 1024
-CUTS = {"y4": 96}
+CUTS = {"y1": 192, "y4": 96}
 
 HOPS = {o: (o, o & 12, 2) if o & 2 else (o, 0, o) for o in range(2, 16, 2)}
 HOPS.update({o + 1: (o + 1, o, 1) for o in range(0, 16, 2)})
@@ -25,27 +25,33 @@
 ORDER_AFTER = (
     "f12", "f6", "f10", "f1", "f3", "f9", "f14", "f7", "f11", "f13", "f15",
 )
-SHRINK_STEPS = ((1, 4, 8, 2), (0, 0, 0, 0))
-EXPAND_STEPS = ((1, 2, 4, 8), (0, 0, 0, 0))
-MIXER_STEPS = ((1, 2, 4, 8), (0, 1, 1, 0))
+SHRINK_STEPS = ((1, 4, 8, 2), (1, 1, 1, 1))
+EXPAND_STEPS = ((1, 2, 4, 8), (1, 1, 1, 1))
+MIXER_STEPS = ((1, 2, 4, 8), (4, 2, 2, 1))
 ORDER_TAIL = (
-    "x", "sf", "s", "ef", "e", "xf", "ef", "x", "input", "sf", "s", "e",
+    "x", "sf", "s", "ef", "e", "xf", "ef", "x", "input", "e", "sf", "s",
     "xf", "x", "s_end", "e_end", "xf", "x",
 )
 WAITS = {
-    "back": ("e2", "s4",),
     "e": ("m15",),
-    "e2": ("e",),
-    "e8": ("x2b",),
+    "e1": ("y30",),
+    "e2": ("f7",),
+    "e4": ("feed_back0",),
+    "e8": ("x2b", "y4a",),
+    "e_end": ("x4a",),
+    "e_to_2": ("s_to_4",),
     "f10": ("attention",),
     "f12": ("attention",),
-    "f7": ("f12",),
+    "f7": ("f4",),
     "f9": ("attention",),
     "m9": ("m8",),
+    "tokens": ("x_to_2",),
     "x4a": ("x_to_4",),
-    "x4b": ("e8",),
     "x_to_2": ("s4", "e2",),
+    "x_to_4": ("e4", "x1c",),
+    "x_to_8": ("x2b",),
     "y21": ("feed0",),
+    "y4b": ("input",),
 }
 
 F32 = jnp.float32
@@ -115,24 +121,21 @@
 
     def send(self):
         step = self.steps.pop(0)
-        count, got = self.count, []
+        count = self.count
         pieces = len(self.sends)
+        per = count // pieces
         for i, array in enumerate(self.sends):
-            name = f"{self.name}{step}" + ("ab"[i] if pieces > 1 else "")
-            got.append(self.plan.swap(name, array, step))
-        if pieces > 1:
-            half = count // 2
-            self.arrived.append((half, half, got[0], self.rider is not None))
-            self.arrived.append((0, half, got[1], False))
-        else:
-            self.arrived.append((0, count, got[0], self.rider is not None))
+            name = f"{self.name}{step}" + ("abcd"[i] if pieces > 1 else "")
+            got = self.plan.swap(name, array, step)
+            self.arrived.append((count - (i + 1) * per, per, got, self.rider is not None and i == 0))
         self.step = step
         self.count = count // 2
 
     def forward(self):
         count = self.count
-        split = self.split.pop(0) and count > 1
-        ranges = [(count + count // 2, count // 2), (count, count // 2)] if split else [(count, count)]
+        parts = min(self.split.pop(0), count)
+        per = count // parts
+        ranges = [(2 * count - (i + 1) * per, per) for i in range(parts)]
         needed = [a for a in self.arrived if a[0] + a[1] > count]
         name = f"{self.name}_to_{self.steps[0]}"
         self.sends = self.total(name, ranges, needed)
@@ -743,7 +746,7 @@
 
     def weight_grad(left, right, name, steps, split):
         wide = right[0].shape[1]
-        parts = 2 if split[0] else 1
+        parts = split[0]
         outs = [((8, piece_rows, wide), BF16)] + [((8 // parts, piece_rows, wide), BF16)] * parts
         kept, *sends = call(
             functools.partial(weight_grad_kernel, offsets_of(steps)),
@@ -815,7 +818,7 @@
 
     if in_pieces:
         steps, split = MIXER_STEPS
-        parts = 2 if split[0] else 1
+        parts = split[0]
         half = piece_rows // 2
         kept, *sends, rider = call(
             functools.partial(mixer_grad_kernel, offsets_of(steps), len(vectors)),

time: 150 us -> 142 us (0.947)
  waiting for transfers between devices: 73.2 us -> 57.1 us
  starting transfers between devices: 41.6 us -> 48.9 us
    ppermute x44 -> x47, waiting for transfers between devices: 59.4 us -> 42.6 us  [swap(): return lax.ppermute(array, axis, [(i, i ^ offset) for i in range(size)])]
    ppermute x44 -> x47, starting transfers between devices: 32.7 us -> 36.4 us  [swap(): return lax.ppermute(array, axis, [(i, i ^ offset) for i in range(size)])]
    ppermute x7 -> x8, starting transfers between devices: 8.81 us -> 12.4 us  [other_half(): return lax.ppermute(array, 'tensor', [(0, 1), (1, 0)])]
    ppermute x7 -> x8, waiting for transfers between devices: 13.7 us -> 14.5 us  [other_half(): return lax.ppermute(array, 'tensor', [(0, 1), (1, 0)])]
  transfers between devices with their start and end apart: 51 -> 55, of which waited for: 24 -> 22; matrix products, arithmetic and copies ran while one was open for 0% -> 0% of each run, Pallas kernels for 11% -> 22%
where the time goes in v5:
time: 142 us; the launch traced here: 141 us
  waiting for transfers between devices  57.1 us (40%)
  starting transfers between devices  48.9 us (34%)
  Pallas kernels  32.7 us (23%)
  local copies, waits for them, and re-layouts  1.59 us (1%)
    ppermute x47, waiting for transfers between devices, swap(): return lax.ppermute(array, axis, [(i, i ^ offset) for i in range(size)])  42.6 us
    ppermute x47, starting transfers between devices, swap(): return lax.ppermute(array, axis, [(i, i ^ offset) for i in range(size)])  36.4 us
    pallas_call x25, Pallas kernels, call(): pl.pallas_call(body, out_shape=tuple((make[k](o[0], o[1]) for o, k in zip...  32.7 us
    ppermute x8, waiting for transfers between devices, other_half(): return lax.ppermute(array, 'tensor', [(0, 1), (1, 0)])  14.5 us
    ppermute x8, starting transfers between devices, other_half(): return lax.ppermute(array, 'tensor', [(0, 1), (1, 0)])  12.4 us
  transfers between devices with their start and end apart: 55, of which 22 were waited for; matrix products, arithmetic and copies ran while one was open for 0% of the time, Pallas kernels for 22%

profile of v5, /device:TPU:0, one launch (start us, length us, event | category | flops | bytes accessed | tf_op | source)
XLA Modules:
  0.0 141.3 jit_solution(4073110742027872674)
XLA Ops:
  1.6 4.1 %collective-permute-start.15 = (bf16[4,48,384]{2,1,0:T(8,128)(2,1)S(1)}, bf16[4,48,384]{2,1,0:T(8,128)(2,1)S(1)}, u32[]{:S(2)}, u32[]{:S(2)}) collective-permute-start(bf16[4,48,384]{2,1,0:T(8,128)(2,1)S(1)} %bundle.1.refs_0_), channel_id=1, source_target_pairs={{0,16},{2,18},{4,20},{6,22},{8,24},{10,26},{12,28},{14,30},{16,0},... | collective-permute-start | bytes 442376 | tf_op jit(solution)/shard_map/ppermute | solution.py:70
  10.1 1.9 %prepare.1 = (bf16[6,384,384]{2,1,0:T(8,128)(2,1)S(1)}, bf16[2,48,1536]{2,1,0:T(8,128)(2,1)S(1)}) custom-call(s32[1,4]{1,0:T(1,128)S(1)} %copy-done.6, s32[6,1,384]{2,1,0:T(1,128)S(1)} %bitcast.8, bf16[48,1536]{1,0:T(8,128)(2,1)} %expand_ref.1, bf16[48,1536]{1,0:T(8,128)(2,1)} %bitcast.10), custom_call_target="tpu_custom_call" | custom-call | tf_op jit(solution)/shard_map/prepare/pallas_call | solution.py:283
  16.9 2.7 %collective-permute-done.19.refs_12_ = bf16[4,48,384]{2,1,0:T(8,128)(2,1)S(1)} collective-permute-done((bf16[4,48,384]{2,1,0:T(8,128)(2,1)S(1)}, bf16[4,48,384]{2,1,0:T(8,128)(2,1)S(1)}, u32[]{:S(2)}, u32[]{:S(2)}) %collective-permute-start.19) | collective-permute-done | bytes 147488 | tf_op jit(solution)/shard_map/ppermute | solution.py:70
  20.2 1.9 %collective-permute-done.13.refs_6_ = bf16[4,48,384]{2,1,0:T(8,128)(2,1)S(1)} collective-permute-done((bf16[4,48,384]{2,1,0:T(8,128)(2,1)S(1)}, bf16[4,48,384]{2,1,0:T(8,128)(2,1)S(1)}, u32[]{:S(2)}, u32[]{:S(2)}) %collective-permute-start.13) | collective-permute-done | bytes 147488 | tf_op jit(solution)/shard_map/ppermute | solution.py:70
  23.5 3.4 %collective-permute-start.7 = (bf16[2,48,1536]{2,1,0:T(8,128)(2,1)S(1)}, bf16[2,48,1536]{2,1,0:T(8,128)(2,1)S(1)}, u32[]{:S(2)}, u32[]{:S(2)}) collective-permute-start(bf16[2,48,1536]{2,1,0:T(8,128)(2,1)S(1)} %get-tuple-element.91.refs_0_), channel_id=1, source_target_pairs={{0,16},{2,18},{4,20},{6,22},{8,24},{10,26},{12,28},{14,30},{16,0},... | collective-permute-start | bytes 884744 | tf_op jit(solution)/shard_map/ppermute | solution.py:70
  30.4 4.9 %attention.1 = (bf16[3,384,384]{2,1,0:T(8,128)(2,1)}, bf16[6,384,384]{2,1,0:T(8,128)(2,1)}, bf16[384,384]{1,0:T(8,128)(2,1)S(1)}, bf16[384,768]{1,0:T(8,128)(2,1)S(1)}, bf16[4,768,384]{2,1,0:T(8,128)(2,1)S(1)}) custom-call(bf16[4,48,384]{2,1,0:T(8,128)(2,1)S(1)} %bundle.1.refs_0_, bf16[4,48,384]{2,1,0:T(8,128)(2,1)S(1)} %collective-permute-done.8.refs_1_, ...), custom_call_target="tpu_custom_call" | custom-call | tf_op jit(solution)/shard_map/attention/pallas_call | solution.py:283
  35.4 3.6 %collective-permute-done.7.refs_8_ = bf16[2,48,1536]{2,1,0:T(8,128)(2,1)S(1)} collective-permute-done((bf16[2,48,1536]{2,1,0:T(8,128)(2,1)S(1)}, bf16[2,48,1536]{2,1,0:T(8,128)(2,1)S(1)}, u32[]{:S(2)}, u32[]{:S(2)}) %collective-permute-start.7) | collective-permute-done | bytes 294944 | tf_op jit(solution)/shard_map/ppermute | solution.py:70
  40.0 4.4 %collective-permute-done.5.refs_6_ = bf16[2,48,1536]{2,1,0:T(8,128)(2,1)S(1)} collective-permute-done((bf16[2,48,1536]{2,1,0:T(8,128)(2,1)S(1)}, bf16[2,48,1536]{2,1,0:T(8,128)(2,1)S(1)}, u32[]{:S(2)}, u32[]{:S(2)}) %collective-permute-start.5) | collective-permute-done | bytes 294944 | tf_op jit(solution)/shard_map/ppermute | solution.py:70
  44.5 3.2 %collective-permute-done.26.refs_12_ = bf16[2,48,1536]{2,1,0:T(8,128)(2,1)S(1)} collective-permute-done((bf16[2,48,1536]{2,1,0:T(8,128)(2,1)S(1)}, bf16[2,48,1536]{2,1,0:T(8,128)(2,1)S(1)}, u32[]{:S(2)}, u32[]{:S(2)}) %collective-permute-start.26) | collective-permute-done | bytes 294944 | tf_op jit(solution)/shard_map/ppermute | solution.py:70
  51.2 5.1 %collective-permute-done.28.refs_14_ = bf16[2,48,1536]{2,1,0:T(8,128)(2,1)S(1)} collective-permute-done((bf16[2,48,1536]{2,1,0:T(8,128)(2,1)S(1)}, bf16[2,48,1536]{2,1,0:T(8,128)(2,1)S(1)}, u32[]{:S(2)}, u32[]{:S(2)}) %collective-permute-start.28) | collective-permute-done | bytes 294944 | tf_op jit(solution)/shard_map/ppermute | solution.py:70
  57.9 2.1 %feed_forward_0.1 = (f32[192,768]{1,0:T(8,128)S(1)}, f32[192,128]{1,0:T(8,128)S(1)}, bf16[192,768]{1,0:T(8,128)(2,1)S(1)}, bf16[192,1536]{1,0:T(8,128)(2,1)S(1)}...) custom-call(bf16[2,48,1536]{2,1,0:T(8,128)(2,1)S(1)} %get-tuple-element.91.refs_0_, ...), custom_call_target="tpu_custom_call" | custom-call | tf_op jit(solution)/shard_map/feed_forward_0/pallas_call | solution.py:283
  61.6 4.5 %collective-permute-done.31.refs_1_ = bf16[192,768]{1,0:T(8,128)(2,1)S(1)} collective-permute-done((bf16[192,768]{1,0:T(8,128)(2,1)S(1)}, bf16[192,768]{1,0:T(8,128)(2,1)S(1)}, u32[]{:S(2)}, u32[]{:S(2)}) %collective-permute-start.31) | collective-permute-done | bytes 294944 | tf_op jit(solution)/shard_map/ppermute | solution.py:272
  69.6 2.9 %collective-permute-done.33.refs_3_ = bf16[192,768]{1,0:T(8,128)(2,1)S(1)} collective-permute-done((bf16[192,768]{1,0:T(8,128)(2,1)S(1)}, bf16[192,768]{1,0:T(8,128)(2,1)S(1)}, u32[]{:S(2)}, u32[]{:S(2)}) %collective-permute-start.33) | collective-permute-done | bytes 294944 | tf_op jit(solution)/shard_map/ppermute | solution.py:272
  72.5 2.2 %feed_backward_0.1 = (bf16[192,768]{1,0:T(8,128)(2,1)S(1)}, f32[192,768]{1,0:T(8,128)S(1)}, bf16[192,768]{1,0:T(8,128)(2,1)S(1)}, bf16[192,1536]{1,0:T(8,128)(2,...) custom-call(bf16[2,768,1536]{2,1,0:T(8,128)(2,1)S(1)} %get-tuple-element.98.refs_0_, ...), custom_call_target="tpu_custom_call" | custom-call | tf_op jit(solution)/shard_map/feed_backward_0/pallas_call | solution.py:283
  76.3 2.5 %collective-permute-done.32.refs_3_ = bf16[192,768]{1,0:T(8,128)(2,1)S(1)} collective-permute-done((bf16[192,768]{1,0:T(8,128)(2,1)S(1)}, bf16[192,768]{1,0:T(8,128)(2,1)S(1)}, u32[]{:S(2)}, u32[]{:S(2)}) %collective-permute-start.32) | collective-permute-done | bytes 294944 | tf_op jit(solution)/shard_map/ppermute | solution.py:272
  78.8 2.8 %feed_backward_1.1 = (bf16[384,768]{1,0:T(8,128)(2,1)}, f32[192,768]{1,0:T(8,128)S(1)}, bf16[192,768]{1,0:T(8,128)(2,1)S(1)}, bf16[192,1536]{1,0:T(8,128)(2,1)S(...) custom-call(bf16[2,768,1536]{2,1,0:T(8,128)(2,1)S(1)} %get-tuple-element.98.refs_0_, ...), custom_call_target="tpu_custom_call" | custom-call | tf_op jit(solution)/shard_map/feed_backward_1/pallas_call | solution.py:283
  89.8 4.6 %collective-permute-done.35.refs_6_ = bf16[192,768]{1,0:T(8,128)(2,1)S(1)} collective-permute-done((bf16[192,768]{1,0:T(8,128)(2,1)S(1)}, bf16[192,768]{1,0:T(8,128)(2,1)S(1)}, u32[]{:S(2)}, u32[]{:S(2)}) %collective-permute-start.35) | collective-permute-done | bytes 294944 | tf_op jit(solution)/shard_map/ppermute | solution.py:272
  94.3 5.5 %attention_backward.1 = (f32[384,768]{1,0:T(8,128)S(1)}, bf16[384,768]{1,0:T(8,128)(2,1)S(1)}, f32[3,768]{1,0:T(4,128)S(1)}, bf16[3,384,384]{2,1,0:T(8,128)(2,1)S(1)}, f32[2,384]{1,0:T(2,128)S(1)}) custom-call(bf16[192,768]{1,0:T(8,128)(2,1)S(1)} %get-tuple-element.110.refs_0_, bf16[192,768]{1,0:T(8,128)(2,1)S(1)} %collective-permute-done.34.refs_1_, ...), custom_call_target="tpu_custom_call" | custom-call | tf_op jit(solution)/shard_map/attention_backward/pallas_call | solution.py:283
  99.9 1.8 %mixer_grad.1 = (bf16[32,48,384]{2,1,0:T(8,128)(2,1)S(1)}, bf16[9,48,384]{2,1,0:T(8,128)(2,1)S(1)}, bf16[8,48,384]{2,1,0:T(8,128)(2,1)S(1)}, bf16[8,48,384]{2,1,...) custom-call(bf16[384,768]{1,0:T(8,128)(2,1)S(1)} %copy-done, ...), custom_call_target="tpu_custom_call" | custom-call | tf_op jit(solution)/shard_map/mixer_grad/pallas_call | solution.py:283
  108.0 3.1 %collective-permute-start.53 = (bf16[2,48,1536]{2,1,0:T(8,128)(2,1)S(1)}, bf16[2,48,1536]{2,1,0:T(8,128)(2,1)S(1)}, u32[]{:S(2)}, u32[]{:S(2)}) collective-permute-start(bf16[2,48,1536]{2,1,0:T(8,128)(2,1)S(1)} %s_to_8.1), channel_id=1, source_target_pairs={{0,16},{2,18},{4,20},{6,22},{8,24},{10,26},{12,28},{14,30},{16,0},... | collective-permute-start | bytes 884744 | tf_op jit(solution)/shard_map/ppermute | solution.py:70
  117.0 3.1 %collective-permute-done.47.refs_5_ = bf16[8,48,384]{2,1,0:T(8,128)(2,1)S(1)} collective-permute-done((bf16[8,48,384]{2,1,0:T(8,128)(2,1)S(1)}, bf16[8,48,384]{2,1,0:T(8,128)(2,1)S(1)}, u32[]{:S(2)}, u32[]{:S(2)}) %collective-permute-start.47) | collective-permute-done | bytes 294944 | tf_op jit(solution)/shard_map/ppermute | solution.py:70
  121.7 5.8 %collective-permute-done.49.refs_6_ = bf16[5,48,384]{2,1,0:T(8,128)(2,1)S(1)} collective-permute-done((bf16[5,48,384]{2,1,0:T(8,128)(2,1)S(1)}, bf16[5,48,384]{2,1,0:T(8,128)(2,1)S(1)}, u32[]{:S(2)}, u32[]{:S(2)}) %collective-permute-start.49) | collective-permute-done | bytes 184352 | tf_op jit(solution)/shard_map/ppermute | solution.py:70
  130.9 2.2 %collective-permute-start.50 = (bf16[4,48,384]{2,1,0:T(8,128)(2,1)S(1)}, bf16[4,48,384]{2,1,0:T(8,128)(2,1)S(1)}, u32[]{:S(2)}, u32[]{:S(2)}) collective-permute-start(bf16[4,48,384]{2,1,0:T(8,128)(2,1)S(1)} %get-tuple-element.157), channel_id=1, source_target_pairs={{0,8},{2,10},{4,12},{6,14},{8,0},{10,2},{12,4},{14,6},{16,24},{18,... | collective-permute-start | bytes 442376 | tf_op jit(solution)/shard_map/ppermute | solution.py:70
  135.1 4.6 %collective-permute-done.52.refs_3_ = bf16[1,48,1536]{2,1,0:T(8,128)(2,1)S(1)} collective-permute-done((bf16[1,48,1536]{2,1,0:T(8,128)(2,1)S(1)}, bf16[1,48,1536]{2,1,0:T(8,128)(2,1)S(1)}, u32[]{:S(2)}, u32[]{:S(2)}) %collective-permute-start.52) | collective-permute-done | bytes 147488 | tf_op jit(solution)/shard_map/ppermute | solution.py:70
  (135 shorter events, 57.5 us)
Async XLA Ops:
  1.6 11.2 %collective-permute-start.15 = (bf16[4,48,384]{2,1,0:T(8,128)(2,1)S(1)}, bf16[4,48,384]{2,1,0:T(8,128)(2,1)S(1)}, u32[]{:S(2)}, u32[]{:S(2)}) collective-permute-start(bf16[4,48,384]{2,1,0:T(8,128)(2,1)S(1)} %bundle.1.refs_0_), channel_id=1, source_target_pairs={{0,16},{2,18},{4,20},{6,22},{8,24},{10,26},{12,28},{14,30},{16,0},... | collective-permute-start | bytes 442376 | tf_op jit(solution)/shard_map/ppermute | solution.py:70
  5.7 9.2 %collective-permute-start.11 = (bf16[4,48,384]{2,1,0:T(8,128)(2,1)S(1)}, bf16[4,48,384]{2,1,0:T(8,128)(2,1)S(1)}, u32[]{:S(2)}, u32[]{:S(2)}) collective-permute-start(bf16[4,48,384]{2,1,0:T(8,128)(2,1)S(1)} %bundle.1.refs_0_), channel_id=1, source_target_pairs={{0,8},{2,10},{4,12},{6,14},{8,0},{10,2},{12,4},{14,6},{16,24},{18,... | collective-permute-start | bytes 442376 | tf_op jit(solution)/shard_map/ppermute | solution.py:70
  14.9 12.6 %collective-permute-start.3 = (bf16[2,48,1536]{2,1,0:T(8,128)(2,1)S(1)}, bf16[2,48,1536]{2,1,0:T(8,128)(2,1)S(1)}, u32[]{:S(2)}, u32[]{:S(2)}) collective-permute-start(bf16[2,48,1536]{2,1,0:T(8,128)(2,1)S(1)} %get-tuple-element.91.refs_0_), channel_id=1, source_target_pairs={{0,8},{2,10},{4,12},{6,14},{8,0},{10,2},{12,4},{14,6},{16,24},{18,... | collective-permute-start | bytes 884744 | tf_op jit(solution)/shard_map/ppermute | solution.py:70
  23.5 15.4 %collective-permute-start.7 = (bf16[2,48,1536]{2,1,0:T(8,128)(2,1)S(1)}, bf16[2,48,1536]{2,1,0:T(8,128)(2,1)S(1)}, u32[]{:S(2)}, u32[]{:S(2)}) collective-permute-start(bf16[2,48,1536]{2,1,0:T(8,128)(2,1)S(1)} %get-tuple-element.91.refs_0_), channel_id=1, source_target_pairs={{0,16},{2,18},{4,20},{6,22},{8,24},{10,26},{12,28},{14,30},{16,0},... | collective-permute-start | bytes 884744 | tf_op jit(solution)/shard_map/ppermute | solution.py:70
  28.3 10.7 %collective-permute-start.1 = (bf16[2,48,1536]{2,1,0:T(8,128)(2,1)S(1)}, bf16[2,48,1536]{2,1,0:T(8,128)(2,1)S(1)}, u32[]{:S(2)}, u32[]{:S(2)}) collective-permute-start(bf16[2,48,1536]{2,1,0:T(8,128)(2,1)S(1)} %get-tuple-element.91.refs_0_), channel_id=1, source_target_pairs={{0,4},{2,6},{4,0},{6,2},{8,12},{10,14},{12,8},{14,10},{16,20},{18,... | collective-permute-start | bytes 884744 | tf_op jit(solution)/shard_map/ppermute | solution.py:70
  28.9 10.7 %collective-permute-start = (bf16[2,48,1536]{2,1,0:T(8,128)(2,1)S(1)}, bf16[2,48,1536]{2,1,0:T(8,128)(2,1)S(1)}, u32[]{:S(2)}, u32[]{:S(2)}) collective-permute-start(bf16[2,48,1536]{2,1,0:T(8,128)(2,1)S(1)} %get-tuple-element.91.refs_0_), channel_id=1, source_target_pairs={{0,2},{2,0},{4,6},{6,4},{8,10},{10,8},{12,14},{14,12},{16,18},{18,... | collective-permute-start | bytes 884744 | tf_op jit(solution)/shard_map/ppermute | solution.py:70
  28.9 15.5 %collective-permute-start.5 = (bf16[2,48,1536]{2,1,0:T(8,128)(2,1)S(1)}, bf16[2,48,1536]{2,1,0:T(8,128)(2,1)S(1)}, u32[]{:S(2)}, u32[]{:S(2)}) collective-permute-start(bf16[2,48,1536]{2,1,0:T(8,128)(2,1)S(1)} %collective-permute-done.3.refs_4_), channel_id=1, source_target_pairs={{0,4},{2,6},{4,0},{6,2},{8,12},{10,14},{12,8},{14,10},{16,20},{18,... | collective-permute-start | bytes 884744 | tf_op jit(solution)/shard_map/ppermute | solution.py:70
  39.0 10.3 %collective-permute-start.2 = (bf16[2,48,1536]{2,1,0:T(8,128)(2,1)S(1)}, bf16[2,48,1536]{2,1,0:T(8,128)(2,1)S(1)}, u32[]{:S(2)}, u32[]{:S(2)}) collective-permute-start(bf16[2,48,1536]{2,1,0:T(8,128)(2,1)S(1)} %collective-permute-done.1.refs_2_), channel_id=1, source_target_pairs={{0,2},{2,0},{4,6},{6,4},{8,10},{10,8},{12,14},{14,12},{16,18},{18,... | collective-permute-start | bytes 884744 | tf_op jit(solution)/shard_map/ppermute | solution.py:70
  39.5 11.2 %collective-permute-start.24 = (bf16[2,48,1536]{2,1,0:T(8,128)(2,1)S(1)}, bf16[2,48,1536]{2,1,0:T(8,128)(2,1)S(1)}, u32[]{:S(2)}, u32[]{:S(2)}) collective-permute-start(bf16[2,48,1536]{2,1,0:T(8,128)(2,1)S(1)} %collective-permute-done.7.refs_8_), channel_id=1, source_target_pairs={{0,4},{2,6},{4,0},{6,2},{8,12},{10,14},{12,8},{14,10},{16,20},{18,... | collective-permute-start | bytes 884744 | tf_op jit(solution)/shard_map/ppermute | solution.py:70
  56.3 9.8 %collective-permute-start.31 = (bf16[192,768]{1,0:T(8,128)(2,1)S(1)}, bf16[192,768]{1,0:T(8,128)(2,1)S(1)}, u32[]{:S(2)}, u32[]{:S(2)}) collective-permute-start(bf16[192,768]{1,0:T(8,128)(2,1)S(1)} %get-tuple-element.171), channel_id=1, source_target_pairs={{0,1},{1,0},{2,3},{3,2},{4,5},{5,4},{6,7},{7,6},{8,9},{9,8},{10,11... | collective-permute-start | bytes 884744 | tf_op jit(solution)/shard_map/ppermute | solution.py:272
  60.0 12.4 %collective-permute-start.33 = (bf16[192,768]{1,0:T(8,128)(2,1)S(1)}, bf16[192,768]{1,0:T(8,128)(2,1)S(1)}, u32[]{:S(2)}, u32[]{:S(2)}) collective-permute-start(bf16[192,768]{1,0:T(8,128)(2,1)S(1)} %get-tuple-element.101.refs_2_), channel_id=1, source_target_pairs={{0,1},{1,0},{2,3},{3,2},{4,5},{5,4},{6,7},{7,6},{8,9},{9,8},{10,11... | collective-permute-start | bytes 884744 | tf_op jit(solution)/shard_map/ppermute | solution.py:272
  67.9 10.9 %collective-permute-start.32 = (bf16[192,768]{1,0:T(8,128)(2,1)S(1)}, bf16[192,768]{1,0:T(8,128)(2,1)S(1)}, u32[]{:S(2)}, u32[]{:S(2)}) collective-permute-start(bf16[192,768]{1,0:T(8,128)(2,1)S(1)} %get-tuple-element.102.refs_2_), channel_id=1, source_target_pairs={{0,1},{1,0},{2,3},{3,2},{4,5},{5,4},{6,7},{7,6},{8,9},{9,8},{10,11... | collective-permute-start | bytes 884744 | tf_op jit(solution)/shard_map/ppermute | solution.py:272
  74.7 10.1 %collective-permute-start.34 = (bf16[192,768]{1,0:T(8,128)(2,1)S(1)}, bf16[192,768]{1,0:T(8,128)(2,1)S(1)}, u32[]{:S(2)}, u32[]{:S(2)}) collective-permute-start(bf16[192,768]{1,0:T(8,128)(2,1)S(1)} %get-tuple-element.110.refs_0_), channel_id=1, source_target_pairs={{0,1},{1,0},{2,3},{3,2},{4,5},{5,4},{6,7},{7,6},{8,9},{9,8},{10,11... | collective-permute-start | bytes 884744 | tf_op jit(solution)/shard_map/ppermute | solution.py:272
  87.9 15.7 %collective-permute-start.42 = (bf16[4,48,1536]{2,1,0:T(8,128)(2,1)S(1)}, bf16[4,48,1536]{2,1,0:T(8,128)(2,1)S(1)}, u32[]{:S(2)}, u32[]{:S(2)}) collective-permute-start(bf16[4,48,1536]{2,1,0:T(8,128)(2,1)S(1)} %e_to_2.1), channel_id=1, source_target_pairs={{0,4},{2,6},{4,0},{6,2},{8,12},{10,14},{12,8},{14,10},{16,20},{18,... | collective-permute-start | bytes 1769480 | tf_op jit(solution)/shard_map/ppermute | solution.py:70
  89.1 15.3 %collective-permute-start.40 = (bf16[4,48,1536]{2,1,0:T(8,128)(2,1)S(1)}, bf16[4,48,1536]{2,1,0:T(8,128)(2,1)S(1)}, u32[]{:S(2)}, u32[]{:S(2)}) collective-permute-start(bf16[4,48,1536]{2,1,0:T(8,128)(2,1)S(1)} %s_to_4.1), channel_id=1, source_target_pairs={{0,8},{2,10},{4,12},{6,14},{8,0},{10,2},{12,4},{14,6},{16,24},{18,... | collective-permute-start | bytes 1769480 | tf_op jit(solution)/shard_map/ppermute | solution.py:70
  104.6 10.8 %collective-permute-start.46 = (bf16[9,48,384]{2,1,0:T(8,128)(2,1)S(1)}, bf16[9,48,384]{2,1,0:T(8,128)(2,1)S(1)}, u32[]{:S(2)}, u32[]{:S(2)}) collective-permute-start(bf16[9,48,384]{2,1,0:T(8,128)(2,1)S(1)} %get-tuple-element.148), channel_id=1, source_target_pairs={{0,4},{2,6},{4,0},{6,2},{8,12},{10,14},{12,8},{14,10},{16,20},{18,... | collective-permute-start | bytes 995336 | tf_op jit(solution)/shard_map/ppermute | solution.py:70
  105.8 14.4 %collective-permute-start.47 = (bf16[8,48,384]{2,1,0:T(8,128)(2,1)S(1)}, bf16[8,48,384]{2,1,0:T(8,128)(2,1)S(1)}, u32[]{:S(2)}, u32[]{:S(2)}) collective-permute-start(bf16[8,48,384]{2,1,0:T(8,128)(2,1)S(1)} %get-tuple-element.152), channel_id=1, source_target_pairs={{0,4},{2,6},{4,0},{6,2},{8,12},{10,14},{12,8},{14,10},{16,20},{18,... | collective-permute-start | bytes 884744 | tf_op jit(solution)/shard_map/ppermute | solution.py:70
  106.7 15.0 %collective-permute-start.45 = (bf16[8,48,384]{2,1,0:T(8,128)(2,1)S(1)}, bf16[8,48,384]{2,1,0:T(8,128)(2,1)S(1)}, u32[]{:S(2)}, u32[]{:S(2)}) collective-permute-start(bf16[8,48,384]{2,1,0:T(8,128)(2,1)S(1)} %get-tuple-element.151), channel_id=1, source_target_pairs={{0,2},{2,0},{4,6},{6,4},{8,10},{10,8},{12,14},{14,12},{16,18},{18,... | collective-permute-start | bytes 884744 | tf_op jit(solution)/shard_map/ppermute | solution.py:70
  108.0 20.7 %collective-permute-start.53 = (bf16[2,48,1536]{2,1,0:T(8,128)(2,1)S(1)}, bf16[2,48,1536]{2,1,0:T(8,128)(2,1)S(1)}, u32[]{:S(2)}, u32[]{:S(2)}) collective-permute-start(bf16[2,48,1536]{2,1,0:T(8,128)(2,1)S(1)} %s_to_8.1), channel_id=1, source_target_pairs={{0,16},{2,18},{4,20},{6,22},{8,24},{10,26},{12,28},{14,30},{16,0},... | collective-permute-start | bytes 884744 | tf_op jit(solution)/shard_map/ppermute | solution.py:70
  112.3 20.8 %collective-permute-start.37 = (bf16[288,768]{1,0:T(8,128)(2,1)S(1)}, bf16[288,768]{1,0:T(8,128)(2,1)S(1)}, u32[]{:S(2)}, u32[]{:S(2)}) collective-permute-start(bf16[288,768]{1,0:T(8,128)(2,1)S(1)} %slice.17), channel_id=1, source_target_pairs={{0,1},{1,0},{2,3},{3,2},{4,5},{5,4},{6,7},{7,6},{8,9},{9,8},{10,11... | collective-permute-start | bytes 1327112 | tf_op jit(solution)/shard_map/ppermute | solution.py:272
  115.6 11.9 %collective-permute-start.49 = (bf16[5,48,384]{2,1,0:T(8,128)(2,1)S(1)}, bf16[5,48,384]{2,1,0:T(8,128)(2,1)S(1)}, u32[]{:S(2)}, u32[]{:S(2)}) collective-permute-start(bf16[5,48,384]{2,1,0:T(8,128)(2,1)S(1)} %get-tuple-element.156), channel_id=1, source_target_pairs={{0,8},{2,10},{4,12},{6,14},{8,0},{10,2},{12,4},{14,6},{16,24},{18,... | collective-permute-start | bytes 552968 | tf_op jit(solution)/shard_map/ppermute | solution.py:70
  120.1 10.3 %collective-permute-start.36 = (bf16[96,768]{1,0:T(8,128)(2,1)S(1)}, bf16[96,768]{1,0:T(8,128)(2,1)S(1)}, u32[]{:S(2)}, u32[]{:S(2)}) collective-permute-start(bf16[96,768]{1,0:T(8,128)(2,1)S(1)} %slice.16), channel_id=1, source_target_pairs={{0,1},{1,0},{2,3},{3,2},{4,5},{5,4},{6,7},{7,6},{8,9},{9,8},{10,11... | collective-permute-start | bytes 442376 | tf_op jit(solution)/shard_map/ppermute | solution.py:272
  127.6 12.9 %collective-permute-start.51 = (bf16[5,48,384]{2,1,0:T(8,128)(2,1)S(1)}, bf16[5,48,384]{2,1,0:T(8,128)(2,1)S(1)}, u32[]{:S(2)}, u32[]{:S(2)}) collective-permute-start(bf16[5,48,384]{2,1,0:T(8,128)(2,1)S(1)} %get-tuple-element.160), channel_id=1, source_target_pairs={{0,16},{2,18},{4,20},{6,22},{8,24},{10,26},{12,28},{14,30},{16,0},... | collective-permute-start | bytes 552968 | tf_op jit(solution)/shard_map/ppermute | solution.py:70
  130.9 9.6 %collective-permute-start.50 = (bf16[4,48,384]{2,1,0:T(8,128)(2,1)S(1)}, bf16[4,48,384]{2,1,0:T(8,128)(2,1)S(1)}, u32[]{:S(2)}, u32[]{:S(2)}) collective-permute-start(bf16[4,48,384]{2,1,0:T(8,128)(2,1)S(1)} %get-tuple-element.157), channel_id=1, source_target_pairs={{0,8},{2,10},{4,12},{6,14},{8,0},{10,2},{12,4},{14,6},{16,24},{18,... | collective-permute-start | bytes 442376 | tf_op jit(solution)/shard_map/ppermute | solution.py:70
  (40 other events, 309.8 us)

commit v6 on v5

--- a/solution.py
+++ b/solution.py
@@ -435,7 +435,7 @@
     scale_ref[...] = jnp.broadcast_to(scale, scale_ref.shape)
     low_ref[...] = (n * gain_ref[0:1, :] + shift_ref[0:1, :]).astype(BF16)
     units = whole.shape[2]
-    step = 256
+    step = 512
     for start in range(0, units, step):
         columns = slice(start, start + step)
         pre = dot(low_ref[...], whole[0, :, columns]) + bias_ref[:, columns]
@@ -472,7 +472,7 @@
         total = jnp.sum(values, axis=0, keepdims=True)
         sums_ref[row : row + 1, :] = total + sums_first[row : row + 1, :] if part else total
     units = whole.shape[2]
-    step = 256
+    step = 512
     for start in range(0, units, step):
         columns = slice(start, start + step)
         slope = slope_ref[:, columns].astype(F32)

time: 142 us -> 142 us (level)
  no operation moved by 1% of the time
where the time goes in v6:
time: 142 us; the launch traced here: 141 us
  waiting for transfers between devices  57.1 us (40%)
  starting transfers between devices  48.8 us (34%)
  Pallas kernels  32.7 us (23%)
  local copies, waits for them, and re-layouts  1.59 us (1%)
    ppermute x47, waiting for transfers between devices, swap(): return lax.ppermute(array, axis, [(i, i ^ offset) for i in range(size)])  42.7 us
    ppermute x47, starting transfers between devices, swap(): return lax.ppermute(array, axis, [(i, i ^ offset) for i in range(size)])  36.4 us
    pallas_call x25, Pallas kernels, call(): pl.pallas_call(body, out_shape=tuple((make[k](o[0], o[1]) for o, k in zip...  32.7 us
    ppermute x8, waiting for transfers between devices, other_half(): return lax.ppermute(array, 'tensor', [(0, 1), (1, 0)])  14.5 us
    ppermute x8, starting transfers between devices, other_half(): return lax.ppermute(array, 'tensor', [(0, 1), (1, 0)])  12.4 us
  transfers between devices with their start and end apart: 55, of which 22 were waited for; matrix products, arithmetic and copies ran while one was open for 0% of the time, Pallas kernels for 22%

profile of v6, /device:TPU:0, one launch (start us, length us, event | category | flops | bytes accessed | tf_op | source)
XLA Modules:
  0.0 141.3 jit_solution(6261127962872387795)
XLA Ops:
  1.6 4.1 %collective-permute-start.15 = (bf16[4,48,384]{2,1,0:T(8,128)(2,1)S(1)}, bf16[4,48,384]{2,1,0:T(8,128)(2,1)S(1)}, u32[]{:S(2)}, u32[]{:S(2)}) collective-permute-start(bf16[4,48,384]{2,1,0:T(8,128)(2,1)S(1)} %bundle.1.refs_0_), channel_id=1, source_target_pairs={{0,16},{2,18},{4,20},{6,22},{8,24},{10,26},{12,28},{14,30},{16,0},... | collective-permute-start | bytes 442376 | tf_op jit(solution)/shard_map/ppermute | solution.py:70
  10.1 1.9 %prepare.1 = (bf16[6,384,384]{2,1,0:T(8,128)(2,1)S(1)}, bf16[2,48,1536]{2,1,0:T(8,128)(2,1)S(1)}) custom-call(s32[1,4]{1,0:T(1,128)S(1)} %copy-done.6, s32[6,1,384]{2,1,0:T(1,128)S(1)} %bitcast.8, bf16[48,1536]{1,0:T(8,128)(2,1)} %expand_ref.1, bf16[48,1536]{1,0:T(8,128)(2,1)} %bitcast.10), custom_call_target="tpu_custom_call" | custom-call | tf_op jit(solution)/shard_map/prepare/pallas_call | solution.py:283
  16.9 2.7 %collective-permute-done.19.refs_12_ = bf16[4,48,384]{2,1,0:T(8,128)(2,1)S(1)} collective-permute-done((bf16[4,48,384]{2,1,0:T(8,128)(2,1)S(1)}, bf16[4,48,384]{2,1,0:T(8,128)(2,1)S(1)}, u32[]{:S(2)}, u32[]{:S(2)}) %collective-permute-start.19) | collective-permute-done | bytes 147488 | tf_op jit(solution)/shard_map/ppermute | solution.py:70
  20.2 1.9 %collective-permute-done.13.refs_6_ = bf16[4,48,384]{2,1,0:T(8,128)(2,1)S(1)} collective-permute-done((bf16[4,48,384]{2,1,0:T(8,128)(2,1)S(1)}, bf16[4,48,384]{2,1,0:T(8,128)(2,1)S(1)}, u32[]{:S(2)}, u32[]{:S(2)}) %collective-permute-start.13) | collective-permute-done | bytes 147488 | tf_op jit(solution)/shard_map/ppermute | solution.py:70
  23.5 3.4 %collective-permute-start.7 = (bf16[2,48,1536]{2,1,0:T(8,128)(2,1)S(1)}, bf16[2,48,1536]{2,1,0:T(8,128)(2,1)S(1)}, u32[]{:S(2)}, u32[]{:S(2)}) collective-permute-start(bf16[2,48,1536]{2,1,0:T(8,128)(2,1)S(1)} %get-tuple-element.91.refs_0_), channel_id=1, source_target_pairs={{0,16},{2,18},{4,20},{6,22},{8,24},{10,26},{12,28},{14,30},{16,0},... | collective-permute-start | bytes 884744 | tf_op jit(solution)/shard_map/ppermute | solution.py:70
  30.4 4.9 %attention.1 = (bf16[3,384,384]{2,1,0:T(8,128)(2,1)}, bf16[6,384,384]{2,1,0:T(8,128)(2,1)}, bf16[384,384]{1,0:T(8,128)(2,1)S(1)}, bf16[384,768]{1,0:T(8,128)(2,1)S(1)}, bf16[4,768,384]{2,1,0:T(8,128)(2,1)S(1)}) custom-call(bf16[4,48,384]{2,1,0:T(8,128)(2,1)S(1)} %bundle.1.refs_0_, bf16[4,48,384]{2,1,0:T(8,128)(2,1)S(1)} %collective-permute-done.8.refs_1_, ...), custom_call_target="tpu_custom_call" | custom-call | tf_op jit(solution)/shard_map/attention/pallas_call | solution.py:283
  35.4 3.6 %collective-permute-done.7.refs_8_ = bf16[2,48,1536]{2,1,0:T(8,128)(2,1)S(1)} collective-permute-done((bf16[2,48,1536]{2,1,0:T(8,128)(2,1)S(1)}, bf16[2,48,1536]{2,1,0:T(8,128)(2,1)S(1)}, u32[]{:S(2)}, u32[]{:S(2)}) %collective-permute-start.7) | collective-permute-done | bytes 294944 | tf_op jit(solution)/shard_map/ppermute | solution.py:70
  40.0 4.4 %collective-permute-done.5.refs_6_ = bf16[2,48,1536]{2,1,0:T(8,128)(2,1)S(1)} collective-permute-done((bf16[2,48,1536]{2,1,0:T(8,128)(2,1)S(1)}, bf16[2,48,1536]{2,1,0:T(8,128)(2,1)S(1)}, u32[]{:S(2)}, u32[]{:S(2)}) %collective-permute-start.5) | collective-permute-done | bytes 294944 | tf_op jit(solution)/shard_map/ppermute | solution.py:70
  44.5 3.2 %collective-permute-done.26.refs_12_ = bf16[2,48,1536]{2,1,0:T(8,128)(2,1)S(1)} collective-permute-done((bf16[2,48,1536]{2,1,0:T(8,128)(2,1)S(1)}, bf16[2,48,1536]{2,1,0:T(8,128)(2,1)S(1)}, u32[]{:S(2)}, u32[]{:S(2)}) %collective-permute-start.26) | collective-permute-done | bytes 294944 | tf_op jit(solution)/shard_map/ppermute | solution.py:70
  51.2 5.1 %collective-permute-done.28.refs_14_ = bf16[2,48,1536]{2,1,0:T(8,128)(2,1)S(1)} collective-permute-done((bf16[2,48,1536]{2,1,0:T(8,128)(2,1)S(1)}, bf16[2,48,1536]{2,1,0:T(8,128)(2,1)S(1)}, u32[]{:S(2)}, u32[]{:S(2)}) %collective-permute-start.28) | collective-permute-done | bytes 294944 | tf_op jit(solution)/shard_map/ppermute | solution.py:70
  57.9 2.1 %feed_forward_0.1 = (f32[192,768]{1,0:T(8,128)S(1)}, f32[192,128]{1,0:T(8,128)S(1)}, bf16[192,768]{1,0:T(8,128)(2,1)S(1)}, bf16[192,1536]{1,0:T(8,128)(2,1)S(1)}...) custom-call(bf16[2,48,1536]{2,1,0:T(8,128)(2,1)S(1)} %get-tuple-element.91.refs_0_, ...), custom_call_target="tpu_custom_call" | custom-call | tf_op jit(solution)/shard_map/feed_forward_0/pallas_call | solution.py:283
  61.6 4.5 %collective-permute-done.31.refs_1_ = bf16[192,768]{1,0:T(8,128)(2,1)S(1)} collective-permute-done((bf16[192,768]{1,0:T(8,128)(2,1)S(1)}, bf16[192,768]{1,0:T(8,128)(2,1)S(1)}, u32[]{:S(2)}, u32[]{:S(2)}) %collective-permute-start.31) | collective-permute-done | bytes 294944 | tf_op jit(solution)/shard_map/ppermute | solution.py:272
  69.6 2.9 %collective-permute-done.33.refs_3_ = bf16[192,768]{1,0:T(8,128)(2,1)S(1)} collective-permute-done((bf16[192,768]{1,0:T(8,128)(2,1)S(1)}, bf16[192,768]{1,0:T(8,128)(2,1)S(1)}, u32[]{:S(2)}, u32[]{:S(2)}) %collective-permute-start.33) | collective-permute-done | bytes 294944 | tf_op jit(solution)/shard_map/ppermute | solution.py:272
  72.5 2.2 %feed_backward_0.1 = (bf16[192,768]{1,0:T(8,128)(2,1)S(1)}, f32[192,768]{1,0:T(8,128)S(1)}, bf16[192,768]{1,0:T(8,128)(2,1)S(1)}, bf16[192,1536]{1,0:T(8,128)(2,...) custom-call(bf16[2,768,1536]{2,1,0:T(8,128)(2,1)S(1)} %get-tuple-element.98.refs_0_, ...), custom_call_target="tpu_custom_call" | custom-call | tf_op jit(solution)/shard_map/feed_backward_0/pallas_call | solution.py:283
  76.3 2.5 %collective-permute-done.32.refs_3_ = bf16[192,768]{1,0:T(8,128)(2,1)S(1)} collective-permute-done((bf16[192,768]{1,0:T(8,128)(2,1)S(1)}, bf16[192,768]{1,0:T(8,128)(2,1)S(1)}, u32[]{:S(2)}, u32[]{:S(2)}) %collective-permute-start.32) | collective-permute-done | bytes 294944 | tf_op jit(solution)/shard_map/ppermute | solution.py:272
  78.8 2.8 %feed_backward_1.1 = (bf16[384,768]{1,0:T(8,128)(2,1)}, f32[192,768]{1,0:T(8,128)S(1)}, bf16[192,768]{1,0:T(8,128)(2,1)S(1)}, bf16[192,1536]{1,0:T(8,128)(2,1)S(...) custom-call(bf16[2,768,1536]{2,1,0:T(8,128)(2,1)S(1)} %get-tuple-element.98.refs_0_, ...), custom_call_target="tpu_custom_call" | custom-call | tf_op jit(solution)/shard_map/feed_backward_1/pallas_call | solution.py:283
  89.8 4.6 %collective-permute-done.35.refs_6_ = bf16[192,768]{1,0:T(8,128)(2,1)S(1)} collective-permute-done((bf16[192,768]{1,0:T(8,128)(2,1)S(1)}, bf16[192,768]{1,0:T(8,128)(2,1)S(1)}, u32[]{:S(2)}, u32[]{:S(2)}) %collective-permute-start.35) | collective-permute-done | bytes 294944 | tf_op jit(solution)/shard_map/ppermute | solution.py:272
  94.3 5.5 %attention_backward.1 = (f32[384,768]{1,0:T(8,128)S(1)}, bf16[384,768]{1,0:T(8,128)(2,1)S(1)}, f32[3,768]{1,0:T(4,128)S(1)}, bf16[3,384,384]{2,1,0:T(8,128)(2,1)S(1)}, f32[2,384]{1,0:T(2,128)S(1)}) custom-call(bf16[192,768]{1,0:T(8,128)(2,1)S(1)} %get-tuple-element.110.refs_0_, bf16[192,768]{1,0:T(8,128)(2,1)S(1)} %collective-permute-done.34.refs_1_, ...), custom_call_target="tpu_custom_call" | custom-call | tf_op jit(solution)/shard_map/attention_backward/pallas_call | solution.py:283
  99.9 1.8 %mixer_grad.1 = (bf16[32,48,384]{2,1,0:T(8,128)(2,1)S(1)}, bf16[9,48,384]{2,1,0:T(8,128)(2,1)S(1)}, bf16[8,48,384]{2,1,0:T(8,128)(2,1)S(1)}, bf16[8,48,384]{2,1,...) custom-call(bf16[384,768]{1,0:T(8,128)(2,1)S(1)} %copy-done, ...), custom_call_target="tpu_custom_call" | custom-call | tf_op jit(solution)/shard_map/mixer_grad/pallas_call | solution.py:283
  108.0 3.1 %collective-permute-start.53 = (bf16[2,48,1536]{2,1,0:T(8,128)(2,1)S(1)}, bf16[2,48,1536]{2,1,0:T(8,128)(2,1)S(1)}, u32[]{:S(2)}, u32[]{:S(2)}) collective-permute-start(bf16[2,48,1536]{2,1,0:T(8,128)(2,1)S(1)} %s_to_8.1), channel_id=1, source_target_pairs={{0,16},{2,18},{4,20},{6,22},{8,24},{10,26},{12,28},{14,30},{16,0},... | collective-permute-start | bytes 884744 | tf_op jit(solution)/shard_map/ppermute | solution.py:70
  117.0 3.1 %collective-permute-done.47.refs_5_ = bf16[8,48,384]{2,1,0:T(8,128)(2,1)S(1)} collective-permute-done((bf16[8,48,384]{2,1,0:T(8,128)(2,1)S(1)}, bf16[8,48,384]{2,1,0:T(8,128)(2,1)S(1)}, u32[]{:S(2)}, u32[]{:S(2)}) %collective-permute-start.47) | collective-permute-done | bytes 294944 | tf_op jit(solution)/shard_map/ppermute | solution.py:70
  121.7 5.8 %collective-permute-done.49.refs_6_ = bf16[5,48,384]{2,1,0:T(8,128)(2,1)S(1)} collective-permute-done((bf16[5,48,384]{2,1,0:T(8,128)(2,1)S(1)}, bf16[5,48,384]{2,1,0:T(8,128)(2,1)S(1)}, u32[]{:S(2)}, u32[]{:S(2)}) %collective-permute-start.49) | collective-permute-done | bytes 184352 | tf_op jit(solution)/shard_map/ppermute | solution.py:70
  130.9 2.2 %collective-permute-start.50 = (bf16[4,48,384]{2,1,0:T(8,128)(2,1)S(1)}, bf16[4,48,384]{2,1,0:T(8,128)(2,1)S(1)}, u32[]{:S(2)}, u32[]{:S(2)}) collective-permute-start(bf16[4,48,384]{2,1,0:T(8,128)(2,1)S(1)} %get-tuple-element.157), channel_id=1, source_target_pairs={{0,8},{2,10},{4,12},{6,14},{8,0},{10,2},{12,4},{14,6},{16,24},{18,... | collective-permute-start | bytes 442376 | tf_op jit(solution)/shard_map/ppermute | solution.py:70
  135.1 4.6 %collective-permute-done.52.refs_3_ = bf16[1,48,1536]{2,1,0:T(8,128)(2,1)S(1)} collective-permute-done((bf16[1,48,1536]{2,1,0:T(8,128)(2,1)S(1)}, bf16[1,48,1536]{2,1,0:T(8,128)(2,1)S(1)}, u32[]{:S(2)}, u32[]{:S(2)}) %collective-permute-start.52) | collective-permute-done | bytes 147488 | tf_op jit(solution)/shard_map/ppermute | solution.py:70
  (135 shorter events, 57.5 us)
Async XLA Ops:
  1.6 11.2 %collective-permute-start.15 = (bf16[4,48,384]{2,1,0:T(8,128)(2,1)S(1)}, bf16[4,48,384]{2,1,0:T(8,128)(2,1)S(1)}, u32[]{:S(2)}, u32[]{:S(2)}) collective-permute-start(bf16[4,48,384]{2,1,0:T(8,128)(2,1)S(1)} %bundle.1.refs_0_), channel_id=1, source_target_pairs={{0,16},{2,18},{4,20},{6,22},{8,24},{10,26},{12,28},{14,30},{16,0},... | collective-permute-start | bytes 442376 | tf_op jit(solution)/shard_map/ppermute | solution.py:70
  5.7 9.2 %collective-permute-start.11 = (bf16[4,48,384]{2,1,0:T(8,128)(2,1)S(1)}, bf16[4,48,384]{2,1,0:T(8,128)(2,1)S(1)}, u32[]{:S(2)}, u32[]{:S(2)}) collective-permute-start(bf16[4,48,384]{2,1,0:T(8,128)(2,1)S(1)} %bundle.1.refs_0_), channel_id=1, source_target_pairs={{0,8},{2,10},{4,12},{6,14},{8,0},{10,2},{12,4},{14,6},{16,24},{18,... | collective-permute-start | bytes 442376 | tf_op jit(solution)/shard_map/ppermute | solution.py:70
  14.9 12.6 %collective-permute-start.3 = (bf16[2,48,1536]{2,1,0:T(8,128)(2,1)S(1)}, bf16[2,48,1536]{2,1,0:T(8,128)(2,1)S(1)}, u32[]{:S(2)}, u32[]{:S(2)}) collective-permute-start(bf16[2,48,1536]{2,1,0:T(8,128)(2,1)S(1)} %get-tuple-element.91.refs_0_), channel_id=1, source_target_pairs={{0,8},{2,10},{4,12},{6,14},{8,0},{10,2},{12,4},{14,6},{16,24},{18,... | collective-permute-start | bytes 884744 | tf_op jit(solution)/shard_map/ppermute | solution.py:70
  23.5 15.4 %collective-permute-start.7 = (bf16[2,48,1536]{2,1,0:T(8,128)(2,1)S(1)}, bf16[2,48,1536]{2,1,0:T(8,128)(2,1)S(1)}, u32[]{:S(2)}, u32[]{:S(2)}) collective-permute-start(bf16[2,48,1536]{2,1,0:T(8,128)(2,1)S(1)} %get-tuple-element.91.refs_0_), channel_id=1, source_target_pairs={{0,16},{2,18},{4,20},{6,22},{8,24},{10,26},{12,28},{14,30},{16,0},... | collective-permute-start | bytes 884744 | tf_op jit(solution)/shard_map/ppermute | solution.py:70
  28.3 10.7 %collective-permute-start.1 = (bf16[2,48,1536]{2,1,0:T(8,128)(2,1)S(1)}, bf16[2,48,1536]{2,1,0:T(8,128)(2,1)S(1)}, u32[]{:S(2)}, u32[]{:S(2)}) collective-permute-start(bf16[2,48,1536]{2,1,0:T(8,128)(2,1)S(1)} %get-tuple-element.91.refs_0_), channel_id=1, source_target_pairs={{0,4},{2,6},{4,0},{6,2},{8,12},{10,14},{12,8},{14,10},{16,20},{18,... | collective-permute-start | bytes 884744 | tf_op jit(solution)/shard_map/ppermute | solution.py:70
  28.9 10.7 %collective-permute-start = (bf16[2,48,1536]{2,1,0:T(8,128)(2,1)S(1)}, bf16[2,48,1536]{2,1,0:T(8,128)(2,1)S(1)}, u32[]{:S(2)}, u32[]{:S(2)}) collective-permute-start(bf16[2,48,1536]{2,1,0:T(8,128)(2,1)S(1)} %get-tuple-element.91.refs_0_), channel_id=1, source_target_pairs={{0,2},{2,0},{4,6},{6,4},{8,10},{10,8},{12,14},{14,12},{16,18},{18,... | collective-permute-start | bytes 884744 | tf_op jit(solution)/shard_map/ppermute | solution.py:70
  28.9 15.5 %collective-permute-start.5 = (bf16[2,48,1536]{2,1,0:T(8,128)(2,1)S(1)}, bf16[2,48,1536]{2,1,0:T(8,128)(2,1)S(1)}, u32[]{:S(2)}, u32[]{:S(2)}) collective-permute-start(bf16[2,48,1536]{2,1,0:T(8,128)(2,1)S(1)} %collective-permute-done.3.refs_4_), channel_id=1, source_target_pairs={{0,4},{2,6},{4,0},{6,2},{8,12},{10,14},{12,8},{14,10},{16,20},{18,... | collective-permute-start | bytes 884744 | tf_op jit(solution)/shard_map/ppermute | solution.py:70
  39.0 10.3 %collective-permute-start.2 = (bf16[2,48,1536]{2,1,0:T(8,128)(2,1)S(1)}, bf16[2,48,1536]{2,1,0:T(8,128)(2,1)S(1)}, u32[]{:S(2)}, u32[]{:S(2)}) collective-permute-start(bf16[2,48,1536]{2,1,0:T(8,128)(2,1)S(1)} %collective-permute-done.1.refs_2_), channel_id=1, source_target_pairs={{0,2},{2,0},{4,6},{6,4},{8,10},{10,8},{12,14},{14,12},{16,18},{18,... | collective-permute-start | bytes 884744 | tf_op jit(solution)/shard_map/ppermute | solution.py:70
  39.5 11.2 %collective-permute-start.24 = (bf16[2,48,1536]{2,1,0:T(8,128)(2,1)S(1)}, bf16[2,48,1536]{2,1,0:T(8,128)(2,1)S(1)}, u32[]{:S(2)}, u32[]{:S(2)}) collective-permute-start(bf16[2,48,1536]{2,1,0:T(8,128)(2,1)S(1)} %collective-permute-done.7.refs_8_), channel_id=1, source_target_pairs={{0,4},{2,6},{4,0},{6,2},{8,12},{10,14},{12,8},{14,10},{16,20},{18,... | collective-permute-start | bytes 884744 | tf_op jit(solution)/shard_map/ppermute | solution.py:70
  56.3 9.8 %collective-permute-start.31 = (bf16[192,768]{1,0:T(8,128)(2,1)S(1)}, bf16[192,768]{1,0:T(8,128)(2,1)S(1)}, u32[]{:S(2)}, u32[]{:S(2)}) collective-permute-start(bf16[192,768]{1,0:T(8,128)(2,1)S(1)} %get-tuple-element.171), channel_id=1, source_target_pairs={{0,1},{1,0},{2,3},{3,2},{4,5},{5,4},{6,7},{7,6},{8,9},{9,8},{10,11... | collective-permute-start | bytes 884744 | tf_op jit(solution)/shard_map/ppermute | solution.py:272
  60.0 12.4 %collective-permute-start.33 = (bf16[192,768]{1,0:T(8,128)(2,1)S(1)}, bf16[192,768]{1,0:T(8,128)(2,1)S(1)}, u32[]{:S(2)}, u32[]{:S(2)}) collective-permute-start(bf16[192,768]{1,0:T(8,128)(2,1)S(1)} %get-tuple-element.101.refs_2_), channel_id=1, source_target_pairs={{0,1},{1,0},{2,3},{3,2},{4,5},{5,4},{6,7},{7,6},{8,9},{9,8},{10,11... | collective-permute-start | bytes 884744 | tf_op jit(solution)/shard_map/ppermute | solution.py:272
  67.9 10.9 %collective-permute-start.32 = (bf16[192,768]{1,0:T(8,128)(2,1)S(1)}, bf16[192,768]{1,0:T(8,128)(2,1)S(1)}, u32[]{:S(2)}, u32[]{:S(2)}) collective-permute-start(bf16[192,768]{1,0:T(8,128)(2,1)S(1)} %get-tuple-element.102.refs_2_), channel_id=1, source_target_pairs={{0,1},{1,0},{2,3},{3,2},{4,5},{5,4},{6,7},{7,6},{8,9},{9,8},{10,11... | collective-permute-start | bytes 884744 | tf_op jit(solution)/shard_map/ppermute | solution.py:272
  74.7 10.1 %collective-permute-start.34 = (bf16[192,768]{1,0:T(8,128)(2,1)S(1)}, bf16[192,768]{1,0:T(8,128)(2,1)S(1)}, u32[]{:S(2)}, u32[]{:S(2)}) collective-permute-start(bf16[192,768]{1,0:T(8,128)(2,1)S(1)} %get-tuple-element.110.refs_0_), channel_id=1, source_target_pairs={{0,1},{1,0},{2,3},{3,2},{4,5},{5,4},{6,7},{7,6},{8,9},{9,8},{10,11... | collective-permute-start | bytes 884744 | tf_op jit(solution)/shard_map/ppermute | solution.py:272
  87.9 15.7 %collective-permute-start.42 = (bf16[4,48,1536]{2,1,0:T(8,128)(2,1)S(1)}, bf16[4,48,1536]{2,1,0:T(8,128)(2,1)S(1)}, u32[]{:S(2)}, u32[]{:S(2)}) collective-permute-start(bf16[4,48,1536]{2,1,0:T(8,128)(2,1)S(1)} %e_to_2.1), channel_id=1, source_target_pairs={{0,4},{2,6},{4,0},{6,2},{8,12},{10,14},{12,8},{14,10},{16,20},{18,... | collective-permute-start | bytes 1769480 | tf_op jit(solution)/shard_map/ppermute | solution.py:70
  89.1 15.3 %collective-permute-start.40 = (bf16[4,48,1536]{2,1,0:T(8,128)(2,1)S(1)}, bf16[4,48,1536]{2,1,0:T(8,128)(2,1)S(1)}, u32[]{:S(2)}, u32[]{:S(2)}) collective-permute-start(bf16[4,48,1536]{2,1,0:T(8,128)(2,1)S(1)} %s_to_4.1), channel_id=1, source_target_pairs={{0,8},{2,10},{4,12},{6,14},{8,0},{10,2},{12,4},{14,6},{16,24},{18,... | collective-permute-start | bytes 1769480 | tf_op jit(solution)/shard_map/ppermute | solution.py:70
  104.6 10.8 %collective-permute-start.46 = (bf16[9,48,384]{2,1,0:T(8,128)(2,1)S(1)}, bf16[9,48,384]{2,1,0:T(8,128)(2,1)S(1)}, u32[]{:S(2)}, u32[]{:S(2)}) collective-permute-start(bf16[9,48,384]{2,1,0:T(8,128)(2,1)S(1)} %get-tuple-element.148), channel_id=1, source_target_pairs={{0,4},{2,6},{4,0},{6,2},{8,12},{10,14},{12,8},{14,10},{16,20},{18,... | collective-permute-start | bytes 995336 | tf_op jit(solution)/shard_map/ppermute | solution.py:70
  105.8 14.4 %collective-permute-start.47 = (bf16[8,48,384]{2,1,0:T(8,128)(2,1)S(1)}, bf16[8,48,384]{2,1,0:T(8,128)(2,1)S(1)}, u32[]{:S(2)}, u32[]{:S(2)}) collective-permute-start(bf16[8,48,384]{2,1,0:T(8,128)(2,1)S(1)} %get-tuple-element.152), channel_id=1, source_target_pairs={{0,4},{2,6},{4,0},{6,2},{8,12},{10,14},{12,8},{14,10},{16,20},{18,... | collective-permute-start | bytes 884744 | tf_op jit(solution)/shard_map/ppermute | solution.py:70
  106.7 15.0 %collective-permute-start.45 = (bf16[8,48,384]{2,1,0:T(8,128)(2,1)S(1)}, bf16[8,48,384]{2,1,0:T(8,128)(2,1)S(1)}, u32[]{:S(2)}, u32[]{:S(2)}) collective-permute-start(bf16[8,48,384]{2,1,0:T(8,128)(2,1)S(1)} %get-tuple-element.151), channel_id=1, source_target_pairs={{0,2},{2,0},{4,6},{6,4},{8,10},{10,8},{12,14},{14,12},{16,18},{18,... | collective-permute-start | bytes 884744 | tf_op jit(solution)/shard_map/ppermute | solution.py:70
  108.0 20.7 %collective-permute-start.53 = (bf16[2,48,1536]{2,1,0:T(8,128)(2,1)S(1)}, bf16[2,48,1536]{2,1,0:T(8,128)(2,1)S(1)}, u32[]{:S(2)}, u32[]{:S(2)}) collective-permute-start(bf16[2,48,1536]{2,1,0:T(8,128)(2,1)S(1)} %s_to_8.1), channel_id=1, source_target_pairs={{0,16},{2,18},{4,20},{6,22},{8,24},{10,26},{12,28},{14,30},{16,0},... | collective-permute-start | bytes 884744 | tf_op jit(solution)/shard_map/ppermute | solution.py:70
  112.3 20.8 %collective-permute-start.37 = (bf16[288,768]{1,0:T(8,128)(2,1)S(1)}, bf16[288,768]{1,0:T(8,128)(2,1)S(1)}, u32[]{:S(2)}, u32[]{:S(2)}) collective-permute-start(bf16[288,768]{1,0:T(8,128)(2,1)S(1)} %slice.17), channel_id=1, source_target_pairs={{0,1},{1,0},{2,3},{3,2},{4,5},{5,4},{6,7},{7,6},{8,9},{9,8},{10,11... | collective-permute-start | bytes 1327112 | tf_op jit(solution)/shard_map/ppermute | solution.py:272
  115.6 11.9 %collective-permute-start.49 = (bf16[5,48,384]{2,1,0:T(8,128)(2,1)S(1)}, bf16[5,48,384]{2,1,0:T(8,128)(2,1)S(1)}, u32[]{:S(2)}, u32[]{:S(2)}) collective-permute-start(bf16[5,48,384]{2,1,0:T(8,128)(2,1)S(1)} %get-tuple-element.156), channel_id=1, source_target_pairs={{0,8},{2,10},{4,12},{6,14},{8,0},{10,2},{12,4},{14,6},{16,24},{18,... | collective-permute-start | bytes 552968 | tf_op jit(solution)/shard_map/ppermute | solution.py:70
  120.1 10.3 %collective-permute-start.36 = (bf16[96,768]{1,0:T(8,128)(2,1)S(1)}, bf16[96,768]{1,0:T(8,128)(2,1)S(1)}, u32[]{:S(2)}, u32[]{:S(2)}) collective-permute-start(bf16[96,768]{1,0:T(8,128)(2,1)S(1)} %slice.16), channel_id=1, source_target_pairs={{0,1},{1,0},{2,3},{3,2},{4,5},{5,4},{6,7},{7,6},{8,9},{9,8},{10,11... | collective-permute-start | bytes 442376 | tf_op jit(solution)/shard_map/ppermute | solution.py:272
  127.5 12.9 %collective-permute-start.51 = (bf16[5,48,384]{2,1,0:T(8,128)(2,1)S(1)}, bf16[5,48,384]{2,1,0:T(8,128)(2,1)S(1)}, u32[]{:S(2)}, u32[]{:S(2)}) collective-permute-start(bf16[5,48,384]{2,1,0:T(8,128)(2,1)S(1)} %get-tuple-element.160), channel_id=1, source_target_pairs={{0,16},{2,18},{4,20},{6,22},{8,24},{10,26},{12,28},{14,30},{16,0},... | collective-permute-start | bytes 552968 | tf_op jit(solution)/shard_map/ppermute | solution.py:70
  130.9 9.6 %collective-permute-start.50 = (bf16[4,48,384]{2,1,0:T(8,128)(2,1)S(1)}, bf16[4,48,384]{2,1,0:T(8,128)(2,1)S(1)}, u32[]{:S(2)}, u32[]{:S(2)}) collective-permute-start(bf16[4,48,384]{2,1,0:T(8,128)(2,1)S(1)} %get-tuple-element.157), channel_id=1, source_target_pairs={{0,8},{2,10},{4,12},{6,14},{8,0},{10,2},{12,4},{14,6},{16,24},{18,... | collective-permute-start | bytes 442376 | tf_op jit(solution)/shard_map/ppermute | solution.py:70
  (40 other events, 309.8 us)
